TPU v7x, 32 devices: a whole 2x2x4 slice. The times are simulated.
32 devices in a mesh: batch: 16 (over z, y, x), rows: 2 (over core).
Axes of the slice: x: 2, y: 2, z: 4, core: 2. Of those that a mesh axis runs over, the one named last changes fastest.
Arguments:
- images: bfloat16 [512, 28, 28, 512], P('batch', 'rows'), may hold values from -6 to 6
- counts: int32 [16], P('batch'), may hold values from 16 to 32, as said below
- w_in: bfloat16 [512, 128], replicated, may hold values from -0.25 to 0.25
- gain_a: float32 [128], replicated, may hold values from 0.5 to 1.5
- shift_a: float32 [128], replicated, may hold values from -3 to 3
- w_mid: bfloat16 [3, 3, 128, 128], replicated, may hold values from -0.1875 to 0.1875
- gain_b: float32 [128], replicated, may hold values from 0.5 to 1.5
- shift_b: float32 [128], replicated, may hold values from -3 to 3
- w_out: bfloat16 [128, 512], replicated, may hold values from -0.5 to 0.5
- gain_c: float32 [512], replicated, may hold values from 0.5 to 1.5
- shift_c: float32 [512], replicated, may hold values from -3 to 3
- cotangent: bfloat16 [512, 28, 28, 512], P('batch', 'rows'), may hold values from -8 to 8
Outputs:
- block_out: bfloat16 [512, 28, 28, 512], P('batch', 'rows')
- grad_images: bfloat16 [512, 28, 28, 512], P('batch', 'rows')
- grad_w_in: float32 [512, 128], replicated
- grad_gain_a: float32 [128], replicated
- grad_shift_a: float32 [128], replicated
- grad_w_mid: float32 [3, 3, 128, 128], replicated
- grad_gain_b: float32 [128], replicated
- grad_shift_b: float32 [128], replicated
- grad_w_out: float32 [128, 512], replicated
- grad_gain_c: float32 [512], replicated
- grad_shift_c: float32 [512], replicated
Inputs may be any that keep to these rules, and one draw needn't show every extreme that they name: Each entry counts the live leading slots of its batch index; at least one index is full.
All inputs are finite; a program needn't handle non-finite values.
Results may differ from a plain program's by a relative error of at most 0.0068.
Values may be sent and summed in bfloat16 or wider, within the bound.
No kernel may reach another device: no remote copies, remote signals or barrier semaphores. Data moves between devices by JAX's collectives and lax.ppermute only.
A program may use at most 256 MiB of HBM per device.

v0:
```python
import jax
import jax.numpy as jnp
from jax import lax
from jax.sharding import PartitionSpec as P

epsilon = 1e-05


def extended(block, sides, width):
    for axis, dim in sides:
        count = lax.axis_size(axis)
        forward = [(i, i + 1) for i in range(count - 1)]
        backward = [(target, source) for source, target in forward]
        low = lax.ppermute(
            lax.slice_in_dim(block, block.shape[dim] - width, None, axis=dim), axis, forward
        )
        high = lax.ppermute(lax.slice_in_dim(block, 0, width, axis=dim), axis, backward)
        block = jnp.concatenate([low, block, high], axis=dim)
    return block


def batch_stats(values, row_mask):
    return (jnp.sum(values * row_mask, axis=0), jnp.sum(values * values * row_mask, axis=0))


def scaled(values, pixel_total, summed, squared, gain_value, shift_value):
    mean_value = summed / pixel_total
    inv_std = lax.rsqrt(squared / pixel_total - mean_value * mean_value + epsilon)
    normed = (values - mean_value) * inv_std
    return (normed, inv_std, normed * gain_value + shift_value)


def norm_back(gradient, normed, inv_std, gain_value, row_mask, pixel_total, grad_total, grad_dot):
    return (
        inv_std
        * gain_value
        * (gradient - row_mask * (grad_total + normed * grad_dot) / pixel_total)
    )


def tap_sum(framed, weights, strip_rows, columns, flipped):
    width_in = framed.shape[3]
    result = jnp.zeros((framed.shape[0] * strip_rows * columns, weights.shape[3]), jnp.float32)
    for row_tap in range(3):
        for col_tap in range(3):
            row_start = 2 - row_tap if flipped else row_tap
            col_start = 2 - col_tap if flipped else col_tap
            window = framed[
                :, row_start : row_start + strip_rows, col_start : col_start + columns, :
            ].reshape(-1, width_in)
            if flipped:
                result = result + lax.dot_general(
                    window,
                    weights[row_tap, col_tap],
                    (((1,), (1,)), ((), ())),
                    preferred_element_type=jnp.float32,
                )
            else:
                result = result + jnp.dot(
                    window, weights[row_tap, col_tap], preferred_element_type=jnp.float32
                )
    return result


def tap_grads(framed, gradient, strip_rows, columns):
    width_in = framed.shape[3]
    stacked = []
    for row_tap in range(3):
        for col_tap in range(3):
            window = framed[
                :, row_tap : row_tap + strip_rows, col_tap : col_tap + columns, :
            ].reshape(-1, width_in)
            stacked.append(
                lax.dot_general(
                    window, gradient, (((0,), (0,)), ((), ())), preferred_element_type=jnp.float32
                )
            )
    return jnp.stack(stacked).reshape(3, 3, width_in, gradient.shape[1])


def local(
    images, counts, w_in, gain_a, shift_a, w_mid, gain_b, shift_b, w_out, gain_c, shift_c, cotangent
):
    img_count, strip_rows, columns, channels = images.shape
    middle = w_in.shape[1]
    valid_mask = (jnp.arange(img_count) < counts[0]).astype(jnp.float32)
    row_mask = jnp.broadcast_to(
        valid_mask[:, None, None, None], (img_count, strip_rows, columns, 1)
    ).reshape(-1, 1)
    image_mask = valid_mask.astype(jnp.bfloat16)[:, None, None, None]
    masked = (images * image_mask).reshape(-1, channels)
    local_pixels = counts[0].astype(jnp.float32) * float(strip_rows * columns)
    side_pad = ((0, 0), (0, 0), (1, 1), (0, 0))
    conv_first = jnp.dot(masked, w_in, preferred_element_type=jnp.float32)
    summed, squared = batch_stats(conv_first, row_mask)
    summed_a, squared_a, pixel_total = lax.psum((summed, squared, local_pixels), ("batch", "rows"))
    normed_a, inv_a, pre_a = scaled(conv_first, pixel_total, summed_a, squared_a, gain_a, shift_a)
    act_a, gelu_back_a = jax.vjp(jax.nn.gelu, pre_a)
    act_a = act_a.astype(jnp.bfloat16).reshape(img_count, strip_rows, columns, middle)
    framed = extended(act_a, (("rows", 1),), 1)
    framed = jnp.pad(framed, side_pad)
    conv_mid = tap_sum(framed, w_mid, strip_rows, columns, False)
    summed, squared = batch_stats(conv_mid, row_mask)
    summed_b, squared_b = lax.psum((summed, squared), ("batch", "rows"))
    normed_b, inv_b, pre_b = scaled(conv_mid, pixel_total, summed_b, squared_b, gain_b, shift_b)
    act_b, gelu_back_b = jax.vjp(jax.nn.gelu, pre_b)
    act_b = act_b.astype(jnp.bfloat16)
    conv_last = jnp.dot(act_b, w_out, preferred_element_type=jnp.float32)
    summed, squared = batch_stats(conv_last, row_mask)
    summed_c, squared_c = lax.psum((summed, squared), ("batch", "rows"))
    normed_c, inv_c, pre_c = scaled(conv_last, pixel_total, summed_c, squared_c, gain_c, shift_c)
    block_out, gelu_back_out = jax.vjp(jax.nn.gelu, pre_c + masked.astype(jnp.float32))
    upstream = (cotangent * image_mask).reshape(-1, channels).astype(jnp.float32)
    grad_pre = gelu_back_out(upstream)[0]
    total_c, dot_c = lax.psum(
        (jnp.sum(grad_pre, axis=0), jnp.sum(grad_pre * normed_c, axis=0)), ("batch", "rows")
    )
    grad_last = norm_back(
        grad_pre, normed_c, inv_c, gain_c, row_mask, pixel_total, total_c, dot_c
    ).astype(jnp.bfloat16)
    weight_last = lax.dot_general(
        act_b, grad_last, (((0,), (0,)), ((), ())), preferred_element_type=jnp.float32
    )
    grad_act_b = lax.dot_general(
        grad_last, w_out, (((1,), (1,)), ((), ())), preferred_element_type=jnp.float32
    )
    grad_pre_b = gelu_back_b(grad_act_b)[0]
    total_b, dot_b = lax.psum(
        (jnp.sum(grad_pre_b, axis=0), jnp.sum(grad_pre_b * normed_b, axis=0)), ("batch", "rows")
    )
    grad_mid = norm_back(
        grad_pre_b, normed_b, inv_b, gain_b, row_mask, pixel_total, total_b, dot_b
    ).astype(jnp.bfloat16)
    weight_mid = tap_grads(framed, grad_mid, strip_rows, columns)
    framed_grad = extended(
        grad_mid.reshape(img_count, strip_rows, columns, middle), (("rows", 1),), 1
    )
    framed_grad = jnp.pad(framed_grad, side_pad)
    grad_act_a = tap_sum(framed_grad, w_mid, strip_rows, columns, True)
    grad_pre_a = gelu_back_a(grad_act_a)[0]
    total_a, dot_a = lax.psum(
        (jnp.sum(grad_pre_a, axis=0), jnp.sum(grad_pre_a * normed_a, axis=0)), ("batch", "rows")
    )
    grad_first = norm_back(
        grad_pre_a, normed_a, inv_a, gain_a, row_mask, pixel_total, total_a, dot_a
    ).astype(jnp.bfloat16)
    weight_first = lax.dot_general(
        masked, grad_first, (((0,), (0,)), ((), ())), preferred_element_type=jnp.float32
    )
    through = lax.dot_general(
        grad_first, w_in, (((1,), (1,)), ((), ())), preferred_element_type=jnp.float32
    )
    grad_images = (
        (row_mask * (grad_pre + through))
        .astype(jnp.bfloat16)
        .reshape(img_count, strip_rows, columns, channels)
    )
    weight_first, weight_mid, weight_last = lax.psum(
        (weight_first, weight_mid, weight_last), ("batch", "rows")
    )
    block_out = block_out.astype(jnp.bfloat16).reshape(img_count, strip_rows, columns, channels)
    return (
        block_out,
        grad_images,
        weight_first,
        dot_a,
        total_a,
        weight_mid,
        dot_b,
        total_b,
        weight_last,
        dot_c,
        total_c,
    )


def solution(mesh):
    placed = (
        P("batch", "rows", None, None),
        P("batch"),
        P(),
        P(),
        P(),
        P(),
        P(),
        P(),
        P(),
        P(),
        P(),
        P("batch", "rows", None, None),
    )
    return jax.shard_map(
        local,
        mesh=mesh,
        in_specs=placed,
        out_specs=(
            P("batch", "rows", None, None),
            P("batch", "rows", None, None),
            P(),
            P(),
            P(),
            P(),
            P(),
            P(),
            P(),
            P(),
            P(),
        ),
        check_vma=False,
    )
```

profile of v0, /device:TPU:0, one launch (start us, length us, event | category | flops | bytes accessed | tf_op | source)
XLA Modules:
  0.0 887.1 jit_solution(13073867344284879811)
XLA Ops:
  8.2 20.1 %multiply_convert_fusion.3 = (f32[32,14,28,512]{3,0,2,1:T(8,128)}, bf16[32,14,28,512]{3,0,2,1:T(8,128)(2,1)S(1)}) fusion(bf16[32,14,28,512]{3,0,2,1:T(8,128)(2,1)} %param.23, bf16[32]{0:T(256)(128)(2,1)S(1)} %get-tuple-element.100, bf16[32,14,28,512]{3,0,2,1:T(8,128)(2,1)} %param.12), kind=kLoop, calls=%fused_computation.32 | loop fusion | flops 19267584 | bytes 64225344 | tf_op jit(solution)/shard_map/convert_element_type | solution.py:113
  28.3 10.0 %copy.27 = bf16[32,14,28,512]{3,2,1,0:T(8,128)(2,1)} copy(bf16[32,14,28,512]{3,0,2,1:T(8,128)(2,1)S(1)} %get-tuple-element.94) | data formatting | bytes 25690112 | tf_op jit(solution)/shard_map/mul | solution.py:91
  38.2 19.1 %reshape.139 = bf16[12544,512]{1,0:T(8,128)(2,1)} reshape(bf16[32,14,28,512]{3,2,1,0:T(8,128)(2,1)} %copy.27) | data formatting | bytes 25690112 | tf_op jit(solution)/shard_map/reshape | solution.py:91
  57.3 9.7 %multiply_reduce_fusion.7 = (f32[128]{0:T(128)S(1)}, f32[128]{0:T(128)S(1)}, f32[12544,128]{1,0:T(8,128)}) fusion(f32[12544]{0:T(1024)S(1)} %broadcast_in_dim.5, bf16[12544,512]{1,0:T(8,128)(2,1)} %reshape.139, bf16[512,128]{1,0:T(8,128)(2,1)S(1)} %copy-done.27), kind=kOutput, calls=%fused_computation.63 | convolution fusion | flops 1652195072 | bytes 19449856 | tf_op jit(solution)/shard_map/dot_general | solution.py:94
  67.0 42.0 %all-reduce.7 = (f32[128]{0:T(128)S(1)}, f32[]{:T(128)}, f32[128]{0:T(128)S(1)}) all-reduce(f32[128]{0:T(128)S(1)} %get-tuple-element.40, f32[]{:T(128)S(6)} %mul.341, f32[128]{0:T(128)S(1)} %get-tuple-element.39), channel_id=1, replica_groups=mesh['batch'=16,'rows'=2] {'batch','rows'}, use_global_device_ids=true, to_apply=%region_1.0 | all-reduce | flops 257 | bytes 2056 | tf_op jit(solution)/shard_map/psum | solution.py:96
  110.6 4.8 multiply_convert_fusion.7
  123.7 26.7 %copy.28 = f32[32,14,28,512]{3,2,1,0:T(8,128)} copy(f32[32,14,28,512]{3,0,2,1:T(8,128)} %get-tuple-element.93) | data formatting | bytes 51380224 | tf_op jit(solution)/shard_map/convert_element_type | solution.py:113
  150.3 28.6 %reshape.161 = f32[12544,512]{1,0:T(8,128)} reshape(f32[32,14,28,512]{3,2,1,0:T(8,128)} %copy.28) | data formatting | bytes 51380224 | tf_op jit(solution)/shard_map/convert_element_type | solution.py:113
  178.9 5.3 pad_maximum_fusion.2
  184.3 6.0 reshape.147
  190.3 6.0 reshape.142
  200.3 10.8 %fusion.83 = (bf16[32,14,28,128]{3,2,1,0:T(8,128)(2,1)}, bf16[32,14,28,128]{3,2,1,0:T(8,128)(2,1)}, bf16[32,14,28,128]{3,2,1,0:T(8,128)(2,1)}, bf16[32,14,28,128...) fusion(bf16[32,16,30,128]{3,2,1,0:T(8,128)(2,1)S(1)} %select_maximum_fusion.2), kind=kLoop, calls=%fused_computation.154 | loop fusion | bytes 38535168 | tf_op jit(solution)/shard_map/slice | solution.py:48
  211.1 6.0 reshape.146
  217.1 6.0 reshape.145
  223.1 6.0 reshape.144
  229.1 6.0 reshape.143
  235.1 6.0 reshape.141
  241.1 6.2 reshape.148
  262.8 6.7 multiply_reduce_fusion.5
  269.5 41.5 %all-reduce.6 = (f32[128]{0:T(128)S(1)}, f32[128]{0:T(128)S(1)}) all-reduce(f32[128]{0:T(128)S(1)} %get-tuple-element.38, f32[128]{0:T(128)S(1)} %get-tuple-element.37), channel_id=1, replica_groups=mesh['batch'=16,'rows'=2] {'batch','rows'}, use_global_device_ids=true, to_apply=%region_6.7 | all-reduce | flops 256 | bytes 2048 | tf_op jit(solution)/shard_map/psum | solution.py:104
  311.7 13.5 %multiply_reduce_fusion.2 = (f32[512]{0:T(512)S(1)}, f32[512]{0:T(512)S(1)}, f32[12544,512]{1,0:T(8,128)}) fusion(f32[12544]{0:T(1024)S(1)} %broadcast_in_dim.5, bf16[128,512]{1,0:T(8,128)(2,1)S(1)} %copy-done, f32[12544,128]{1,0:T(8,128)} %get-tuple-element.96, f32[128]{0:T(128)S(1)} %copy-done.47, f32[128]{0:T(128)S(1)} %copy-done.44, ...), kind=kOutput, calls=%fused_computation.15 | convolution fusion | flops 1697152000 | bytes 32300032 | tf_op jit(solution)/shard_map/dot_general | solution.py:108
  325.2 39.4 %all-reduce.5 = (f32[512]{0:T(512)S(1)}, f32[512]{0:T(512)S(1)}) all-reduce(f32[512]{0:T(512)S(1)} %get-tuple-element.34, f32[512]{0:T(512)S(1)} %get-tuple-element.33), channel_id=1, replica_groups=mesh['batch'=16,'rows'=2] {'batch','rows'}, use_global_device_ids=true, to_apply=%region_12.13 | all-reduce | flops 1024 | bytes 8192 | tf_op jit(solution)/shard_map/psum | solution.py:110
  365.3 43.8 %fusion.74 = (f32[512]{0:T(512)S(1)}, f32[512]{0:T(512)S(1)}, f32[12544,512]{1,0:T(8,128)}, bf16[12544,512]{1,0:T(8,128)(2,1)}) fusion(f32[512]{0:T(512)S(1)} %get-tuple-element.69, f32[12544,512]{1,0:T(8,128)} %get-tuple-element.97, f32[512]{0:T(512)S(1)} %get-tuple-element.92, f32[12544,512]{1,0:T(8,128)} %reshape.161, bf16[12544,512]{1,0:T(8,128)(2,1)} %reshape.139, ...), kind=kLoop, calls=%fused_computation.147 | loop fusion | flops 192674816 | bytes 102772736 | tf_op jit(solution)/shard_map/reduce_sum | solution.py:116
  409.1 41.0 %all-reduce.4 = (f32[512]{0:T(512)S(1)}, f32[512]{0:T(512)S(1)}) all-reduce(f32[512]{0:T(512)S(1)} %get-tuple-element.36, f32[512]{0:T(512)S(1)} %get-tuple-element.35), channel_id=1, replica_groups=mesh['batch'=16,'rows'=2] {'batch','rows'}, use_global_device_ids=true, to_apply=%region_16.17 | all-reduce | flops 1024 | bytes 8192 | tf_op jit(solution)/shard_map/psum | solution.py:115
  450.1 18.5 %multiply_convert_fusion.1 = bf16[12544,512]{1,0:T(8,128)(2,1)S(1)} fusion(f32[12544,512]{1,0:T(8,128)} %get-tuple-element.70, f32[12544,512]{1,0:T(8,128)} %get-tuple-element.97, f32[]{:T(128)} %get-tuple-element.56, f32[512]{0:T(512)S(1)} %get-tuple-element.110, f32[512]{0:T(512)S(1)} %get-tuple-element.111, f32[512]{0:T(512)S(1)} %get-tuple-element.68, ...), kind=kLoop, calls=%fused_computation.9 | loop fusion | flops 57802752 | bytes 64285700 | tf_op jit(solution)/shard_map/convert_element_type | solution.py:120
  468.6 4.7 fusion.72
  473.3 7.8 fusion.76
  481.1 39.1 %all-reduce.3 = (f32[128]{0:T(128)S(1)}, f32[128]{0:T(128)S(1)}) all-reduce(f32[128]{0:T(128)S(1)} %get-tuple-element.44, f32[128]{0:T(128)S(1)} %get-tuple-element.43), channel_id=1, replica_groups=mesh['batch'=16,'rows'=2] {'batch','rows'}, use_global_device_ids=true, to_apply=%region_20.21 | all-reduce | flops 256 | bytes 2048 | tf_op jit(solution)/shard_map/psum | solution.py:128
  520.3 8.8 multiply_convert_fusion.5
  552.6 19.2 %reshape.149 = bf16[32,14,28,512]{3,2,1,0:T(8,128)(2,1)} reshape(bf16[12544,512]{1,0:T(8,128)(2,1)} %get-tuple-element.71) | data formatting | bytes 25690112 | tf_op jit(solution)/shard_map/reshape | solution.py:161
  571.8 13.8 %copy.29 = bf16[32,14,28,512]{3,0,2,1:T(8,128)(2,1)} copy(bf16[32,14,28,512]{3,2,1,0:T(8,128)(2,1)} %reshape.149) | data formatting | bytes 25690112
  592.0 6.0 reshape.157
  598.0 6.0 reshape.152
  608.0 10.1 %fusion.82 = (bf16[32,14,28,128]{3,2,1,0:T(8,128)(2,1)}, bf16[32,14,28,128]{3,2,1,0:T(8,128)(2,1)}, bf16[32,14,28,128]{3,2,1,0:T(8,128)(2,1)}, bf16[32,14,28,128...) fusion(bf16[32,16,30,128]{3,2,1,0:T(8,128)(2,1)S(1)} %select_maximum_fusion), kind=kLoop, calls=%fused_computation.153 | loop fusion | bytes 38535168 | tf_op jit(solution)/shard_map/slice | solution.py:48
  618.0 6.0 reshape.156
  624.0 6.0 reshape.155
  630.0 6.0 reshape.154
  636.0 6.0 reshape.153
  642.0 6.4 reshape.151
  661.6 6.1 reshape.158
  676.9 8.4 fusion.75
  685.3 41.5 %all-reduce.2 = (f32[128]{0:T(128)S(1)}, f32[128]{0:T(128)S(1)}) all-reduce(f32[128]{0:T(128)S(1)} %get-tuple-element.42, f32[128]{0:T(128)S(1)} %get-tuple-element.41), channel_id=1, replica_groups=mesh['batch'=16,'rows'=2] {'batch','rows'}, use_global_device_ids=true, to_apply=%region_24.25 | all-reduce | flops 256 | bytes 2048 | tf_op jit(solution)/shard_map/psum | solution.py:141
  726.9 8.5 multiply_convert_fusion.4
  735.5 7.3 fusion.86
  742.8 15.9 %multiply_convert_fusion = bf16[12544,512]{1,0:T(8,128)(2,1)} fusion(f32[12544,512]{1,0:T(8,128)} %get-tuple-element.70, bf16[12544,128]{1,0:T(8,128)(2,1)S(1)} %multiply_convert_fusion.4, bf16[512,128]{1,0:T(8,128)(2,1)S(1)} %copy-done.28, f32[12544]{0:T(1024)S(1)} %broadcast_in_dim.5), kind=kOutput, calls=%fused_computation.8 | convolution fusion | flops 1663434752 | bytes 41927680 | tf_op jit(solution)/shard_map/dot_general | solution.py:150
  758.7 19.0 %reshape.159 = bf16[32,14,28,512]{3,2,1,0:T(8,128)(2,1)} reshape(bf16[12544,512]{1,0:T(8,128)(2,1)} %multiply_convert_fusion) | data formatting | bytes 25690112 | tf_op jit(solution)/shard_map/reshape | solution.py:156
  777.7 13.7 %copy.30 = bf16[32,14,28,512]{3,0,2,1:T(8,128)(2,1)} copy(bf16[32,14,28,512]{3,2,1,0:T(8,128)(2,1)} %reshape.159) | data formatting | bytes 25690112
  791.4 83.4 %all-reduce.11.cloned.1.call-done = (f32[512,128]{1,0:T(8,128)}, f32[3,3,128,128]{3,2,1,0:T(8,128)}, f32[128,512]{1,0:T(8,128)}) async-done(((f32[512,128]{1,0:T(8,128)}, f32[3,3,128,128]{3,2,1,0:T(8,128)}, f32[128,512]{1,0:T(8,128)}), (f32[512,128]{1,0:T(8,128)}, f32[3,3,128,128]{3,2,1,0:T(8,128)}, f32[128,512]{1,0:T(8,128)})) %all-reduce.11.cloned.1.call-update) | async-done | bytes 1114128 | tf_op jit(solution)/shard_map/psum | solution.py:158
  (157 shorter events, 92.1 us)
Async XLA Ops:
  7.2 304.5 %copy-start = (bf16[128,512]{1,0:T(8,128)(2,1)S(1)}, bf16[128,512]{1,0:T(8,128)(2,1)}, u32[]{:S(2)}) copy-start(bf16[128,512]{1,0:T(8,128)(2,1)} %param.20) | copy-start | bytes 393220
  7.2 867.6 %all-reduce.11.cloned.1.call-start = ((), (), s32[]{:S(2)}) async-start(), calls=%async_computation | async-start | bytes 2228224 | tf_op jit(solution)/shard_map/psum | solution.py:158
  38.2 19.1 %copy-start.27 = (bf16[512,128]{1,0:T(8,128)(2,1)S(1)}, bf16[512,128]{1,0:T(8,128)(2,1)}, u32[]{:S(2)}) copy-start(bf16[512,128]{1,0:T(8,128)(2,1)} %param.14) | copy-start | bytes 393220
  57.3 51.6 %copy-start.38 = (f32[128]{0:T(128)S(1)}, f32[128]{0:T(128)}, u32[]{:S(2)}) copy-start(f32[128]{0:T(128)} %param.15) | copy-start | bytes 1540
  57.3 53.3 %copy-start.45 = (f32[128]{0:T(128)S(1)}, f32[128]{0:T(128)}, u32[]{:S(2)}) copy-start(f32[128]{0:T(128)} %param.16) | copy-start | bytes 1540
  115.5 141.6 %copy-start.2 = (bf16[12544,128]{1,0:T(8,128)(2,1)}, bf16[12544,128]{1,0:T(8,128)(2,1)S(1)}, u32[]{:S(2)}) copy-start(bf16[12544,128]{1,0:T(8,128)(2,1)S(1)} %multiply_convert_fusion.7) | copy-start | bytes 9633796
  120.2 58.7 %collective-permute-start = (bf16[32,1,28,128]{3,2,1,0:T(8,128)(2,1)}, bf16[32,1,28,128]{3,2,1,0:T(8,128)(2,1)}, u32[]{:S(2)}, u32[]{:S(2)}) collective-permute-start(bf16[32,1,28,128]{3,2,1,0:T(8,128)(2,1)} %get-tuple-element.90), channel_id=1, source_target_pairs={{0,1},{2,3},{4,5},{6,7},{8,9},{10,11},{12,13},{14,15},{16,17},{18,... | collective-permute-start | bytes 688136 | tf_op jit(solution)/shard_map/ppermute | solution.py:14
  122.2 56.7 %collective-permute-start.1 = (bf16[32,1,28,128]{3,2,1,0:T(8,128)(2,1)}, bf16[32,1,28,128]{3,2,1,0:T(8,128)(2,1)}, u32[]{:S(2)}, u32[]{:S(2)}) collective-permute-start(bf16[32,1,28,128]{3,2,1,0:T(8,128)(2,1)} %get-tuple-element.91), channel_id=1, source_target_pairs={{1,0},{3,2},{5,4},{7,6},{9,8},{11,10},{13,12},{15,14},{17,16},{19,... | collective-permute-start | bytes 688136 | tf_op jit(solution)/shard_map/ppermute | solution.py:17
  247.3 3.1 copy-start.15
  247.3 3.1 copy-start.26
  262.8 48.2 %copy-start.44 = (f32[128]{0:T(128)S(1)}, f32[128]{0:T(128)}, u32[]{:S(2)}) copy-start(f32[128]{0:T(128)} %param.18) | copy-start | bytes 1540
  262.8 48.9 %copy-start.47 = (f32[128]{0:T(128)S(1)}, f32[128]{0:T(128)}, u32[]{:S(2)}) copy-start(f32[128]{0:T(128)} %param.19) | copy-start | bytes 1540
  311.7 52.9 %copy-start.29 = (f32[512]{0:T(512)S(1)}, f32[512]{0:T(512)}, u32[]{:S(2)}) copy-start(f32[512]{0:T(512)} %param.21) | copy-start | bytes 6148
  311.7 53.6 %copy-start.36 = (f32[512]{0:T(512)S(1)}, f32[512]{0:T(512)}, u32[]{:S(2)}) copy-start(f32[512]{0:T(512)} %param.22) | copy-start | bytes 6148
  450.1 18.5 %copy-start.34 = (f32[512]{0:T(512)}, f32[512]{0:T(512)S(1)}, u32[]{:S(2)}) copy-start(f32[512]{0:T(512)S(1)} %get-tuple-element.110) | copy-start | bytes 6148
  450.1 18.5 %copy-start.35 = (f32[512]{0:T(512)}, f32[512]{0:T(512)S(1)}, u32[]{:S(2)}) copy-start(f32[512]{0:T(512)S(1)} %get-tuple-element.111) | copy-start | bytes 6148
  450.1 18.5 %copy-start.19 = (f32[12544,128]{1,0:T(8,128)S(1)}, f32[12544,128]{1,0:T(8,128)}, u32[]{:S(2)}) copy-start(f32[12544,128]{1,0:T(8,128)} %get-tuple-element.96) | copy-start | bytes 19267588
  520.3 8.9 copy-start.40
  520.3 8.9 copy-start.41
  520.3 8.9 copy-start.16
  533.4 3.7 copy-start.12
  533.4 5.4 copy-start.10
  537.1 3.4 copy-start.3
  538.9 3.4 copy-start.8
  540.6 3.4 copy-start.5
  542.3 3.4 copy-start.18
  549.3 38.0 %collective-permute-start.2 = (bf16[32,1,28,128]{3,2,1,0:T(8,128)(2,1)}, bf16[32,1,28,128]{3,2,1,0:T(8,128)(2,1)}, u32[]{:S(2)}, u32[]{:S(2)}) collective-permute-start(bf16[32,1,28,128]{3,2,1,0:T(8,128)(2,1)} %get-tuple-element.86), channel_id=1, source_target_pairs={{0,1},{2,3},{4,5},{6,7},{8,9},{10,11},{12,13},{14,15},{16,17},{18,... | collective-permute-start | bytes 688136 | tf_op jit(solution)/shard_map/ppermute | solution.py:14
  551.3 36.0 %collective-permute-start.3 = (bf16[32,1,28,128]{3,2,1,0:T(8,128)(2,1)}, bf16[32,1,28,128]{3,2,1,0:T(8,128)(2,1)}, u32[]{:S(2)}, u32[]{:S(2)}) collective-permute-start(bf16[32,1,28,128]{3,2,1,0:T(8,128)(2,1)} %get-tuple-element.87), channel_id=1, source_target_pairs={{1,0},{3,2},{5,4},{7,6},{9,8},{11,10},{13,12},{15,14},{17,16},{19,... | collective-permute-start | bytes 688136 | tf_op jit(solution)/shard_map/ppermute | solution.py:17
  571.7 13.8 %copy-start.14 = (bf16[12544,128]{1,0:T(8,128)(2,1)S(1)}, bf16[12544,128]{1,0:T(8,128)(2,1)}, u32[]{:S(2)}) copy-start(bf16[12544,128]{1,0:T(8,128)(2,1)} %reshape.148) | copy-start | bytes 9633796
  585.6 2.0 copy-start.13
  648.4 3.1 copy-start.22
  651.5 1.9 copy-start.24
  653.4 1.9 copy-start.23
  661.6 9.2 %slice-start = ((s8[6422528]{0:T(1024)(128)(4,1)}), s8[2228224]{0:T(1024)(128)(4,1)S(1)}, s32[]{:S(2)}) async-start(s8[6422528]{0:T(1024)(128)(4,1)} %bitcast.135), calls=%async_computation.1 | async-start | bytes 4456448
  667.7 3.2 slice-start.1
  667.7 4.2 copy-start.21
  671.9 4.0 slice-start.2
  673.8 2.1 slice-start.3
  673.8 3.0 copy-start.25
  673.8 3.0 copy-start.31
  673.8 3.0 copy-start.33
  673.9 3.0 copy-start.39
  673.9 3.0 copy-start.46
  676.9 50.0 %copy-start.37 = (f32[128]{0:T(128)S(1)}, f32[128]{0:T(128)}, u32[]{:S(2)}) copy-start(f32[128]{0:T(128)} %get-tuple-element.61) | copy-start | bytes 1540
  726.9 8.6 copy-start.42
  726.9 8.6 copy-start.43
  735.4 7.3 copy-start.28
  777.7 102.4 %copy-start.1 = (bf16[128,512]{1,0:T(8,128)(2,1)S(1)}, bf16[128,512]{1,0:T(8,128)(2,1)}, u32[]{:S(2)}) copy-start(bf16[128,512]{1,0:T(8,128)(2,1)} %param.20) | copy-start | bytes 393220
  (9 other events, 14.4 us)
Sparse Core Ops, SparseCore 0:
  742.9 131.8 all-reduce.10
where the time goes:
time: 899 us; the launch traced here: 887 us
  local copies, waits for them, and re-layouts  291 us (32%)
  blocking collectives  244 us (27%)
  other arithmetic  125 us (14%)
  matrix products  121 us (13%)
  waiting for transfers between devices  83.5 us (9%)
  between operations  15.5 us (2%)
    reshape x16, local copies, waits for them, and re-layouts, tap_sum(): window = framed[:, row_start:row_start + strip_rows, col_start:col_start...  96.7 us
    psum x1, waiting for transfers between devices, local(): lax.psum((weight_first, weight_mid, weight_last), ('batch', 'rows'))  83.4 us
    convert_element_type x2, local copies, waits for them, and re-layouts, local(): (cotangent * image_mask).reshape(-1, channels).astype(jnp.float32)  55.3 us
    reduce_sum x1, other arithmetic, local(): jnp.sum(grad_pre, axis=0)  43.8 us
    psum x1, blocking collectives, local(): lax.psum((summed, squared, local_pixels), ('batch', 'rows'))  42 us
    psum x1, blocking collectives, local(): lax.psum((jnp.sum(grad_pre_a, axis=0), jnp.sum(grad_pre_a * normed_a, axi...  41.5 us
    psum x1, blocking collectives, local(): summed_b, squared_b = lax.psum((summed, squared), ('batch', 'rows'))  41.5 us
    unnamed x109, local copies, waits for them, and re-layouts  41.3 us
  transfers between devices with their start and end apart: 5, of which 1 were waited for; matrix products, arithmetic and copies ran while one was open for 16% of the time, Pallas kernels for 0%

commit v1 on v0

v1 whole, which is shorter than its diff:
```python
import functools
import math

import jax
import jax.numpy as jnp
from jax import lax
from jax.experimental import pallas as pl
from jax.experimental.pallas import tpu as pltpu
from jax.sharding import PartitionSpec as P

epsilon = 1e-05
axes = ("batch", "rows")
f32 = jnp.float32
bf16 = jnp.bfloat16
C0 = math.sqrt(2.0 / math.pi)
C1 = C0 * 0.044715
HIGH = lax.Precision.HIGHEST


def partner(block, mask):
    total = lax.axis_size("batch") * lax.axis_size("rows")
    return lax.ppermute(block, axes, [(i, i ^ mask) for i in range(total)])


def swapped_sum(block, groups):
    size = len(groups[0])
    spread = jnp.broadcast_to(block[None], (size,) + block.shape)
    arrived = lax.all_to_all(spread, "batch", 0, 0, axis_index_groups=groups, tiled=True)
    return jnp.sum(arrived, axis=0)


def summed_at_once(block):
    total = lax.axis_size("batch") * lax.axis_size("rows")
    spread = jnp.broadcast_to(block[None], (total,) + block.shape)
    return jnp.sum(lax.all_to_all(spread, axes, 0, 0, tiled=True), axis=0)


def summed_by_swap(block, near=None):
    block = block + partner(block, 1)
    count = lax.axis_size("batch")
    if near is None or count % near:
        return swapped_sum(block, [list(range(count))])
    block = swapped_sum(block, [list(range(i, i + near)) for i in range(0, count, near)])
    return swapped_sum(block, [list(range(i, count, near)) for i in range(near)])


def gelu_terms(u):
    square = u * u
    inner = C0 + C1 * square
    half = 0.5 * jnp.tanh(u * inner) + 0.5
    value = u * half
    slope = half + value * (1.0 - half) * (6.0 * inner - 4.0 * C0)
    return value, slope


def gelu_value(u):
    return u * (0.5 * jnp.tanh(u * (C0 + C1 * u * u)) + 0.5)


def moments(total, squares, pixels):
    mean = total / pixels
    return mean, lax.rsqrt(squares / pixels - mean * mean + epsilon)


def fold8(values):
    lanes = values.shape[-1]
    return jnp.sum(values.reshape(values.size // (8 * lanes), 8, lanes), axis=0)


def total_row(values):
    return jnp.sum(values, axis=0, keepdims=True)


def wide(ref, start):
    return jnp.concatenate([ref[start + i : start + i + 1, :] for i in range(4)], axis=1)


def put_wide(ref, start, row):
    for i in range(4):
        ref[start + i : start + i + 1, :] = row[:, i * 128 : (i + 1) * 128]


def dot_tn(a, b):
    return lax.dot_general(a, b, (((0,), (0,)), ((), ())), preferred_element_type=f32)


def dot_nt(a, b, precision=None):
    return lax.dot_general(
        a, b, (((1,), (1,)), ((), ())), preferred_element_type=f32, precision=precision
    )


def dot(a, b, precision=None):
    return jnp.dot(a, b, preferred_element_type=f32, precision=precision)


def split_two(values):
    high = values.astype(bf16)
    return high, (values - high.astype(f32)).astype(bf16)


def dot_halves(a, b):
    high, low = split_two(a)
    return dot(high, b) + dot(low, b)


def row_of_sums(values):
    high, low = split_two(values)
    one = jnp.ones((16, values.shape[1]), bf16)
    return (dot_nt(one, high) + dot_nt(one, low))[0:8, :]


def call(body, grid, ins, outs, scratch, name, flops, bytes_moved, aliases=None):
    return pl.pallas_call(
        body,
        grid=(grid,),
        in_specs=ins,
        out_specs=[spec for spec, _ in outs],
        out_shape=[shape for _, shape in outs],
        scratch_shapes=scratch,
        name=name,
        input_output_aliases=aliases or {},
        compiler_params=pltpu.CompilerParams(
            dimension_semantics=("arbitrary",), vmem_limit_bytes=52 << 20
        ),
        cost_estimate=pl.CostEstimate(
            flops=int(flops), bytes_accessed=int(bytes_moved), transcendentals=0
        ),
    )


SMEM = pl.BlockSpec(memory_space=pltpu.SMEM)
ANY = pl.BlockSpec(memory_space=pl.ANY)


def whole_spec(shape):
    return pl.BlockSpec(tuple(shape), lambda i: (0,) * len(shape))


def step_spec(shape, place=lambda i: i):
    return pl.BlockSpec(tuple(shape), lambda i: (place(i),) + (0,) * (len(shape) - 1))


def whole_out(shape, dtype=f32):
    return (whole_spec(shape), jax.ShapeDtypeStruct(shape, dtype))


def step_out(count, shape, dtype, place=lambda i: i):
    return (
        step_spec(shape, place),
        jax.ShapeDtypeStruct((count,) + tuple(shape[1:]), dtype),
    )


def live(info, images, lanes):
    return lax.broadcasted_iota(jnp.int32, (images, lanes), 0) < info[0]


def groups(columns):
    return [(c, min(4, columns - c)) for c in range(0, columns, 4)]


def take_edge(info, edge_ref, ref):
    step = pl.program_id(0)

    @pl.when((step == 0) & (info[1] == 1))
    def _():
        edge_ref[...] = ref[0].astype(edge_ref.dtype)

    @pl.when((step == pl.num_programs(0) - 1) & (info[1] == 0))
    def _():
        edge_ref[...] = ref[ref.shape[0] - 1].astype(edge_ref.dtype)


def first_body(info, x_ref, w_ref, z_ref, edge_ref, stat_ref, zacc):
    step = pl.program_id(0)
    tall, columns, images = x_ref.shape[:3]
    area = columns * images

    @pl.when(step == 0)
    def _():
        zacc[...] = jnp.zeros_like(zacc)

    mask = live(info, images, 128)
    for r in range(tall):
        x = x_ref[r].reshape(area, 512)
        z = dot(x, w_ref[...]).reshape(columns, images, 128)
        z = jnp.where(mask, z, 0.0)
        z_ref[r] = z
        zacc[0] += fold8(z)
        zacc[1] += fold8(z * z)
    take_edge(info, edge_ref, z_ref)

    @pl.when(step == pl.num_programs(0) - 1)
    def _():
        pixels = (info[0] * (pl.num_programs(0) * tall * columns)).astype(f32)
        stat_ref[...] = jnp.zeros_like(stat_ref)
        stat_ref[0:1, :] = total_row(zacc[0])
        stat_ref[1:2, :] = total_row(zacc[1])
        stat_ref[2:3, :] = jnp.full((1, 128), pixels, f32)


def cross_body(x_ref, z_ref, xz_ref, acc):
    step = pl.program_id(0)
    tall, columns, images = x_ref.shape[:3]
    area = columns * images

    @pl.when(step == 0)
    def _():
        acc[...] = jnp.zeros_like(acc)

    for r in range(tall):
        z = z_ref[r].astype(bf16).reshape(area, 128)
        acc[...] += dot_tn(z, x_ref[r].reshape(area, 512))

    @pl.when(step == pl.num_programs(0) - 1)
    def _():
        for i in range(4):
            xz_ref[i * 128 : (i + 1) * 128, :] = acc[:, i * 128 : (i + 1) * 128]


def paired_weights(w_ref, target):
    for r in range(4):
        for u in range(3):
            for o in range(2):
                t = r - o
                base = (r * 3 + u) * 128
                if 0 <= t <= 2:
                    block = w_ref[t, u]
                else:
                    block = jnp.zeros((128, 128), bf16)
                target[base : base + 128, o * 128 : (o + 1) * 128] = block


def window(frame, pair):
    columns, images = frame.shape[1] - 2, frame.shape[2]
    parts = [
        frame[2 * pair + r, u : u + columns].reshape(columns * images, 128)
        for r in range(4)
        for u in range(3)
    ]
    return jnp.concatenate(parts, axis=1)


def clear_frame(frame):
    tall, wide_columns = frame.shape[:2]
    zero = jnp.zeros(frame.shape[2:], frame.dtype)
    for e in range(tall):
        frame[e, 0] = zero
        frame[e, wide_columns - 1] = zero
    for c in range(wide_columns):
        frame[0, c] = zero
        frame[tall - 1, c] = zero


def middle_body(
    info, st1, ga, sa, z_ref, edge_ref, w_ref, xz_ref,
    z2_ref, a_ref, stat_ref, frame, wide_w, coef, zacc,
):
    step = pl.program_id(0)
    last = pl.num_programs(0) - 1
    columns, images = z_ref.shape[1:3]
    area = columns * images

    def activated(z):
        return gelu_value(z * coef[0:1, :] + coef[1:2, :]).astype(bf16)

    @pl.when(step == 0)
    def _():
        mean, inv = moments(st1[0:1, :], st1[1:2, :], st1[2:3, :])
        scale = ga[...] * inv
        coef[0:1, :] = scale
        coef[1:2, :] = sa[...] - mean * scale
        paired_weights(w_ref, wide_w)
        zacc[...] = jnp.zeros_like(zacc)
        clear_frame(frame)
        place = (1 - info[1]) * (frame.shape[0] - 1)
        for c, n in groups(columns):
            frame[place, 1 + c : 1 + c + n] = activated(edge_ref[c : c + n])

    @pl.when(step < last)
    def _():
        for r in range(2):
            for c, n in groups(columns):
                value = activated(z_ref[r, c : c + n])
                frame[2 * step + 1 + r, 1 + c : 1 + c + n] = value
                a_ref[r, c : c + n] = value

    @pl.when(step > 0)
    def _():
        mask = live(info, images, 128)
        y = dot(window(frame, step - 1), wide_w[...])
        for r in range(2):
            z = y[:, r * 128 : (r + 1) * 128].reshape(columns, images, 128)
            z2_ref[r] = z
            z = jnp.where(mask, z, 0.0)
            zacc[0] += fold8(z)
            zacc[1] += fold8(z * z)

    @pl.when(step == last)
    def _():
        stat_ref[...] = jnp.zeros_like(stat_ref)
        for k in range(2):
            stat_ref[k : k + 1, :] = total_row(zacc[k])


def second_coef(st1, st2, gb, sb, coef):
    mean, inv = moments(st2[0:1, :], st2[1:2, :], st1[2:3, :])
    scale = gb[...] * inv
    coef[0:1, :] = scale
    coef[1:2, :] = sb[...] - mean * scale
    coef[2:3, :] = inv
    coef[3:4, :] = -mean * inv


def second_body(
    info, st1, st2, gb, sb, z_ref, wo_ref,
    act_ref, g_ref, gx_ref, ye_ref, ze_ref, st_ref, gram_ref, coef, cross, sums,
):
    step = pl.program_id(0)
    tall, columns, images = z_ref.shape[:3]
    area = columns * images

    @pl.when(step == 0)
    def _():
        second_coef(st1, st2, gb, sb, coef)
        cross[...] = jnp.zeros_like(cross)
        sums[...] = jnp.zeros_like(sums)

    mask = live(info, images, 128)
    scale, bias, inv, shift = (coef[i : i + 1, :] for i in range(4))
    edge_row = (1 - info[1]) * (tall - 1)
    at_edge = step == (1 - info[1]) * (pl.num_programs(0) - 1)
    totals = [jnp.zeros((8, 128), f32) for _ in range(3)]
    for r in range(tall):
        acts, others = [], []
        for c, n in groups(columns):
            z = z_ref[r, c : c + n]
            value, slope = gelu_terms(z * scale + bias)
            dotted = jnp.where(mask, slope * (z * inv + shift), 0.0).astype(bf16)
            slope = jnp.where(mask, slope, 0.0).astype(bf16)
            g_ref[r, c : c + n] = slope
            gx_ref[r, c : c + n] = dotted
            value = value.astype(bf16)
            act_ref[r, c : c + n] = value
            value = jnp.where(mask, value, jnp.zeros((), bf16))
            acts.append(value.reshape(n * images, 128))
            for k, part in enumerate((slope, dotted, value)):
                totals[k] += fold8(part.astype(f32))
        acts = jnp.concatenate(acts, axis=0)
        cross[...] += dot_tn(
            acts,
            jnp.concatenate(
                [acts, g_ref[r].reshape(area, 128), gx_ref[r].reshape(area, 128)], axis=1
            ),
        )

        @pl.when(at_edge & (edge_row == r))
        def _():
            ye_ref[:, :, 0:128] = act_ref[r]
            ye_ref[:, :, 128:256] = g_ref[r]
            ze_ref[...] = z_ref[r]

    for k in range(3):
        sums[k] += totals[k]

    @pl.when(step == pl.num_programs(0) - 1)
    def _():
        gram = cross[:, 0:128]
        gram_ref[0:128, :] = gram
        st_ref[8:16, :] = jnp.zeros((8, 128), f32)
        st_ref[8:9, :] = total_row(sums[2])
        gram_ref[128:136, :] = st_ref[8:16, :]
        spread = dot_halves(gram_ref[...], wo_ref[...])
        put_wide(st_ref, 0, spread[128:129, :])
        put_wide(st_ref, 4, total_row(spread[0:128, :] * wo_ref[...].astype(f32)))
        st_ref[9:16, :] = jnp.zeros((7, 128), f32)
        for k in range(2):
            st_ref[9 + k : 10 + k, :] = total_row(sums[k])
        st_ref[16:144, :] = cross[:, 128:256]
        st_ref[144:272, :] = cross[:, 256:384]


def last_body(
    info, st1, st3, gc, sc, y_ref, g_ref, gx_ref, x_ref, cot_ref, wo_ref,
    out_ref, e_ref, t_ref, te_ref, st_ref, u_ref, ws_ref,
    coef, w_two, w_turn, z_buf, cross, sums, sums_b,
):
    step = pl.program_id(0)
    tall, columns, images = x_ref.shape[:3]
    area = columns * images

    @pl.when(step == 0)
    def _():
        mean, inv = moments(wide(st3, 0), wide(st3, 4), st1[2:3, 0:1])
        scale = gc[...] * inv
        coef[0:1, :] = sc[...] - mean * scale
        high, low = split_two(wo_ref[...].astype(f32) * scale)
        w_two[0:128, :] = high
        w_two[128:256, :] = low
        ws_ref[...] = w_two[...]
        w_turn[:, 0:128] = jnp.transpose(w_two[0:128, :])
        w_turn[:, 128:256] = jnp.transpose(w_two[128:256, :])
        cross[...] = jnp.zeros_like(cross)
        sums[...] = jnp.zeros_like(sums)
        sums_b[...] = jnp.zeros_like(sums_b)

    mask = live(info, images, 512)
    bias = coef[0:1, :]
    zero = jnp.zeros((), bf16)
    half = columns // 2
    parts = [(r, c) for r in range(tall) for c in range(0, columns, half)]
    n = half * images

    def product(r, c):
        act = y_ref[r, c : c + half].reshape(n, 128)
        z = dot(jnp.concatenate([act, act], axis=1), w_two[...])
        z_buf[r, c : c + half] = z.reshape(half, images, 512)

    def pointwise(r, first):
        total_e = jnp.zeros((8, 512), f32)
        total_x = jnp.zeros((8, 512), f32)
        for c in range(first, first + half):
            x = jnp.where(mask, x_ref[r, c], zero).astype(f32)
            total_x += fold8(x)
            value, slope = gelu_terms(z_buf[r, c] + (bias + x))
            out_ref[r, c] = value.astype(bf16)
            cot = jnp.where(mask, cot_ref[r, c], zero).astype(f32)
            e = slope * cot
            total_e += fold8(e)
            e_ref[r, c] = e.astype(bf16)
        sums[0] += total_e
        sums[1] += total_x

    def collect(r, c):
        e = e_ref[r, c : c + half].reshape(n, 512)
        cross[...] += dot_tn(y_ref[r, c : c + half].reshape(n, 128), e)
        y = dot(e, w_turn[...])
        t = (y[:, 0:128] + y[:, 128:256]).reshape(half, images, 128)
        t_ref[r, c : c + half] = t
        sums_b[0] += fold8(t * g_ref[r, c : c + half].astype(f32))
        sums_b[1] += fold8(t * gx_ref[r, c : c + half].astype(f32))

    product(*parts[0])
    for k in range(len(parts) + 1):
        if k + 1 < len(parts):
            product(*parts[k + 1])
        if k > 0:
            collect(*parts[k - 1])
        if k < len(parts):
            pointwise(*parts[k])
    take_edge(info, te_ref, t_ref)

    @pl.when(step == pl.num_programs(0) - 1)
    def _():
        u_ref[...] = cross[...]
        put_wide(st_ref, 0, total_row(sums[0]))
        put_wide(st_ref, 4, total_row(wo_ref[...].astype(f32) * cross[...]))
        put_wide(st_ref, 10, total_row(sums[1]))
        for k in range(2):
            st_ref[8 + k : 9 + k, :] = total_row(sums_b[k])
            st_ref[14 + k : 15 + k, :] = jnp.zeros((1, 128), f32)


def back_body(
    info, st1, st2, st3, st4, kept_ref, other_ref, own4, xz_ref, gram_ref, u_ref, ga, sa, gb, gc, wo_ref, ws_ref, wt_ref,
    y_ref, s_ref, ye_ref, z2_ref, ze_ref, t_ref, te_ref, a_ref, z1_ref, x_ref,
    h_ref, mine_ref, sent_ref, small_ref,
    coef, mm, wide_w, frame, dacc, vacc, sums, packed,
):
    step = pl.program_id(0)
    last = pl.num_programs(0) - 1
    columns, images = z1_ref.shape[1:3]
    area = columns * images
    mask = live(info, images, 128)

    def second_back(t, product, slope, z):
        kappa, scale_b, beta, alpha = (coef[i : i + 1, :] for i in range(4))
        through = t - kappa - product[..., 0:128] - product[..., 128:256]
        grad = scale_b * (slope.astype(f32) * through) - (alpha + beta * z)
        return jnp.where(mask, grad, 0.0).astype(bf16)

    @pl.when(step == 0)
    def _():
        pixels = st1[2:3, :]
        pixel = st1[2:3, 0:1]
        mean_a, inv_a = moments(st1[0:1, :], st1[1:2, :], pixels)
        mean_b, inv_b = moments(st2[0:1, :], st2[1:2, :], pixels)
        mean_c, inv_c = moments(wide(st3, 0), wide(st3, 4), pixel)
        total_c = wide(st4, 0)
        dot_c = inv_c * (wide(st4, 4) - mean_c * total_c)
        weights = wo_ref[...].astype(f32)
        scaled = ws_ref[0:128, :].astype(f32) + ws_ref[128:256, :].astype(f32)
        near, far = split_two(weights * (inv_c * dot_c / pixel))
        mat = dot_nt(near, ws_ref[0:128, :]) + dot_nt(near, ws_ref[128:256, :])
        mat = mat + dot_nt(far, ws_ref[0:128, :])
        high, low = split_two(mat)
        mm[:, 0:128] = high
        mm[:, 128:256] = low
        kappa = row_of_sums(scaled * (total_c / pixel))[0:1, :]
        mean_act = jnp.transpose(jnp.broadcast_to(st3[8:9, :] / pixels, (8, 128)))[:, 0:1]
        kappa = kappa - total_row(mean_act * mat)
        p_sum = jnp.where(info[1] == 0, kept_ref[...], other_ref[...])
        q_sum = jnp.where(info[1] == 0, other_ref[...], kept_ref[...])
        total_b = st4[8:9, :] - kappa * st3[9:10, :] - total_row(mat * p_sum)
        dot_b = st4[9:10, :] - kappa * st3[10:11, :] - total_row(mat * q_sum)
        scale_b = gb[...] * inv_b
        scale_a = ga[...] * inv_a
        coef[0:1, :] = kappa
        coef[1:2, :] = scale_b
        coef[2:3, :] = scale_b * inv_b * dot_b / pixels
        coef[3:4, :] = scale_b * (total_b - mean_b * inv_b * dot_b) / pixels
        coef[4:5, :] = scale_a
        coef[5:6, :] = sa[...] - mean_a * scale_a
        small_ref[...] = jnp.zeros_like(small_ref)
        put_wide(small_ref, 0, total_c)
        put_wide(small_ref, 4, dot_c)
        small_ref[8:9, :] = total_b
        small_ref[9:10, :] = dot_b
        column = jnp.transpose(gram_ref[128:136, :])[:, 0:1]
        product = dot_halves(gram_ref[0:128, :], wo_ref[...])
        grad = u_ref[...] - column * (total_c / pixel) - (product - column * mean_c) * (
            inv_c * dot_c / pixel
        )
        grad = grad * (gc[...] * inv_c)
        for i in range(4):
            packed[1152 + i * 128 : 1280 + i * 128, :] = grad[:, i * 128 : (i + 1) * 128]
        paired_weights(wt_ref, wide_w)
        dacc[...] = jnp.zeros_like(dacc)
        vacc[...] = jnp.zeros_like(vacc)
        sums[...] = jnp.zeros_like(sums)
        clear_frame(frame)
        place = (1 - info[1]) * (frame.shape[0] - 1)
        for c, n in groups(columns):
            act = ye_ref[c : c + n, :, 0:128].reshape(n * images, 128)
            extra = dot(act, mm[...]).reshape(n, images, 256)
            frame[place, 1 + c : 1 + c + n] = second_back(
                te_ref[c : c + n], extra, ye_ref[c : c + n, :, 128:256], ze_ref[c : c + n]
            )

    @pl.when(step < last)
    def _():
        for r in range(2):
            act = y_ref[r].reshape(area, 128)
            extra = dot(act, mm[...]).reshape(columns, images, 256)
            for c, n in groups(columns):
                frame[2 * step + 1 + r, 1 + c : 1 + c + n] = second_back(
                    t_ref[r, c : c + n],
                    extra[c : c + n],
                    s_ref[r, c : c + n],
                    z2_ref[r, c : c + n],
                )

    @pl.when(step > 0)
    def _():
        scale_a, bias_a = coef[4:5, :], coef[5:6, :]
        near = window(frame, step - 1)
        through = dot(near, wide_w[...])
        act = jnp.concatenate([a_ref[r].reshape(area, 128) for r in range(2)], axis=1)
        dacc[...] += dot_tn(act, near)
        total = jnp.zeros((8, 128), f32)
        dots = jnp.zeros((8, 128), f32)
        for r in range(2):
            part = through[:, r * 128 : (r + 1) * 128].reshape(columns, images, 128)
            for c, n in groups(columns):
                z = z1_ref[r, c : c + n]
                slope = gelu_terms(z * scale_a + bias_a)[1]
                grad = jnp.where(mask, part[c : c + n] * slope, 0.0)
                total += fold8(grad)
                dots += fold8(grad * z)
                h_ref[r, c : c + n] = grad.astype(bf16)
        sums[0] += total
        sums[1] += dots
        vacc[...] += dot_tn(h_ref[...].reshape(2 * area, 128), x_ref[...].reshape(2 * area, 512))

    @pl.when(step == last)
    def _():
        pixels = st1[2:3, :]
        total_h, dot_h = total_row(sums[0]), total_row(sums[1])
        tail = jnp.concatenate(
            [total_h, dot_h, st1[0:1, :] / pixels, jnp.zeros((5, 128), f32)], axis=0
        )
        columns2 = jnp.transpose(tail)
        column_h, mean_a = columns2[:, 0:1], columns2[:, 2:3]
        for i in range(4):
            lanes = slice(i * 128, (i + 1) * 128)
            center = st4[10 + i : 11 + i, :] / pixels
            packed[1664 + i * 128 : 1792 + i * 128, :] = vacc[:, lanes] - column_h * center
            packed[2176 + i * 128 : 2304 + i * 128, :] = (
                xz_ref[lanes, :] - mean_a * own4[10 + i : 11 + i, :]
            )
        for t in range(3):
            for u in range(3):
                parts = []
                for o in range(2):
                    base = ((o + 2 - t) * 3 + 2 - u) * 128
                    parts.append(dacc[o * 128 : (o + 1) * 128, base : base + 128])
                packed[(t * 3 + u) * 128 : (t * 3 + u + 1) * 128, :] = parts[0] + parts[1]
        if packed.shape[0] > 2688:
            packed[2688:, :] = jnp.zeros((packed.shape[0] - 2688, 128), f32)
        half = packed.shape[0] // 2
        low = info[1] == 0
        mine_ref[0:half, :] = jnp.where(low, packed[0:half, :], packed[half:, :])
        sent_ref[0:half, :] = jnp.where(low, packed[half:, :], packed[0:half, :])
        mine_ref[half : half + 8, :] = tail
        sent_ref[half : half + 8, :] = tail


def pack_body(mine_ref, arrived_ref, out_ref):
    shares, block = out_ref.shape[:2]
    share = (mine_ref.shape[0] - 8) // shares
    small = mine_ref[shares * share :, :] + arrived_ref[shares * share :, :]
    high = small.astype(bf16).astype(f32)
    middle = (small - high).astype(bf16).astype(f32)
    low = small - high - middle
    tail = jnp.concatenate(
        [high[0:2], middle[0:2], low[0:2], jnp.zeros((block - share - 6, 128), f32)], axis=0
    )
    for k in range(shares):
        rows = slice(k * share, (k + 1) * share)
        total = mine_ref[rows, :] + arrived_ref[rows, :]
        out_ref[k] = jnp.concatenate([total, tail], axis=0).astype(bf16)


def share_body(share, in_ref, small_ref, out_ref):
    total = in_ref[0].astype(f32)
    for k in range(1, in_ref.shape[0]):
        total = total + in_ref[k].astype(f32)
    sums = total[share : share + 2] + total[share + 2 : share + 4] + total[share + 4 : share + 6]
    small_ref[...] = jnp.concatenate([sums, jnp.zeros((6, 128), f32)], axis=0)
    for k in range(out_ref.shape[0]):
        out_ref[k] = total.astype(bf16)


def input_body(info, st1, st5, ga, wi_ref, h_ref, z_ref, e_ref, g_ref, coef, w_turn):
    step = pl.program_id(0)
    tall, columns, images = z_ref.shape[:3]
    area = columns * images

    @pl.when(step == 0)
    def _():
        pixels = st1[2:3, :]
        mean, inv = moments(st1[0:1, :], st1[1:2, :], pixels)
        scale = ga[...] * inv
        w_turn[...] = jnp.transpose(wi_ref[...])
        total = st5[0:1, :]
        dot_a = inv * (st5[1:2, :] - mean * total)
        coef[0:1, :] = scale
        coef[1:2, :] = scale * inv * dot_a / pixels
        coef[2:3, :] = scale * (total - mean * inv * dot_a) / pixels

    mask = live(info, images, 128)
    scale, beta, alpha = (coef[i : i + 1, :] for i in range(3))
    for r in range(tall):
        parts = []
        for c, n in groups(columns):
            grad = scale * h_ref[r, c : c + n].astype(f32) - (alpha + beta * z_ref[r, c : c + n])
            parts.append(jnp.where(mask, grad, 0.0).astype(bf16).reshape(n * images, 128))
        through = dot(jnp.concatenate(parts, axis=0), w_turn[...])
        through = through.reshape(columns, images, 512)
        for c in range(columns):
            g_ref[r, c] = (through[c] + e_ref[r, c].astype(f32)).astype(bf16)


def final_body(
    share, info, st1, st5, ga, small_ref, mine_ref, other_ref,
    gwi_ref, gga_ref, gsa_ref, gwm_ref, ggb_ref, gsb_ref, gwo_ref, ggc_ref, gsc_ref, total_ref,
):
    shares = mine_ref.shape[0]
    for k in range(shares):
        mine, other = mine_ref[k].astype(f32), other_ref[k].astype(f32)
        low = jnp.where(info[1] == 0, mine, other)
        high = jnp.where(info[1] == 0, other, mine)
        total_ref[k * share : (k + 1) * share, :] = low[0:share]
        total_ref[(shares + k) * share : (shares + k + 1) * share, :] = high[0:share]
    pixels = st1[2:3, :]
    mean, inv = moments(st1[0:1, :], st1[1:2, :], pixels)
    total = st5[0:1, :]
    dot = inv * (st5[1:2, :] - mean * total)
    gsa_ref[...] = total
    gga_ref[...] = dot
    gsb_ref[...] = small_ref[8:9, :]
    ggb_ref[...] = small_ref[9:10, :]
    gsc_ref[...] = wide(small_ref, 0)
    ggc_ref[...] = wide(small_ref, 4)
    gwm_ref[...] = total_ref[0:1152, :]
    for i in range(4):
        gwo_ref[:, i * 128 : (i + 1) * 128] = total_ref[1152 + i * 128 : 1280 + i * 128, :]
        v = jnp.transpose(total_ref[1664 + i * 128 : 1792 + i * 128, :])
        xz = jnp.transpose(total_ref[2176 + i * 128 : 2304 + i * 128, :])
        gwi_ref[i * 128 : (i + 1) * 128, :] = (ga[...] * inv) * (v - xz * (inv * dot / pixels))


def local(
    images, counts, w_in, gain_a, shift_a, w_mid, gain_b, shift_b, w_out, gain_c, shift_c, cotangent
):
    count, rows, columns, channels = images.shape
    steps = rows // 2
    info = jnp.stack([counts[0], lax.axis_index("rows").astype(jnp.int32)])
    images = jnp.transpose(images, (1, 2, 0, 3))
    cotangent = jnp.transpose(cotangent, (1, 2, 0, 3))
    ga, sa, gb, sb = (v.reshape(1, 128) for v in (gain_a, shift_a, gain_b, shift_b))
    gc, sc = gain_c.reshape(1, 512), shift_c.reshape(1, 512)
    small = whole_spec((1, 128))
    large = whole_spec((1, 512))
    eight = whole_spec((8, 128))
    taps = whole_spec((3, 3, 128, 128))

    def tile(lanes):
        return (2, columns, count, lanes)

    def edge(lanes):
        return (columns, count, lanes)

    def ahead(i):
        return jnp.minimum(i, steps - 1)

    def behind(i):
        return jnp.maximum(i - 1, 0)

    def frame_like():
        return pltpu.VMEM((rows + 2, columns + 2, count, 128), bf16)

    pixels = count * rows * columns

    z1, z1_edge, st1 = call(
        first_body,
        steps,
        [SMEM, step_spec(tile(512)), whole_spec((512, 128))],
        [
            step_out(rows, tile(128), f32),
            whole_out(edge(128)),
            whole_out((8, 128)),
        ],
        [pltpu.VMEM((2, 8, 128), f32)],
        "first_norm_sums",
        pixels * 512 * 128 * 2,
        pixels * 1536,
    )(info, images, w_in)
    z1_edge = partner(z1_edge, 1)
    st1 = summed_at_once(st1)
    xz = call(
        cross_body,
        steps,
        [step_spec(tile(512)), step_spec(tile(128))],
        [whole_out((512, 128))],
        [pltpu.VMEM((128, 512), f32)],
        "input_cross",
        pixels * 512 * 128 * 2,
        pixels * 1536,
    )(images, z1)[0]

    everyone = [list(range(lax.axis_size("batch")))]
    z2, act_a, st2 = call(
        middle_body,
        steps + 1,
        [
            SMEM, eight, small, small, step_spec(tile(128), ahead), whole_spec(edge(128)), taps,
            whole_spec((512, 128)),
        ],
        [
            step_out(rows, tile(128), f32, behind),
            step_out(rows, tile(128), bf16, ahead),
            whole_out((8, 128)),
        ],
        [
            frame_like(),
            pltpu.VMEM((1536, 256), bf16),
            pltpu.VMEM((8, 128), f32),
            pltpu.VMEM((2, 8, 128), f32),
        ],
        "middle_conv",
        pixels * 12 * 128 * 128 * 2,
        pixels * 1280,
    )(info, st1, ga, sa, z1, z1_edge, w_mid, xz)
    st2 = summed_by_swap(st2)

    act_b, slope_b, dotted_b, y_edge, z2_edge, st3, gram = call(
        second_body,
        steps,
        [SMEM, eight, eight, small, small, step_spec(tile(128)), whole_spec((128, 512))],
        [
            step_out(rows, tile(128), bf16),
            step_out(rows, tile(128), bf16),
            step_out(rows, tile(128), bf16),
            whole_out(edge(256), bf16),
            whole_out(edge(128)),
            whole_out((272, 128)),
            whole_out((136, 128)),
        ],
        [pltpu.VMEM((8, 128), f32), pltpu.VMEM((128, 384), f32), pltpu.VMEM((3, 8, 128), f32)],
        "second_norm",
        pixels * 384 * 128 * 2,
        pixels * 1280,
    )(info, st1, st2, gb, sb, z2, w_out)
    on_low = info[1] == 0
    kept = jnp.where(on_low, st3[16:144], st3[144:272])
    sent = jnp.where(on_low, st3[144:272], st3[16:144])
    arrived = partner(jnp.concatenate([st3[:16], sent]), 1)
    st3 = swapped_sum(st3[:16] + arrived[:16], everyone)
    kept = kept + arrived[16:]
    kept = swapped_sum(kept, everyone)
    y_edge = partner(y_edge, 1)
    z2_edge = partner(z2_edge, 1)

    block_out, e, t, t_edge, own4, u_local, w_scaled = call(
        last_body,
        steps,
        [
            SMEM, eight, whole_spec((16, 128)), large, large, step_spec(tile(128)),
            step_spec(tile(128)), step_spec(tile(128)), step_spec(tile(512)),
            step_spec(tile(512)), whole_spec((128, 512)),
        ],
        [
            step_out(rows, tile(512), bf16),
            step_out(rows, tile(512), bf16),
            step_out(rows, tile(128), f32),
            whole_out(edge(128)),
            whole_out((16, 128)),
            whole_out((128, 512)),
            whole_out((256, 512), bf16),
        ],
        [
            pltpu.VMEM((8, 512), f32),
            pltpu.VMEM((256, 512), bf16),
            pltpu.VMEM((512, 256), bf16),
            pltpu.VMEM(tile(512), f32),
            pltpu.VMEM((128, 512), f32),
            pltpu.VMEM((2, 8, 512), f32),
            pltpu.VMEM((2, 8, 128), f32),
        ],
        "last_norm",
        pixels * 512 * 128 * 10,
        pixels * 4864,
    )(info, st1, st3, gc, sc, act_b, slope_b, dotted_b, images, cotangent, w_out)

    own4, kept = lax.optimization_barrier((own4, kept))
    st4 = swapped_sum(own4 + partner(own4, 1), everyone)
    other = partner(kept, 1)
    t_edge = partner(t_edge, 1)

    w_back = jnp.swapaxes(w_mid[::-1, ::-1], 2, 3)
    shares = lax.axis_size("batch")
    share = -(-1344 // (8 * shares)) * 8
    half = share * shares
    block = -(-(share + 6) // 16) * 16
    h, mine, sent, small_sums = call(
        back_body,
        steps + 1,
        [
            SMEM, eight, eight, whole_spec((16, 128)), whole_spec((16, 128)),
            whole_spec((128, 128)), whole_spec((128, 128)), whole_spec((16, 128)),
            whole_spec((512, 128)), whole_spec((136, 128)),
            whole_spec((128, 512)), small, small, small, large, whole_spec((128, 512)),
            whole_spec((256, 512)), taps,
            step_spec(tile(128), ahead), step_spec(tile(128), ahead), whole_spec(edge(256)),
            step_spec(tile(128), ahead), whole_spec(edge(128)),
            step_spec(tile(128), ahead), whole_spec(edge(128)),
            step_spec(tile(128), behind), step_spec(tile(128), behind),
            step_spec(tile(512), behind),
        ],
        [
            step_out(rows, tile(128), bf16, behind),
            whole_out((half + 8, 128)),
            whole_out((half + 8, 128)),
            whole_out((16, 128)),
        ],
        [
            pltpu.VMEM((8, 128), f32),
            pltpu.VMEM((128, 256), bf16),
            pltpu.VMEM((1536, 256), bf16),
            frame_like(),
            pltpu.VMEM((256, 1536), f32),
            pltpu.VMEM((128, 512), f32),
            pltpu.VMEM((2, 8, 128), f32),
            pltpu.VMEM((2 * half, 128), f32),
        ],
        "middle_back",
        pixels * 32 * 128 * 128 * 2,
        pixels * 4000,
    )(
        info, st1, st2, st3, st4, kept, other, own4, xz, gram, u_local, ga, sa, gb, gc,
        w_out, w_scaled, w_back,
        act_b, slope_b, y_edge, z2, z2_edge, t, t_edge, act_a, z1, images,
    )
    arrived = partner(sent, 1)
    spread = call(
        pack_body,
        1,
        [whole_spec((half + 8, 128)), whole_spec((half + 8, 128))],
        [whole_out((shares, block, 128), bf16)],
        [],
        "pack_shares",
        1e6,
        2e6,
    )(mine, arrived)[0]
    spread = lax.all_to_all(spread, "batch", 0, 0, tiled=True)
    st5, spread = call(
        functools.partial(share_body, share),
        1,
        [whole_spec((shares, block, 128))],
        [whole_out((8, 128)), whole_out((shares, block, 128), bf16)],
        [],
        "sum_shares",
        1e6,
        1e6,
    )(spread)
    gathered = lax.all_to_all(spread, "batch", 0, 0, tiled=True)

    grad_images = call(
        input_body,
        steps,
        [
            SMEM, eight, eight, small, whole_spec((512, 128)),
            step_spec(tile(128)), step_spec(tile(128)), step_spec(tile(512)),
        ],
        [step_out(rows, tile(512), bf16)],
        [pltpu.VMEM((8, 128), f32), pltpu.VMEM((128, 512), bf16)],
        "input_grad",
        pixels * 512 * 128 * 2,
        pixels * 2816,
    )(info, st1, st5, ga, w_in, h, z1, e)[0]

    gathered, grad_images = lax.optimization_barrier((gathered, grad_images))
    shared = whole_spec((shares, block, 128))
    gwi, gga, gsa, gwm, ggb, gsb, gwo, ggc, gsc = call(
        functools.partial(final_body, share),
        1,
        [SMEM, eight, eight, small, whole_spec((16, 128)), shared, shared],
        [
            whole_out((512, 128)), whole_out((1, 128)), whole_out((1, 128)),
            whole_out((1152, 128)), whole_out((1, 128)), whole_out((1, 128)),
            whole_out((128, 512)), whole_out((1, 512)), whole_out((1, 512)),
        ],
        [pltpu.VMEM((2 * half, 128), f32)],
        "replicated_grads",
        1e6,
        3e6,
    )(info, st1, st5, ga, small_sums, gathered, partner(gathered, 1))
    return (
        jnp.transpose(block_out, (2, 0, 1, 3)),
        jnp.transpose(grad_images, (2, 0, 1, 3)),
        gwi,
        gga.reshape(128),
        gsa.reshape(128),
        gwm.reshape(3, 3, 128, 128),
        ggb.reshape(128),
        gsb.reshape(128),
        gwo,
        ggc.reshape(512),
        gsc.reshape(512),
    )


def solution(mesh):
    split = P("batch", "rows", None, None)
    placed = (split, P("batch"), P(), P(), P(), P(), P(), P(), P(), P(), P(), split)
    return jax.shard_map(
        local,
        mesh=mesh,
        in_specs=placed,
        out_specs=(split, split) + (P(),) * 9,
        check_vma=False,
    )
```

time: 899 us -> 215 us (0.24); the launches traced: 887 us -> 214 us
  local copies, waits for them, and re-layouts: 291 us -> 7.65 us
  blocking collectives: 244 us -> 15.9 us
  Pallas kernels: 0 us -> 124 us
  other arithmetic: 125 us -> 2.4 us
  matrix products: 121 us -> 0 us
  waiting for transfers between devices: 83.5 us -> 28.7 us
  starting transfers between devices: 6.76 us -> 34.2 us
  between operations: 15.5 us -> 1.59 us
    psum x6 -> x0, blocking collectives: 244 us -> none  [the longest x1 42 us: local(): lax.psum((summed, squared, local_pixels), ('batch', 'rows'))]
    reshape x21 -> x0, local copies, waits for them, and re-layouts: 159 us -> none  [the longest x16 96.7 us: tap_sum(): window = framed[:, row_start:row_start + strip_rows, col_start:col_start...]
    pallas_call x0 -> x10, Pallas kernels: none -> 124 us  [the longest x1 31.7 us: local(): call(last_body, steps, [SMEM, eight, whole_spec((16, 128)), large, large,...]
    dot_general x33 -> x0, matrix products: 121 us -> none  [the longest x9 28.5 us: tap_sum(): lax.dot_general(window, weights[row_tap, col_tap], (((1,), (1,)), ((), ()...]
    psum x1 -> x0, waiting for transfers between devices: 83.4 us -> none  [local(): lax.psum((weight_first, weight_mid, weight_last), ('batch', 'rows'))]
    convert_element_type x6 -> x0, other arithmetic: 60.9 us -> none  [the longest x1 20.1 us: local(): (cotangent * image_mask).reshape(-1, channels).astype(jnp.float32)]
    convert_element_type x2 -> x0, local copies, waits for them, and re-layouts: 55.3 us -> none  [local(): (cotangent * image_mask).reshape(-1, channels).astype(jnp.float32)]
    reduce_sum x1 -> x5, other arithmetic: 43.8 us -> 2.29 us  [the longest x4 2.25 us: swapped_sum(): return jnp.sum(arrived, axis=0)]
  transfers between devices with their start and end apart: 5 -> 16, of which waited for: 1 -> 8; matrix products, arithmetic and copies ran while one was open for 16% -> 3% of each run, Pallas kernels for 0% -> 27%
where the time goes in v1:
time: 215 us; the launch traced here: 214 us
  Pallas kernels  124 us (58%)
  starting transfers between devices  34.2 us (16%)
  waiting for transfers between devices  28.7 us (13%)
  blocking collectives  15.9 us (7%)
  local copies, waits for them, and re-layouts  7.65 us (4%)
  other arithmetic  2.4 us (1%)
    pallas_call x1, Pallas kernels, local(): call(last_body, steps, [SMEM, eight, whole_spec((16, 128)), large, large,...  31.7 us
    pallas_call x1, Pallas kernels, local(): call(back_body, steps + 1, [SMEM, eight, eight, whole_spec((16, 128)), wh...  26.8 us
    all_to_all x4, waiting for transfers between devices, swapped_sum(): lax.all_to_all(spread, 'batch', 0, 0, axis_index_groups=groups, tiled=True)  21.6 us
    all_to_all x4, starting transfers between devices, swapped_sum(): lax.all_to_all(spread, 'batch', 0, 0, axis_index_groups=groups, tiled=True)  21.5 us
    all_to_all x1, blocking collectives, local(): spread = lax.all_to_all(spread, 'batch', 0, 0, tiled=True)  15.9 us
    pallas_call x1, Pallas kernels, local(): call(input_body, steps, [SMEM, eight, eight, small, whole_spec((512, 128)...  15.8 us
    pallas_call x1, Pallas kernels, local(): call(second_body, steps, [SMEM, eight, eight, small, small, step_spec(til...  13.1 us
    pallas_call x1, Pallas kernels, local(): call(middle_body, steps + 1, [SMEM, eight, small, small, step_spec(tile(1...  12.5 us
  transfers between devices with their start and end apart: 16, of which 8 were waited for; matrix products, arithmetic and copies ran while one was open for 3% of the time, Pallas kernels for 27%

profile of v1, /device:TPU:0, one launch (start us, length us, event | category | flops | bytes accessed | tf_op | source)
XLA Modules:
  0.0 214.0 jit_solution(2330262421706052903)
XLA Ops:
  1.3 0.1 pad_add_fusion.info
  1.4 0.9 copy-done.1
  2.3 11.7 %first_norm_sums.1 = (f32[14,28,32,128]{3,2,1,0:T(8,128)}, f32[28,32,128]{2,1,0:T(8,128)S(1)}, f32[8,128]{1,0:T(8,128)S(1)}) custom-call(s32[2]{0:T(128)S(1)} %pad_add_fusion.info, bf16[14,28,32,512]{3,2,1,0:T(8,128)(2,1)} %bitcast.32, bf16[512,128]{1,0:T(8,128)(2,1)S(1)} %copy-done.1), custom_call_target="tpu_custom_call" | custom-call | flops 1644167168 | bytes 19267584 | tf_op jit(solution)/shard_map/first_norm_sums/pallas_call | solution.py:726
  13.9 0.5 collective-permute-start
  14.4 0.7 broadcast_in_dim.10
  15.1 7.0 %all-to-all-start = ((f32[32,8,128]{2,1,0:T(8,128)}), f32[32,8,128]{2,1,0:T(8,128)S(1)}, u32[]{:S(2)}, u32[]{:S(2)}) async-start(f32[32,8,128]{2,1,0:T(8,128)} %broadcast_in_dim.10), calls=%async_computation | async-start | bytes 262144 | tf_op jit(solution)/shard_map/all_to_all | solution.py:35
  22.0 0.0 copy-start.4
  22.0 0.0 copy-start.10
  22.1 9.3 %input_cross.1.xz_ref = f32[512,128]{1,0:T(8,128)S(1)} custom-call(bf16[14,28,32,512]{3,2,1,0:T(8,128)(2,1)} %bitcast.33, f32[14,28,32,128]{3,2,1,0:T(8,128)} %get-tuple-element.51.z_ref.z1_ref), custom_call_target="tpu_custom_call" | custom-call | flops 1644167168 | bytes 19267584 | tf_op jit(solution)/shard_map/input_cross/pallas_call | solution.py:742
  31.5 12.5 %middle_conv.1 = (f32[14,28,32,128]{3,2,1,0:T(8,128)}, bf16[14,28,32,128]{3,2,1,0:T(8,128)(2,1)}, f32[8,128]{1,0:T(8,128)S(1)}) custom-call(s32[2]{0:T(128)S(1)} %pad_add_fusion.info, f32[8,128]{1,0:T(8,128)S(1)} %reduce_sum.45.st1, f32[1,128]{1,0:T(1,128)S(1)} %bitcast.23, f32[1,128]{1,0:T(1,128)S(1)} %bitcast.30, ...), custom_call_target="tpu_custom_call" | custom-call | flops 4932501504 | bytes 16056320 | tf_op jit(solution)/shard_map/middle_conv/pallas_call | solution.py:754
  44.0 0.3 collective-permute-start.1
  44.3 0.9 collective-permute-done.1
  45.2 0.6 broadcast_in_dim.11
  45.8 6.8 %all-to-all-start.1 = ((f32[16,8,128]{2,1,0:T(8,128)}), f32[16,8,128]{2,1,0:T(8,128)S(1)}, u32[]{:S(2)}, u32[]{:S(2)}) async-start(f32[16,8,128]{2,1,0:T(8,128)} %broadcast_in_dim.11), calls=%async_computation.1 | async-start | bytes 131072 | tf_op jit(solution)/shard_map/all_to_all | solution.py:28
  52.7 7.5 %all-to-all-done.1 = f32[16,8,128]{2,1,0:T(8,128)S(1)} async-done(((f32[16,8,128]{2,1,0:T(8,128)}), f32[16,8,128]{2,1,0:T(8,128)S(1)}, u32[]{:S(2)}, u32[]{:S(2)}) %all-to-all-start.1) | async-done | bytes 65568 | tf_op jit(solution)/shard_map/all_to_all | solution.py:28
  60.3 13.1 %second_norm.1 = (bf16[14,28,32,128]{3,2,1,0:T(8,128)(2,1)}, bf16[14,28,32,128]{3,2,1,0:T(8,128)(2,1)}, bf16[14,28,32,128]{3,2,1,0:T(8,128)(2,1)}, bf16[28,32,25...) custom-call(s32[2]{0:T(128)S(1)} %pad_add_fusion.info, ...), custom_call_target="tpu_custom_call" | custom-call | flops 1233125376 | bytes 16056320 | tf_op jit(solution)/shard_map/second_norm/pallas_call | solution.py:778
  73.4 0.1 collective-permute-start.2
  73.5 1.3 collective-permute-done.2
  74.8 0.7 broadcast_in_dim.12
  75.4 3.5 %all-to-all-start.2 = ((f32[16,16,128]{2,1,0:T(8,128)}), f32[16,16,128]{2,1,0:T(8,128)S(1)}, u32[]{:S(2)}, u32[]{:S(2)}) async-start(f32[16,16,128]{2,1,0:T(8,128)} %broadcast_in_dim.12), calls=%async_computation.2 | async-start | bytes 262144 | tf_op jit(solution)/shard_map/all_to_all | solution.py:28
  79.0 8.0 %all-to-all-done.2 = f32[16,16,128]{2,1,0:T(8,128)S(1)} async-done(((f32[16,16,128]{2,1,0:T(8,128)}), f32[16,16,128]{2,1,0:T(8,128)S(1)}, u32[]{:S(2)}, u32[]{:S(2)}) %all-to-all-start.2) | async-done | bytes 131104 | tf_op jit(solution)/shard_map/all_to_all | solution.py:28
  87.0 1.1 broadcast_in_dim.13
  88.0 4.3 %all-to-all-start.3 = ((f32[16,128,128]{2,1,0:T(8,128)}), f32[16,128,128]{2,1,0:T(8,128)}, u32[]{:S(2)}, u32[]{:S(2)}) async-start(f32[16,128,128]{2,1,0:T(8,128)} %broadcast_in_dim.13), calls=%async_computation.3 | async-start | bytes 2097152 | tf_op jit(solution)/shard_map/all_to_all | solution.py:28
  92.4 0.1 collective-permute-start.5
  92.5 0.5 collective-permute-start.6
  93.0 31.7 %last_norm.1 = (bf16[14,28,32,512]{3,2,1,0:T(8,128)(2,1)}, bf16[14,28,32,512]{3,2,1,0:T(8,128)(2,1)}, f32[14,28,32,128]{3,2,1,0:T(8,128)}, f32[28,32,128]{2,1,0:...) custom-call(s32[2]{0:T(128)S(1)} %pad_add_fusion.info, ...), custom_call_target="tpu_custom_call" | custom-call | flops 8220835840 | bytes 61014016 | tf_op jit(solution)/shard_map/last_norm/pallas_call | solution.py:806
  124.7 0.1 collective-permute-start.7
  124.8 1.3 reduce_sum.48.kept_ref
  126.1 0.5 collective-permute-start.3
  126.6 0.8 collective-permute-done.3
  127.4 0.7 broadcast_in_dim.14
  128.1 6.8 %all-to-all-start.4 = ((f32[16,16,128]{2,1,0:T(8,128)}), f32[16,16,128]{2,1,0:T(8,128)}, u32[]{:S(2)}, u32[]{:S(2)}) async-start(f32[16,16,128]{2,1,0:T(8,128)} %broadcast_in_dim.14), calls=%async_computation.4 | async-start | bytes 262144 | tf_op jit(solution)/shard_map/all_to_all | solution.py:28
  134.9 0.9 copy.24
  135.8 0.1 collective-permute-start.4
  135.9 1.0 reverse_bitcast_fusion.wt_ref
  136.9 6.0 %all-to-all-done.4 = f32[16,16,128]{2,1,0:T(8,128)} async-done(((f32[16,16,128]{2,1,0:T(8,128)}), f32[16,16,128]{2,1,0:T(8,128)}, u32[]{:S(2)}, u32[]{:S(2)}) %all-to-all-start.4) | async-done | bytes 131104 | tf_op jit(solution)/shard_map/all_to_all | solution.py:28
  142.9 0.9 reduce_sum.49.st4
  143.9 26.8 %middle_back.1 = (bf16[14,28,32,128]{3,2,1,0:T(8,128)(2,1)}, f32[1416,128]{1,0:T(8,128)}, f32[1416,128]{1,0:T(8,128)}, f32[16,128]{1,0:T(8,128)S(1)}) custom-call(s32[2]{0:T(128)S(1)} %pad_add_fusion.info, f32[8,128]{1,0:T(8,128)S(1)} %reduce_sum.45.st1, f32[8,128]{1,0:T(8,128)S(1)} %reduce_sum.46.st2, f32[16,128]{1,0:T(8,128)S(1)} %reduce_sum.47.st3, ...), custom_call_target="tpu_custom_call" | custom-call | flops 13153337344 | bytes 50176000 | tf_op jit(solution)/shard_map/middle_back/pallas_call | solution.py:847
  170.7 0.1 collective-permute-start.8
  170.8 2.4 %collective-permute-done.8.arrived_ref = f32[1416,128]{1,0:T(8,128)S(1)} collective-permute-done((f32[1416,128]{1,0:T(8,128)}, f32[1416,128]{1,0:T(8,128)S(1)}, u32[]{:S(2)}, u32[]{:S(2)}) %collective-permute-start.8) | collective-permute-done | bytes 725024 | tf_op jit(solution)/shard_map/ppermute | solution.py:22
  173.2 1.1 copy-done
  174.3 0.1 pack_shares.1
  174.4 15.9 %all_to_all.35.in_ref = bf16[16,96,128]{2,1,0:T(8,128)(2,1)S(1)} all-to-all(bf16[16,96,128]{2,1,0:T(8,128)(2,1)S(1)} %pack_shares.1), channel_id=1, replica_groups=mesh['batch'=16,'rows'=2] {'batch'}, dimensions={0} | all-to-all | bytes 786432 | tf_op jit(solution)/shard_map/all_to_all | solution.py:897
  190.3 0.8 sum_shares.1
  191.1 3.6 %all-to-all-start.6 = ((bf16[16,96,128]{2,1,0:T(8,128)(2,1)}), bf16[16,96,128]{2,1,0:T(8,128)(2,1)S(1)}, u32[]{:S(2)}, u32[]{:S(2)}) async-start(bf16[16,96,128]{2,1,0:T(8,128)(2,1)} %get-tuple-element.73), calls=%async_computation.6 | async-start | bytes 786432 | tf_op jit(solution)/shard_map/all_to_all | solution.py:908
  194.7 15.8 %input_grad.1 = bf16[14,28,32,512]{3,2,1,0:T(8,128)(2,1)} custom-call(s32[2]{0:T(128)S(1)} %pad_add_fusion.info, f32[8,128]{1,0:T(8,128)S(1)} %reduce_sum.45.st1, f32[8,128]{1,0:T(8,128)S(1)} %get-tuple-element.74.st5, f32[1,128]{1,0:T(1,128)S(1)} %bitcast.25, bf16[512,128]{1,0:T(8,128)(2,1)S(1)} %copy-done.2, ...), custom_call_target="tpu_custom_call" | custom-call | flops 1644167168 | bytes 35323904 | tf_op jit(solution)/shard_map/input_grad/pallas_call | solution.py:910
  210.5 1.7 collective-permute-done.9.other_ref
  212.3 1.7 replicated_grads.1
  (37 shorter events, 0.2 us)
Async XLA Ops:
  1.4 0.9 copy-start.1
  13.9 17.5 %collective-permute-start = (f32[28,32,128]{2,1,0:T(8,128)S(1)}, f32[28,32,128]{2,1,0:T(8,128)S(1)}, u32[]{:S(2)}, u32[]{:S(2)}) collective-permute-start(f32[28,32,128]{2,1,0:T(8,128)S(1)} %get-tuple-element.52), channel_id=1, source_target_pairs={{0,1},{1,0},{2,3},{3,2},{4,5},{5,4},{6,7},{7,6},{8,9},{9,8},{10,11... | collective-permute-start | bytes 1376264 | tf_op jit(solution)/shard_map/ppermute | solution.py:22
  15.1 16.3 %all-to-all-start = ((f32[32,8,128]{2,1,0:T(8,128)}), f32[32,8,128]{2,1,0:T(8,128)S(1)}, u32[]{:S(2)}, u32[]{:S(2)}) async-start(f32[32,8,128]{2,1,0:T(8,128)} %broadcast_in_dim.10), calls=%async_computation | async-start | bytes 262144 | tf_op jit(solution)/shard_map/all_to_all | solution.py:35
  22.0 9.4 %copy-start.4 = (bf16[3,3,128,128]{3,2,1,0:T(8,128)(2,1)S(1)}, bf16[3,3,128,128]{3,2,1,0:T(8,128)(2,1)}, u32[]{:S(2)}) copy-start(bf16[3,3,128,128]{3,2,1,0:T(8,128)(2,1)} %w_ref.3) | copy-start | bytes 884740
  22.0 9.4 %copy-start.7 = (f32[128]{0:T(128)S(1)}, f32[128]{0:T(128)}, u32[]{:S(2)}) copy-start(f32[128]{0:T(128)} %param.15) | copy-start | bytes 1540
  22.0 9.4 %copy-start.10 = (f32[128]{0:T(128)S(1)}, f32[128]{0:T(128)}, u32[]{:S(2)}) copy-start(f32[128]{0:T(128)} %param.16) | copy-start | bytes 1540
  31.4 28.8 %copy-start.3 = (bf16[128,512]{1,0:T(8,128)(2,1)S(1)}, bf16[128,512]{1,0:T(8,128)(2,1)}, u32[]{:S(2)}) copy-start(bf16[128,512]{1,0:T(8,128)(2,1)} %wo_ref.5) | copy-start | bytes 393220
  31.4 28.8 %copy-start.8 = (f32[128]{0:T(128)S(1)}, f32[128]{0:T(128)}, u32[]{:S(2)}) copy-start(f32[128]{0:T(128)} %param.19) | copy-start | bytes 1540
  31.4 28.8 %copy-start.9 = (f32[128]{0:T(128)S(1)}, f32[128]{0:T(128)}, u32[]{:S(2)}) copy-start(f32[128]{0:T(128)} %param.18) | copy-start | bytes 1540
  44.0 49.0 %copy-start.5 = (f32[512]{0:T(512)S(1)}, f32[512]{0:T(512)}, u32[]{:S(2)}) copy-start(f32[512]{0:T(512)} %param.22) | copy-start | bytes 6148
  44.0 49.0 %copy-start.6 = (f32[512]{0:T(512)S(1)}, f32[512]{0:T(512)}, u32[]{:S(2)}) copy-start(f32[512]{0:T(512)} %param.21) | copy-start | bytes 6148
  44.0 1.2 collective-permute-start.1
  45.8 14.4 %all-to-all-start.1 = ((f32[16,8,128]{2,1,0:T(8,128)}), f32[16,8,128]{2,1,0:T(8,128)S(1)}, u32[]{:S(2)}, u32[]{:S(2)}) async-start(f32[16,8,128]{2,1,0:T(8,128)} %broadcast_in_dim.11), calls=%async_computation.1 | async-start | bytes 131072 | tf_op jit(solution)/shard_map/all_to_all | solution.py:28
  73.4 1.3 collective-permute-start.2
  75.4 11.5 %all-to-all-start.2 = ((f32[16,16,128]{2,1,0:T(8,128)}), f32[16,16,128]{2,1,0:T(8,128)S(1)}, u32[]{:S(2)}, u32[]{:S(2)}) async-start(f32[16,16,128]{2,1,0:T(8,128)} %broadcast_in_dim.12), calls=%async_computation.2 | async-start | bytes 262144 | tf_op jit(solution)/shard_map/all_to_all | solution.py:28
  88.0 36.8 %all-to-all-start.3 = ((f32[16,128,128]{2,1,0:T(8,128)}), f32[16,128,128]{2,1,0:T(8,128)}, u32[]{:S(2)}, u32[]{:S(2)}) async-start(f32[16,128,128]{2,1,0:T(8,128)} %broadcast_in_dim.13), calls=%async_computation.3 | async-start | bytes 2097152 | tf_op jit(solution)/shard_map/all_to_all | solution.py:28
  92.4 51.5 %collective-permute-start.5 = (bf16[28,32,256]{2,1,0:T(8,128)(2,1)S(1)}, bf16[28,32,256]{2,1,0:T(8,128)(2,1)S(1)}, u32[]{:S(2)}, u32[]{:S(2)}) collective-permute-start(bf16[28,32,256]{2,1,0:T(8,128)(2,1)S(1)} %get-tuple-element.66), channel_id=1, source_target_pairs={{0,1},{1,0},{2,3},{3,2},{4,5},{5,4},{6,7},{7,6},{8,9},{9,8},{10,11... | collective-permute-start | bytes 1376264 | tf_op jit(solution)/shard_map/ppermute | solution.py:22
  92.5 51.4 %collective-permute-start.6 = (f32[28,32,128]{2,1,0:T(8,128)S(1)}, f32[28,32,128]{2,1,0:T(8,128)}, u32[]{:S(2)}, u32[]{:S(2)}) collective-permute-start(f32[28,32,128]{2,1,0:T(8,128)S(1)} %get-tuple-element.67), channel_id=1, source_target_pairs={{0,1},{1,0},{2,3},{3,2},{4,5},{5,4},{6,7},{7,6},{8,9},{9,8},{10,11... | collective-permute-start | bytes 1376264 | tf_op jit(solution)/shard_map/ppermute | solution.py:22
  124.7 19.1 %collective-permute-start.7 = (f32[28,32,128]{2,1,0:T(8,128)S(1)}, f32[28,32,128]{2,1,0:T(8,128)}, u32[]{:S(2)}, u32[]{:S(2)}) collective-permute-start(f32[28,32,128]{2,1,0:T(8,128)S(1)} %get-tuple-element.69), channel_id=1, source_target_pairs={{0,1},{1,0},{2,3},{3,2},{4,5},{5,4},{6,7},{7,6},{8,9},{9,8},{10,11... | collective-permute-start | bytes 1376264 | tf_op jit(solution)/shard_map/ppermute | solution.py:22
  126.1 1.3 collective-permute-start.3
  128.1 14.8 %all-to-all-start.4 = ((f32[16,16,128]{2,1,0:T(8,128)}), f32[16,16,128]{2,1,0:T(8,128)}, u32[]{:S(2)}, u32[]{:S(2)}) async-start(f32[16,16,128]{2,1,0:T(8,128)} %broadcast_in_dim.14), calls=%async_computation.4 | async-start | bytes 262144 | tf_op jit(solution)/shard_map/all_to_all | solution.py:28
  135.8 8.0 %collective-permute-start.4 = (f32[128,128]{1,0:T(8,128)S(1)}, f32[128,128]{1,0:T(8,128)S(1)}, u32[]{:S(2)}, u32[]{:S(2)}) collective-permute-start(f32[128,128]{1,0:T(8,128)S(1)} %reduce_sum.48.kept_ref), channel_id=1, source_target_pairs={{0,1},{1,0},{2,3},{3,2},{4,5},{5,4},{6,7},{7,6},{8,9},{9,8},{10,11... | collective-permute-start | bytes 196616 | tf_op jit(solution)/shard_map/ppermute | solution.py:22
  143.9 50.8 %copy-start.2 = (bf16[512,128]{1,0:T(8,128)(2,1)S(1)}, bf16[512,128]{1,0:T(8,128)(2,1)}, u32[]{:S(2)}) copy-start(bf16[512,128]{1,0:T(8,128)(2,1)} %wi_ref.1) | copy-start | bytes 393220
  170.7 2.5 %collective-permute-start.8 = (f32[1416,128]{1,0:T(8,128)}, f32[1416,128]{1,0:T(8,128)S(1)}, u32[]{:S(2)}, u32[]{:S(2)}) collective-permute-start(f32[1416,128]{1,0:T(8,128)} %get-tuple-element.72), channel_id=1, source_target_pairs={{0,1},{1,0},{2,3},{3,2},{4,5},{5,4},{6,7},{7,6},{8,9},{9,8},{10,11... | collective-permute-start | bytes 2174984 | tf_op jit(solution)/shard_map/ppermute | solution.py:22
  173.2 1.1 copy-start
  191.1 19.5 %all-to-all-start.6 = ((bf16[16,96,128]{2,1,0:T(8,128)(2,1)}), bf16[16,96,128]{2,1,0:T(8,128)(2,1)S(1)}, u32[]{:S(2)}, u32[]{:S(2)}) async-start(bf16[16,96,128]{2,1,0:T(8,128)(2,1)} %get-tuple-element.73), calls=%async_computation.6 | async-start | bytes 786432 | tf_op jit(solution)/shard_map/all_to_all | solution.py:908
  210.5 1.7 collective-permute-start.9

commit v2 on v1

--- a/solution.py
+++ b/solution.py
@@ -315,7 +315,7 @@
 
 def second_body(
     info, st1, st2, gb, sb, z_ref, wo_ref,
-    act_ref, g_ref, gx_ref, ye_ref, ze_ref, st_ref, gram_ref, coef, cross, sums,
+    act_ref, g_ref, gx_ref, ye_ref, ze_ref, st_ref, keep_ref, gram_ref, coef, cross, sums,
 ):
     step = pl.program_id(0)
     tall, columns, images = z_ref.shape[:3]
@@ -377,8 +377,9 @@
         st_ref[9:16, :] = jnp.zeros((7, 128), f32)
         for k in range(2):
             st_ref[9 + k : 10 + k, :] = total_row(sums[k])
-        st_ref[16:144, :] = cross[:, 128:256]
-        st_ref[144:272, :] = cross[:, 256:384]
+        low = info[1] == 0
+        keep_ref[...] = jnp.where(low, cross[:, 128:256], cross[:, 256:384])
+        st_ref[16:144, :] = jnp.where(low, cross[:, 256:384], cross[:, 128:256])
 
 
 def last_body(
@@ -408,47 +409,57 @@
     mask = live(info, images, 512)
     bias = coef[0:1, :]
     zero = jnp.zeros((), bf16)
-    half = columns // 2
-    parts = [(r, c) for r in range(tall) for c in range(0, columns, half)]
-    n = half * images
+    piece = columns // 4
+    parts = [(r, c) for r in range(tall) for c in range(0, columns, piece)]
+    n = piece * images
 
     def product(r, c):
-        act = y_ref[r, c : c + half].reshape(n, 128)
+        act = y_ref[r, c : c + piece].reshape(n, 128)
         z = dot(jnp.concatenate([act, act], axis=1), w_two[...])
-        z_buf[r, c : c + half] = z.reshape(half, images, 512)
-
-    def pointwise(r, first):
-        total_e = jnp.zeros((8, 512), f32)
-        total_x = jnp.zeros((8, 512), f32)
-        for c in range(first, first + half):
-            x = jnp.where(mask, x_ref[r, c], zero).astype(f32)
-            total_x += fold8(x)
-            value, slope = gelu_terms(z_buf[r, c] + (bias + x))
-            out_ref[r, c] = value.astype(bf16)
-            cot = jnp.where(mask, cot_ref[r, c], zero).astype(f32)
-            e = slope * cot
-            total_e += fold8(e)
-            e_ref[r, c] = e.astype(bf16)
-        sums[0] += total_e
-        sums[1] += total_x
+        z_buf[r, c : c + piece] = z.reshape(piece, images, 512)
+
+    def pointwise(r, c):
+        x = jnp.where(mask, x_ref[r, c], zero).astype(f32)
+        value, slope = gelu_terms(z_buf[r, c] + (bias + x))
+        out_ref[r, c] = value.astype(bf16)
+        cot = jnp.where(mask, cot_ref[r, c], zero).astype(f32)
+        e = slope * cot
+        e_ref[r, c] = e.astype(bf16)
+        return fold8(e), fold8(x)
 
     def collect(r, c):
-        e = e_ref[r, c : c + half].reshape(n, 512)
-        cross[...] += dot_tn(y_ref[r, c : c + half].reshape(n, 128), e)
-        y = dot(e, w_turn[...])
-        t = (y[:, 0:128] + y[:, 128:256]).reshape(half, images, 128)
-        t_ref[r, c : c + half] = t
-        sums_b[0] += fold8(t * g_ref[r, c : c + half].astype(f32))
-        sums_b[1] += fold8(t * gx_ref[r, c : c + half].astype(f32))
+        e = e_ref[r, c : c + piece].reshape(n, 512)
+        cross[...] += dot_tn(y_ref[r, c : c + piece].reshape(n, 128), e)
+
+    def through(r, c):
+        y = dot(e_ref[r, c : c + piece].reshape(n, 512), w_turn[...])
+        t = (y[:, 0:128] + y[:, 128:256]).reshape(piece, images, 128)
+        t_ref[r, c : c + piece] = t
+        sums_b[0] += fold8(t * g_ref[r, c : c + piece].astype(f32))
+        sums_b[1] += fold8(t * gx_ref[r, c : c + piece].astype(f32))
 
     product(*parts[0])
     for k in range(len(parts) + 1):
+        work = []
         if k + 1 < len(parts):
-            product(*parts[k + 1])
+            work.append(functools.partial(product, *parts[k + 1]))
         if k > 0:
-            collect(*parts[k - 1])
+            work.append(functools.partial(through, *parts[k - 1]))
+            work.append(functools.partial(collect, *parts[k - 1]))
         if k < len(parts):
-            pointwise(*parts[k])
+            r, first = parts[k]
+            total_e = jnp.zeros((8, 512), f32)
+            total_x = jnp.zeros((8, 512), f32)
+            for c in range(piece):
+                if c % 2 == 0 and work:
+                    work.pop(0)()
+                add_e, add_x = pointwise(r, first + c)
+                total_e += add_e
+                total_x += add_x
+            sums[0] += total_e
+            sums[1] += total_x
+        for rest in work:
+            rest()
     take_edge(info, te_ref, t_ref)
 
     @pl.when(step == pl.num_programs(0) - 1)
@@ -500,8 +511,8 @@
         kappa = row_of_sums(scaled * (total_c / pixel))[0:1, :]
         mean_act = jnp.transpose(jnp.broadcast_to(st3[8:9, :] / pixels, (8, 128)))[:, 0:1]
         kappa = kappa - total_row(mean_act * mat)
-        p_sum = jnp.where(info[1] == 0, kept_ref[...], other_ref[...])
-        q_sum = jnp.where(info[1] == 0, other_ref[...], kept_ref[...])
+        p_sum = jnp.where(info[1] == 0, kept_ref[...], other_ref[16:144, :])
+        q_sum = jnp.where(info[1] == 0, other_ref[16:144, :], kept_ref[...])
         total_b = st4[8:9, :] - kappa * st3[9:10, :] - total_row(mat * p_sum)
         dot_b = st4[9:10, :] - kappa * st3[10:11, :] - total_row(mat * q_sum)
         scale_b = gb[...] * inv_b
@@ -749,6 +760,8 @@
         pixels * 512 * 128 * 2,
         pixels * 1536,
     )(images, z1)[0]
+    w_back = jnp.swapaxes(w_mid[::-1, ::-1], 2, 3)
+    xz, w_back = lax.optimization_barrier((xz, w_back))
 
     everyone = [list(range(lax.axis_size("batch")))]
     z2, act_a, st2 = call(
@@ -775,7 +788,7 @@
     )(info, st1, ga, sa, z1, z1_edge, w_mid, xz)
     st2 = summed_by_swap(st2)
 
-    act_b, slope_b, dotted_b, y_edge, z2_edge, st3, gram = call(
+    act_b, slope_b, dotted_b, y_edge, z2_edge, head, kept, gram = call(
         second_body,
         steps,
         [SMEM, eight, eight, small, small, step_spec(tile(128)), whole_spec((128, 512))],
@@ -785,7 +798,8 @@
             step_out(rows, tile(128), bf16),
             whole_out(edge(256), bf16),
             whole_out(edge(128)),
-            whole_out((272, 128)),
+            whole_out((144, 128)),
+            whole_out((128, 128)),
             whole_out((136, 128)),
         ],
         [pltpu.VMEM((8, 128), f32), pltpu.VMEM((128, 384), f32), pltpu.VMEM((3, 8, 128), f32)],
@@ -793,13 +807,10 @@
         pixels * 384 * 128 * 2,
         pixels * 1280,
     )(info, st1, st2, gb, sb, z2, w_out)
-    on_low = info[1] == 0
-    kept = jnp.where(on_low, st3[16:144], st3[144:272])
-    sent = jnp.where(on_low, st3[144:272], st3[16:144])
-    arrived = partner(jnp.concatenate([st3[:16], sent]), 1)
-    st3 = swapped_sum(st3[:16] + arrived[:16], everyone)
-    kept = kept + arrived[16:]
-    kept = swapped_sum(kept, everyone)
+    arrived = partner(head, 1)
+    st3 = swapped_sum(head[:16] + arrived[:16], everyone)
+    st3, kept, arrived = lax.optimization_barrier((st3, kept, arrived))
+    kept = swapped_sum(kept + arrived[16:], everyone)
     y_edge = partner(y_edge, 1)
     z2_edge = partner(z2_edge, 1)
 
@@ -834,12 +845,11 @@
         pixels * 4864,
     )(info, st1, st3, gc, sc, act_b, slope_b, dotted_b, images, cotangent, w_out)
 
-    own4, kept = lax.optimization_barrier((own4, kept))
-    st4 = swapped_sum(own4 + partner(own4, 1), everyone)
-    other = partner(kept, 1)
+    arrived = partner(jnp.concatenate([own4, kept]), 1)
+    st4 = swapped_sum(own4 + arrived[:16], everyone)
+    other = arrived
     t_edge = partner(t_edge, 1)
 
-    w_back = jnp.swapaxes(w_mid[::-1, ::-1], 2, 3)
     shares = lax.axis_size("batch")
     share = -(-1344 // (8 * shares)) * 8
     half = share * shares
@@ -849,7 +859,7 @@
         steps + 1,
         [
             SMEM, eight, eight, whole_spec((16, 128)), whole_spec((16, 128)),
-            whole_spec((128, 128)), whole_spec((128, 128)), whole_spec((16, 128)),
+            whole_spec((128, 128)), whole_spec((144, 128)), whole_spec((16, 128)),
             whole_spec((512, 128)), whole_spec((136, 128)),
             whole_spec((128, 512)), small, small, small, large, whole_spec((128, 512)),
             whole_spec((256, 512)), taps,

time: 215 us -> 210 us (0.977)
  blocking collectives: 15.9 us -> 55 us
  waiting for transfers between devices: 28.7 us -> 6.55 us
  starting transfers between devices: 34.2 us -> 16.8 us
  local copies, waits for them, and re-layouts: 7.65 us -> 4.11 us
    all_to_all x0 -> x3, blocking collectives: none -> 39.2 us  [swapped_sum(): lax.all_to_all(spread, 'batch', 0, 0, axis_index_groups=groups, tiled=True)]
    all_to_all x4 -> x1, waiting for transfers between devices: 21.6 us -> 0.01 us  [swapped_sum(): lax.all_to_all(spread, 'batch', 0, 0, axis_index_groups=groups, tiled=True)]
    all_to_all x4 -> x1, starting transfers between devices: 21.5 us -> 4.34 us  [swapped_sum(): lax.all_to_all(spread, 'batch', 0, 0, axis_index_groups=groups, tiled=True)]
    ppermute x10 -> x9, waiting for transfers between devices: 7.11 us -> 6.55 us  [partner(): return lax.ppermute(block, axes, [(i, i ^ mask) for i in range(total)])]
  transfers between devices with their start and end apart: 16 -> 12, of which waited for: 8 -> 5; matrix products, arithmetic and copies ran while one was open for 3% -> 0% of each run, Pallas kernels for 27% -> 27%
where the time goes in v2:
time: 210 us; the launch traced here: 209 us
  Pallas kernels  123 us (59%)
  blocking collectives  55 us (26%)
  starting transfers between devices  16.8 us (8%)
  waiting for transfers between devices  6.55 us (3%)
  local copies, waits for them, and re-layouts  4.11 us (2%)
    all_to_all x3, blocking collectives, swapped_sum(): lax.all_to_all(spread, 'batch', 0, 0, axis_index_groups=groups, tiled=True)  39.2 us
    pallas_call x1, Pallas kernels, local(): call(last_body, steps, [SMEM, eight, whole_spec((16, 128)), large, large,...  31.3 us
    pallas_call x1, Pallas kernels, local(): call(back_body, steps + 1, [SMEM, eight, eight, whole_spec((16, 128)), wh...  26.8 us
    all_to_all x1, blocking collectives, local(): spread = lax.all_to_all(spread, 'batch', 0, 0, tiled=True)  15.8 us
    pallas_call x1, Pallas kernels, local(): call(input_body, steps, [SMEM, eight, eight, small, whole_spec((512, 128)...  15.8 us
    pallas_call x1, Pallas kernels, local(): call(second_body, steps, [SMEM, eight, eight, small, small, step_spec(til...  13.2 us
    pallas_call x1, Pallas kernels, local(): call(middle_body, steps + 1, [SMEM, eight, small, small, step_spec(tile(1...  12.5 us
    pallas_call x1, Pallas kernels, local(): call(first_body, steps, [SMEM, step_spec(tile(512)), whole_spec((512, 128...  11.7 us
  transfers between devices with their start and end apart: 12, of which 5 were waited for; matrix products, arithmetic and copies ran while one was open for 0% of the time, Pallas kernels for 27%

profile of v2, /device:TPU:0, one launch (start us, length us, event | category | flops | bytes accessed | tf_op | source)
XLA Modules:
  0.0 208.8 jit_solution(1879434412220954266)
XLA Ops:
  1.3 0.1 pad_add_fusion.info
  1.4 0.9 copy-done.1
  2.3 11.7 %first_norm_sums.1 = (f32[14,28,32,128]{3,2,1,0:T(8,128)}, f32[28,32,128]{2,1,0:T(8,128)S(1)}, f32[8,128]{1,0:T(8,128)S(1)}) custom-call(s32[2]{0:T(128)S(1)} %pad_add_fusion.info, bf16[14,28,32,512]{3,2,1,0:T(8,128)(2,1)} %bitcast.32, bf16[512,128]{1,0:T(8,128)(2,1)S(1)} %copy-done.1), custom_call_target="tpu_custom_call" | custom-call | flops 1644167168 | bytes 19267584 | tf_op jit(solution)/shard_map/first_norm_sums/pallas_call | solution.py:737
  14.0 0.4 collective-permute-start
  14.4 0.7 broadcast_in_dim.10
  15.1 7.0 %all-to-all-start = ((f32[32,8,128]{2,1,0:T(8,128)}), f32[32,8,128]{2,1,0:T(8,128)S(1)}, u32[]{:S(2)}, u32[]{:S(2)}) async-start(f32[32,8,128]{2,1,0:T(8,128)} %broadcast_in_dim.10), calls=%async_computation | async-start | bytes 262144 | tf_op jit(solution)/shard_map/all_to_all | solution.py:35
  22.1 0.2 copy.24
  22.3 0.0 copy-start.7
  22.3 0.0 copy-start.10
  22.4 9.2 %input_cross.1.xz_ref = f32[512,128]{1,0:T(8,128)S(1)} custom-call(bf16[14,28,32,512]{3,2,1,0:T(8,128)(2,1)} %bitcast.33, f32[14,28,32,128]{3,2,1,0:T(8,128)} %get-tuple-element.55.z_ref.z1_ref), custom_call_target="tpu_custom_call" | custom-call | flops 1644167168 | bytes 19267584 | tf_op jit(solution)/shard_map/input_cross/pallas_call | solution.py:753
  31.6 0.0 all-to-all-done
  31.7 0.0 copy-start.3
  31.7 0.0 copy-start.8
  31.7 0.0 copy-start.9
  31.7 12.5 %middle_conv.1 = (f32[14,28,32,128]{3,2,1,0:T(8,128)}, bf16[14,28,32,128]{3,2,1,0:T(8,128)(2,1)}, f32[8,128]{1,0:T(8,128)S(1)}) custom-call(s32[2]{0:T(128)S(1)} %pad_add_fusion.info, f32[8,128]{1,0:T(8,128)S(1)} %reduce_sum.45.st1, f32[1,128]{1,0:T(1,128)S(1)} %bitcast.23, f32[1,128]{1,0:T(1,128)S(1)} %bitcast.30, ...), custom_call_target="tpu_custom_call" | custom-call | flops 4932501504 | bytes 16056320 | tf_op jit(solution)/shard_map/middle_conv/pallas_call | solution.py:767
  44.2 0.3 collective-permute-start.1
  44.5 0.9 collective-permute-done.1
  45.4 14.2 %all_to_all.35 = f32[16,8,128]{2,1,0:T(8,128)S(1)} all-to-all(f32[16,8,128]{2,1,0:T(8,128)S(1)} %broadcast_in_dim.11), channel_id=1, replica_groups={{0,2,4,6,8,10,12,14,16,18,20,22,24,26,28,30},{1,3,5,7,9,11,13,15,17,19,..., dimensions={0} | all-to-all | bytes 131072 | tf_op jit(solution)/shard_map/all_to_all | solution.py:28
  59.7 13.2 %second_norm.1 = (bf16[14,28,32,128]{3,2,1,0:T(8,128)(2,1)}, bf16[14,28,32,128]{3,2,1,0:T(8,128)(2,1)}, bf16[14,28,32,128]{3,2,1,0:T(8,128)(2,1)}, bf16[28,32,25...) custom-call(s32[2]{0:T(128)S(1)} %pad_add_fusion.info, ...), custom_call_target="tpu_custom_call" | custom-call | flops 1233125376 | bytes 16056320 | tf_op jit(solution)/shard_map/second_norm/pallas_call | solution.py:791
  72.8 0.0 collective-permute-start.2
  72.8 1.3 collective-permute-done.2
  74.1 10.6 %all_to_all.36 = f32[16,16,128]{2,1,0:T(8,128)S(1)} all-to-all(f32[16,16,128]{2,1,0:T(8,128)S(1)} %broadcast_in_dim.12), channel_id=1, replica_groups={{0,2,4,6,8,10,12,14,16,18,20,22,24,26,28,30},{1,3,5,7,9,11,13,15,17,19,..., dimensions={0} | all-to-all | bytes 262144 | tf_op jit(solution)/shard_map/all_to_all | solution.py:28
  84.8 1.1 broadcast_in_dim.13
  85.9 4.3 %all-to-all-start.3 = ((f32[16,128,128]{2,1,0:T(8,128)}), f32[16,128,128]{2,1,0:T(8,128)}, u32[]{:S(2)}, u32[]{:S(2)}) async-start(f32[16,128,128]{2,1,0:T(8,128)} %broadcast_in_dim.13), calls=%async_computation.3 | async-start | bytes 2097152 | tf_op jit(solution)/shard_map/all_to_all | solution.py:28
  90.3 31.3 %last_norm.1 = (bf16[14,28,32,512]{3,2,1,0:T(8,128)(2,1)}, bf16[14,28,32,512]{3,2,1,0:T(8,128)(2,1)}, f32[14,28,32,128]{3,2,1,0:T(8,128)}, f32[28,32,128]{2,1,0:...) custom-call(s32[2]{0:T(128)S(1)} %pad_add_fusion.info, ...), custom_call_target="tpu_custom_call" | custom-call | flops 8220835840 | bytes 61014016 | tf_op jit(solution)/shard_map/last_norm/pallas_call | solution.py:817
  121.6 0.0 all-to-all-done.3
  121.6 1.3 reduce_sum.48.kept_ref
  122.9 0.1 collective-permute-start.3
  123.0 0.5 collective-permute-start.4
  123.5 0.1 collective-permute-start.5
  123.6 0.4 collective-permute-start.6
  124.0 0.2 collective-permute-done.3.other_ref
  124.3 14.4 %all_to_all.37 = f32[16,16,128]{2,1,0:T(8,128)S(1)} all-to-all(f32[16,16,128]{2,1,0:T(8,128)S(1)} %broadcast_in_dim.14), channel_id=1, replica_groups={{0,2,4,6,8,10,12,14,16,18,20,22,24,26,28,30},{1,3,5,7,9,11,13,15,17,19,..., dimensions={0} | all-to-all | bytes 262144 | tf_op jit(solution)/shard_map/all_to_all | solution.py:28
  138.7 0.0 collective-permute-done.6.te_ref
  138.7 0.0 copy-start.2
  138.7 26.8 %middle_back.1 = (bf16[14,28,32,128]{3,2,1,0:T(8,128)(2,1)}, f32[1416,128]{1,0:T(8,128)}, f32[1416,128]{1,0:T(8,128)}, f32[16,128]{1,0:T(8,128)S(1)}) custom-call(s32[2]{0:T(128)S(1)} %pad_add_fusion.info, f32[8,128]{1,0:T(8,128)S(1)} %reduce_sum.45.st1, f32[8,128]{1,0:T(8,128)S(1)} %reduce_sum.46.st2, f32[16,128]{1,0:T(8,128)S(1)} %reduce_sum.47.st3, ...), custom_call_target="tpu_custom_call" | custom-call | flops 13153337344 | bytes 50176000 | tf_op jit(solution)/shard_map/middle_back/pallas_call | solution.py:857
  165.6 0.1 collective-permute-start.7
  165.7 2.4 %collective-permute-done.7.arrived_ref = f32[1416,128]{1,0:T(8,128)S(1)} collective-permute-done((f32[1416,128]{1,0:T(8,128)}, f32[1416,128]{1,0:T(8,128)S(1)}, u32[]{:S(2)}, u32[]{:S(2)}) %collective-permute-start.7) | collective-permute-done | bytes 725024 | tf_op jit(solution)/shard_map/ppermute | solution.py:22
  168.1 1.1 copy-done
  169.2 0.1 pack_shares.1
  169.3 15.8 %all_to_all.38.in_ref = bf16[16,96,128]{2,1,0:T(8,128)(2,1)S(1)} all-to-all(bf16[16,96,128]{2,1,0:T(8,128)(2,1)S(1)} %pack_shares.1), channel_id=1, replica_groups=mesh['batch'=16,'rows'=2] {'batch'}, dimensions={0} | all-to-all | bytes 786432 | tf_op jit(solution)/shard_map/all_to_all | solution.py:907
  185.1 0.8 sum_shares.1
  185.9 3.6 %all-to-all-start.6 = ((bf16[16,96,128]{2,1,0:T(8,128)(2,1)}), bf16[16,96,128]{2,1,0:T(8,128)(2,1)S(1)}, u32[]{:S(2)}, u32[]{:S(2)}) async-start(bf16[16,96,128]{2,1,0:T(8,128)(2,1)} %get-tuple-element.81), calls=%async_computation.6 | async-start | bytes 786432 | tf_op jit(solution)/shard_map/all_to_all | solution.py:918
  189.6 15.8 %input_grad.1 = bf16[14,28,32,512]{3,2,1,0:T(8,128)(2,1)} custom-call(s32[2]{0:T(128)S(1)} %pad_add_fusion.info, f32[8,128]{1,0:T(8,128)S(1)} %reduce_sum.45.st1, f32[8,128]{1,0:T(8,128)S(1)} %get-tuple-element.82.st5, f32[1,128]{1,0:T(1,128)S(1)} %bitcast.25, bf16[512,128]{1,0:T(8,128)(2,1)S(1)} %copy-done.2, ...), custom_call_target="tpu_custom_call" | custom-call | flops 1644167168 | bytes 35323904 | tf_op jit(solution)/shard_map/input_grad/pallas_call | solution.py:920
  205.4 0.0 all-to-all-done.6.mine_ref
  205.4 0.0 collective-permute-start.8
  205.4 1.7 collective-permute-done.8.other_ref
  207.1 1.7 replicated_grads.1
  (30 shorter events, 0.2 us)
Async XLA Ops:
  1.4 0.9 copy-start.1
  2.3 19.8 %copy-start.4 = (bf16[3,3,128,128]{3,2,1,0:T(8,128)(2,1)S(1)}, bf16[3,3,128,128]{3,2,1,0:T(8,128)(2,1)}, u32[]{:S(2)}) copy-start(bf16[3,3,128,128]{3,2,1,0:T(8,128)(2,1)} %w_ref.3) | copy-start | bytes 884740
  14.0 17.7 %collective-permute-start = (f32[28,32,128]{2,1,0:T(8,128)S(1)}, f32[28,32,128]{2,1,0:T(8,128)S(1)}, u32[]{:S(2)}, u32[]{:S(2)}) collective-permute-start(f32[28,32,128]{2,1,0:T(8,128)S(1)} %get-tuple-element.56), channel_id=1, source_target_pairs={{0,1},{1,0},{2,3},{3,2},{4,5},{5,4},{6,7},{7,6},{8,9},{9,8},{10,11... | collective-permute-start | bytes 1376264 | tf_op jit(solution)/shard_map/ppermute | solution.py:22
  15.1 16.5 %all-to-all-start = ((f32[32,8,128]{2,1,0:T(8,128)}), f32[32,8,128]{2,1,0:T(8,128)S(1)}, u32[]{:S(2)}, u32[]{:S(2)}) async-start(f32[32,8,128]{2,1,0:T(8,128)} %broadcast_in_dim.10), calls=%async_computation | async-start | bytes 262144 | tf_op jit(solution)/shard_map/all_to_all | solution.py:35
  22.3 9.3 %copy-start.7 = (f32[128]{0:T(128)S(1)}, f32[128]{0:T(128)}, u32[]{:S(2)}) copy-start(f32[128]{0:T(128)} %param.15) | copy-start | bytes 1540
  22.3 9.3 %copy-start.10 = (f32[128]{0:T(128)S(1)}, f32[128]{0:T(128)}, u32[]{:S(2)}) copy-start(f32[128]{0:T(128)} %param.16) | copy-start | bytes 1540
  31.7 28.0 %copy-start.3 = (bf16[128,512]{1,0:T(8,128)(2,1)S(1)}, bf16[128,512]{1,0:T(8,128)(2,1)}, u32[]{:S(2)}) copy-start(bf16[128,512]{1,0:T(8,128)(2,1)} %wo_ref.5) | copy-start | bytes 393220
  31.7 28.0 %copy-start.8 = (f32[128]{0:T(128)S(1)}, f32[128]{0:T(128)}, u32[]{:S(2)}) copy-start(f32[128]{0:T(128)} %param.19) | copy-start | bytes 1540
  31.7 28.0 %copy-start.9 = (f32[128]{0:T(128)S(1)}, f32[128]{0:T(128)}, u32[]{:S(2)}) copy-start(f32[128]{0:T(128)} %param.18) | copy-start | bytes 1540
  44.2 46.0 %copy-start.5 = (f32[512]{0:T(512)S(1)}, f32[512]{0:T(512)}, u32[]{:S(2)}) copy-start(f32[512]{0:T(512)} %param.22) | copy-start | bytes 6148
  44.2 46.0 %copy-start.6 = (f32[512]{0:T(512)S(1)}, f32[512]{0:T(512)}, u32[]{:S(2)}) copy-start(f32[512]{0:T(512)} %param.21) | copy-start | bytes 6148
  44.2 1.2 collective-permute-start.1
  72.8 1.3 collective-permute-start.2
  85.9 35.7 %all-to-all-start.3 = ((f32[16,128,128]{2,1,0:T(8,128)}), f32[16,128,128]{2,1,0:T(8,128)}, u32[]{:S(2)}, u32[]{:S(2)}) async-start(f32[16,128,128]{2,1,0:T(8,128)} %broadcast_in_dim.13), calls=%async_computation.3 | async-start | bytes 2097152 | tf_op jit(solution)/shard_map/all_to_all | solution.py:28
  122.9 1.3 collective-permute-start.3
  123.0 15.7 %collective-permute-start.4 = (bf16[28,32,256]{2,1,0:T(8,128)(2,1)S(1)}, bf16[28,32,256]{2,1,0:T(8,128)(2,1)S(1)}, u32[]{:S(2)}, u32[]{:S(2)}) collective-permute-start(bf16[28,32,256]{2,1,0:T(8,128)(2,1)S(1)} %get-tuple-element.74), channel_id=1, source_target_pairs={{0,1},{1,0},{2,3},{3,2},{4,5},{5,4},{6,7},{7,6},{8,9},{9,8},{10,11... | collective-permute-start | bytes 1376264 | tf_op jit(solution)/shard_map/ppermute | solution.py:22
  123.5 15.2 %collective-permute-start.5 = (f32[28,32,128]{2,1,0:T(8,128)S(1)}, f32[28,32,128]{2,1,0:T(8,128)}, u32[]{:S(2)}, u32[]{:S(2)}) collective-permute-start(f32[28,32,128]{2,1,0:T(8,128)S(1)} %get-tuple-element.75), channel_id=1, source_target_pairs={{0,1},{1,0},{2,3},{3,2},{4,5},{5,4},{6,7},{7,6},{8,9},{9,8},{10,11... | collective-permute-start | bytes 1376264 | tf_op jit(solution)/shard_map/ppermute | solution.py:22
  123.6 15.2 %collective-permute-start.6 = (f32[28,32,128]{2,1,0:T(8,128)S(1)}, f32[28,32,128]{2,1,0:T(8,128)}, u32[]{:S(2)}, u32[]{:S(2)}) collective-permute-start(f32[28,32,128]{2,1,0:T(8,128)S(1)} %get-tuple-element.77), channel_id=1, source_target_pairs={{0,1},{1,0},{2,3},{3,2},{4,5},{5,4},{6,7},{7,6},{8,9},{9,8},{10,11... | collective-permute-start | bytes 1376264 | tf_op jit(solution)/shard_map/ppermute | solution.py:22
  138.7 50.8 %copy-start.2 = (bf16[512,128]{1,0:T(8,128)(2,1)S(1)}, bf16[512,128]{1,0:T(8,128)(2,1)}, u32[]{:S(2)}) copy-start(bf16[512,128]{1,0:T(8,128)(2,1)} %wi_ref.1) | copy-start | bytes 393220
  165.6 2.5 %collective-permute-start.7 = (f32[1416,128]{1,0:T(8,128)}, f32[1416,128]{1,0:T(8,128)S(1)}, u32[]{:S(2)}, u32[]{:S(2)}) collective-permute-start(f32[1416,128]{1,0:T(8,128)} %get-tuple-element.80), channel_id=1, source_target_pairs={{0,1},{1,0},{2,3},{3,2},{4,5},{5,4},{6,7},{7,6},{8,9},{9,8},{10,11... | collective-permute-start | bytes 2174984 | tf_op jit(solution)/shard_map/ppermute | solution.py:22
  168.1 1.1 copy-start
  185.9 19.5 %all-to-all-start.6 = ((bf16[16,96,128]{2,1,0:T(8,128)(2,1)}), bf16[16,96,128]{2,1,0:T(8,128)(2,1)S(1)}, u32[]{:S(2)}, u32[]{:S(2)}) async-start(bf16[16,96,128]{2,1,0:T(8,128)(2,1)} %get-tuple-element.81), calls=%async_computation.6 | async-start | bytes 786432 | tf_op jit(solution)/shard_map/all_to_all | solution.py:918
  205.4 1.7 collective-permute-start.8

commit v3 on v2

--- a/solution.py
+++ b/solution.py
@@ -14,6 +14,9 @@
 bf16 = jnp.bfloat16
 C0 = math.sqrt(2.0 / math.pi)
 C1 = C0 * 0.044715
+K0 = -2.0 * C0 / math.log(2.0)
+K1 = -2.0 * C1 / math.log(2.0)
+K2 = -3.0 * math.log(2.0)
 HIGH = lax.Precision.HIGHEST
 
 
@@ -27,6 +30,10 @@
     spread = jnp.broadcast_to(block[None], (size,) + block.shape)
     arrived = lax.all_to_all(spread, "batch", 0, 0, axis_index_groups=groups, tiled=True)
     return jnp.sum(arrived, axis=0)
+
+
+def swapped(spread):
+    return lax.all_to_all(spread, "batch", 0, 0, tiled=True)
 
 
 def summed_at_once(block):
@@ -44,17 +51,20 @@
     return swapped_sum(block, [list(range(i, count, near)) for i in range(near)])
 
 
+def gate(u):
+    inner = K0 + K1 * (u * u)
+    return pltpu.reciprocal(1.0 + jnp.exp2(u * inner), approx=True), inner
+
+
 def gelu_terms(u):
-    square = u * u
-    inner = C0 + C1 * square
-    half = 0.5 * jnp.tanh(u * inner) + 0.5
+    half, inner = gate(u)
     value = u * half
-    slope = half + value * (1.0 - half) * (6.0 * inner - 4.0 * C0)
+    slope = half + value * (1.0 - half) * (K2 * inner - 4.0 * C0)
     return value, slope
 
 
 def gelu_value(u):
-    return u * (0.5 * jnp.tanh(u * (C0 + C1 * u * u)) + 0.5)
+    return u * gate(u)[0]
 
 
 def moments(total, squares, pixels):
@@ -110,7 +120,7 @@
     return (dot_nt(one, high) + dot_nt(one, low))[0:8, :]
 
 
-def call(body, grid, ins, outs, scratch, name, flops, bytes_moved, aliases=None):
+def call(body, grid, ins, outs, scratch, name, flops, bytes_moved):
     return pl.pallas_call(
         body,
         grid=(grid,),
@@ -119,7 +129,6 @@
         out_shape=[shape for _, shape in outs],
         scratch_shapes=scratch,
         name=name,
-        input_output_aliases=aliases or {},
         compiler_params=pltpu.CompilerParams(
             dimension_semantics=("arbitrary",), vmem_limit_bytes=52 << 20
         ),
@@ -293,9 +302,8 @@
         for r in range(2):
             z = y[:, r * 128 : (r + 1) * 128].reshape(columns, images, 128)
             z2_ref[r] = z
-            z = jnp.where(mask, z, 0.0)
-            zacc[0] += fold8(z)
-            zacc[1] += fold8(z * z)
+            zacc[0] += fold8(jnp.where(mask, jnp.sum(z, axis=0), 0.0))
+            zacc[1] += fold8(jnp.where(mask, jnp.sum(z * z, axis=0), 0.0))
 
     @pl.when(step == last)
     def _():
@@ -331,22 +339,21 @@
     scale, bias, inv, shift = (coef[i : i + 1, :] for i in range(4))
     edge_row = (1 - info[1]) * (tall - 1)
     at_edge = step == (1 - info[1]) * (pl.num_programs(0) - 1)
-    totals = [jnp.zeros((8, 128), f32) for _ in range(3)]
+    totals = [jnp.zeros((images, 128), f32) for _ in range(3)]
     for r in range(tall):
         acts, others = [], []
         for c, n in groups(columns):
             z = z_ref[r, c : c + n]
             value, slope = gelu_terms(z * scale + bias)
-            dotted = jnp.where(mask, slope * (z * inv + shift), 0.0).astype(bf16)
-            slope = jnp.where(mask, slope, 0.0).astype(bf16)
+            dotted = slope * (z * inv + shift)
+            slope, dotted, value = (v.astype(bf16) for v in (slope, dotted, value))
+            for k, part in enumerate((slope, dotted, value)):
+                totals[k] += jnp.sum(part.astype(f32), axis=0)
             g_ref[r, c : c + n] = slope
             gx_ref[r, c : c + n] = dotted
-            value = value.astype(bf16)
             act_ref[r, c : c + n] = value
             value = jnp.where(mask, value, jnp.zeros((), bf16))
             acts.append(value.reshape(n * images, 128))
-            for k, part in enumerate((slope, dotted, value)):
-                totals[k] += fold8(part.astype(f32))
         acts = jnp.concatenate(acts, axis=0)
         cross[...] += dot_tn(
             acts,
@@ -362,7 +369,7 @@
             ze_ref[...] = z_ref[r]
 
     for k in range(3):
-        sums[k] += totals[k]
+        sums[k] += fold8(jnp.where(mask, totals[k], 0.0))
 
     @pl.when(step == pl.num_programs(0) - 1)
     def _():
@@ -382,9 +389,31 @@
         st_ref[16:144, :] = jnp.where(low, cross[:, 256:384], cross[:, 128:256])
 
 
+def spread_body(head_ref, arrived_ref, keep_ref, out_ref):
+    sums = head_ref[0:16, :] + arrived_ref[0:16, :]
+    share = 128 // out_ref.shape[0]
+    for k in range(out_ref.shape[0]):
+        rows = slice(k * share, (k + 1) * share)
+        out_ref[k, 0:16] = sums
+        out_ref[k, 16 : 16 + share] = keep_ref[rows, :] + arrived_ref[16 + k * share : 16 + (k + 1) * share, :]
+        if share < 8:
+            out_ref[k, 16 + share :] = jnp.zeros((8 - share, 128), f32)
+
+
+def both_body(info, own_ref, arrived_ref, out_ref):
+    sums = own_ref[0:16, :] + arrived_ref[0:16, :]
+    mine, other = own_ref[16:, :], arrived_ref[16:, :]
+    low = info[1] == 0
+    block = jnp.concatenate(
+        [sums, jnp.where(low, mine, other), jnp.where(low, other, mine)], axis=0
+    )
+    for k in range(out_ref.shape[0]):
+        out_ref[k] = block
+
+
 def last_body(
-    info, st1, st3, gc, sc, y_ref, g_ref, gx_ref, x_ref, cot_ref, wo_ref,
-    out_ref, e_ref, t_ref, te_ref, st_ref, u_ref, ws_ref,
+    info, st1, in3, gc, sc, y_ref, g_ref, gx_ref, x_ref, cot_ref, wo_ref,
+    out_ref, e_ref, t_ref, te_ref, st_ref, st3, u_ref, ws_ref,
     coef, w_two, w_turn, z_buf, cross, sums, sums_b,
 ):
     step = pl.program_id(0)
@@ -393,6 +422,11 @@
 
     @pl.when(step == 0)
     def _():
+        total = in3[0]
+        for k in range(1, in3.shape[0]):
+            total = total + in3[k]
+        st3[...] = total[0:16]
+        st_ref[16:, :] = total[16:]
         mean, inv = moments(wide(st3, 0), wide(st3, 4), st1[2:3, 0:1])
         scale = gc[...] * inv
         coef[0:1, :] = sc[...] - mean * scale
@@ -474,10 +508,10 @@
 
 
 def back_body(
-    info, st1, st2, st3, st4, kept_ref, other_ref, own4, xz_ref, gram_ref, u_ref, ga, sa, gb, gc, wo_ref, ws_ref, wt_ref,
+    info, st1, st2, st3, in4, own4, xz_ref, gram_ref, u_ref, ga, sa, gb, gc, wo_ref, ws_ref, wt_ref,
     y_ref, s_ref, ye_ref, z2_ref, ze_ref, t_ref, te_ref, a_ref, z1_ref, x_ref,
     h_ref, mine_ref, sent_ref, small_ref,
-    coef, mm, wide_w, frame, dacc, vacc, sums, packed,
+    coef, mm, wide_w, frame, dacc, vacc, sums, packed, st4, pq,
 ):
     step = pl.program_id(0)
     last = pl.num_programs(0) - 1
@@ -498,6 +532,16 @@
         mean_a, inv_a = moments(st1[0:1, :], st1[1:2, :], pixels)
         mean_b, inv_b = moments(st2[0:1, :], st2[1:2, :], pixels)
         mean_c, inv_c = moments(wide(st3, 0), wide(st3, 4), pixel)
+        total = in4[0, 0:16]
+        share = 128 // in4.shape[0]
+        span = (in4.shape[1] - 16) // 2
+        for k in range(in4.shape[0]):
+            if k > 0:
+                total = total + in4[k, 0:16]
+            rows = slice(k * share, (k + 1) * share)
+            pq[0, rows] = in4[k, 16 : 16 + share]
+            pq[1, rows] = in4[k, 16 + span : 16 + span + share]
+        st4[...] = total
         total_c = wide(st4, 0)
         dot_c = inv_c * (wide(st4, 4) - mean_c * total_c)
         weights = wo_ref[...].astype(f32)
@@ -511,10 +555,8 @@
         kappa = row_of_sums(scaled * (total_c / pixel))[0:1, :]
         mean_act = jnp.transpose(jnp.broadcast_to(st3[8:9, :] / pixels, (8, 128)))[:, 0:1]
         kappa = kappa - total_row(mean_act * mat)
-        p_sum = jnp.where(info[1] == 0, kept_ref[...], other_ref[16:144, :])
-        q_sum = jnp.where(info[1] == 0, other_ref[16:144, :], kept_ref[...])
-        total_b = st4[8:9, :] - kappa * st3[9:10, :] - total_row(mat * p_sum)
-        dot_b = st4[9:10, :] - kappa * st3[10:11, :] - total_row(mat * q_sum)
+        total_b = st4[8:9, :] - kappa * st3[9:10, :] - total_row(mat * pq[0])
+        dot_b = st4[9:10, :] - kappa * st3[10:11, :] - total_row(mat * pq[1])
         scale_b = gb[...] * inv_b
         scale_a = ga[...] * inv_a
         coef[0:1, :] = kappa
@@ -576,7 +618,7 @@
             for c, n in groups(columns):
                 z = z1_ref[r, c : c + n]
                 slope = gelu_terms(z * scale_a + bias_a)[1]
-                grad = jnp.where(mask, part[c : c + n] * slope, 0.0)
+                grad = part[c : c + n] * slope
                 total += fold8(grad)
                 dots += fold8(grad * z)
                 h_ref[r, c : c + n] = grad.astype(bf16)
@@ -763,6 +805,8 @@
     w_back = jnp.swapaxes(w_mid[::-1, ::-1], 2, 3)
     xz, w_back = lax.optimization_barrier((xz, w_back))
 
+    shares = lax.axis_size("batch")
+    span = max(8, 128 // shares)
     everyone = [list(range(lax.axis_size("batch")))]
     z2, act_a, st2 = call(
         middle_body,
@@ -807,18 +851,24 @@
         pixels * 384 * 128 * 2,
         pixels * 1280,
     )(info, st1, st2, gb, sb, z2, w_out)
-    arrived = partner(head, 1)
-    st3 = swapped_sum(head[:16] + arrived[:16], everyone)
-    st3, kept, arrived = lax.optimization_barrier((st3, kept, arrived))
-    kept = swapped_sum(kept + arrived[16:], everyone)
-    y_edge = partner(y_edge, 1)
-    z2_edge = partner(z2_edge, 1)
-
-    block_out, e, t, t_edge, own4, u_local, w_scaled = call(
+    arrived3 = swapped(
+        call(
+            spread_body,
+            1,
+            [whole_spec((144, 128)), whole_spec((144, 128)), whole_spec((128, 128))],
+            [whole_out((shares, 16 + span, 128))],
+            [],
+            "spread_third",
+            1e5,
+            1e6,
+        )(head, partner(head, 1), kept)[0]
+    )
+
+    block_out, e, t, t_edge, own4, st3, u_local, w_scaled = call(
         last_body,
         steps,
         [
-            SMEM, eight, whole_spec((16, 128)), large, large, step_spec(tile(128)),
+            SMEM, eight, whole_spec((shares, 16 + span, 128)), large, large, step_spec(tile(128)),
             step_spec(tile(128)), step_spec(tile(128)), step_spec(tile(512)),
             step_spec(tile(512)), whole_spec((128, 512)),
         ],
@@ -827,6 +877,7 @@
             step_out(rows, tile(512), bf16),
             step_out(rows, tile(128), f32),
             whole_out(edge(128)),
+            whole_out((16 + span, 128)),
             whole_out((16, 128)),
             whole_out((128, 512)),
             whole_out((256, 512), bf16),
@@ -843,14 +894,27 @@
         "last_norm",
         pixels * 512 * 128 * 10,
         pixels * 4864,
-    )(info, st1, st3, gc, sc, act_b, slope_b, dotted_b, images, cotangent, w_out)
-
-    arrived = partner(jnp.concatenate([own4, kept]), 1)
-    st4 = swapped_sum(own4 + arrived[:16], everyone)
-    other = arrived
-    t_edge = partner(t_edge, 1)
-
-    shares = lax.axis_size("batch")
+    )(info, st1, arrived3, gc, sc, act_b, slope_b, dotted_b, images, cotangent, w_out)
+
+    other4, y_edge, z2_edge, t_edge = lax.optimization_barrier(
+        tuple(
+            partner(v, 1)
+            for v in lax.optimization_barrier((own4, y_edge, z2_edge, t_edge))
+        )
+    )
+    arrived4 = swapped(
+        call(
+            both_body,
+            1,
+            [SMEM, whole_spec((16 + span, 128)), whole_spec((16 + span, 128))],
+            [whole_out((shares, 16 + 2 * span, 128))],
+            [],
+            "spread_fourth",
+            1e5,
+            1e6,
+        )(info, own4, other4)[0]
+    )
+
     share = -(-1344 // (8 * shares)) * 8
     half = share * shares
     block = -(-(share + 6) // 16) * 16
@@ -858,8 +922,8 @@
         back_body,
         steps + 1,
         [
-            SMEM, eight, eight, whole_spec((16, 128)), whole_spec((16, 128)),
-            whole_spec((128, 128)), whole_spec((144, 128)), whole_spec((16, 128)),
+            SMEM, eight, eight, whole_spec((16, 128)), whole_spec((shares, 16 + 2 * span, 128)),
+            whole_spec((16 + span, 128)),
             whole_spec((512, 128)), whole_spec((136, 128)),
             whole_spec((128, 512)), small, small, small, large, whole_spec((128, 512)),
             whole_spec((256, 512)), taps,
@@ -884,12 +948,14 @@
             pltpu.VMEM((128, 512), f32),
             pltpu.VMEM((2, 8, 128), f32),
             pltpu.VMEM((2 * half, 128), f32),
+            pltpu.VMEM((16, 128), f32),
+            pltpu.VMEM((2, 128, 128), f32),
         ],
         "middle_back",
         pixels * 32 * 128 * 128 * 2,
         pixels * 4000,
     )(
-        info, st1, st2, st3, st4, kept, other, own4, xz, gram, u_local, ga, sa, gb, gc,
+        info, st1, st2, st3, arrived4, own4, xz, gram, u_local, ga, sa, gb, gc,
         w_out, w_scaled, w_back,
         act_b, slope_b, y_edge, z2, z2_edge, t, t_edge, act_a, z1, images,
     )
@@ -904,7 +970,7 @@
         1e6,
         2e6,
     )(mine, arrived)[0]
-    spread = lax.all_to_all(spread, "batch", 0, 0, tiled=True)
+    spread = swapped(spread)
     st5, spread = call(
         functools.partial(share_body, share),
         1,
@@ -915,7 +981,7 @@
         1e6,
         1e6,
     )(spread)
-    gathered = lax.all_to_all(spread, "batch", 0, 0, tiled=True)
+    gathered = swapped(spread)
 
     grad_images = call(
         input_body,

time: 210 us -> 206 us (0.981)
  starting transfers between devices: 16.8 us -> 12.4 us
    all_to_all x1 -> x3, blocking collectives: 15.8 us -> 41.4 us  [swapped(): return lax.all_to_all(spread, 'batch', 0, 0, tiled=True)]
    all_to_all x3 -> x1, blocking collectives: 39.2 us -> 14.2 us  [swapped_sum(): lax.all_to_all(spread, 'batch', 0, 0, axis_index_groups=groups, tiled=True)]
    all_to_all x2 -> x1, starting transfers between devices: 7.97 us -> 3.63 us  [swapped(): return lax.all_to_all(spread, 'batch', 0, 0, tiled=True)]
    pallas_call x1 -> x3, Pallas kernels: 31.3 us -> 32 us  [the longest x1 31.4 us: local(): call(last_body, steps, [SMEM, eight, whole_spec((shares, 16 + span, 128))...]
  transfers between devices with their start and end apart: 12 -> 11, of which waited for: 5 -> 5; matrix products, arithmetic and copies ran while one was open for 0% -> 0% of each run, Pallas kernels for 27% -> 12%
where the time goes in v3:
time: 206 us; the launch traced here: 205 us
  Pallas kernels  124 us (60%)
  blocking collectives  55.5 us (27%)
  starting transfers between devices  12.4 us (6%)
  waiting for transfers between devices  8.44 us (4%)
  local copies, waits for them, and re-layouts  2.99 us (1%)
    all_to_all x3, blocking collectives, swapped(): return lax.all_to_all(spread, 'batch', 0, 0, tiled=True)  41.4 us
    pallas_call x1, Pallas kernels, local(): call(last_body, steps, [SMEM, eight, whole_spec((shares, 16 + span, 128))...  31.4 us
    pallas_call x1, Pallas kernels, local(): call(back_body, steps + 1, [SMEM, eight, eight, whole_spec((16, 128)), wh...  26.7 us
    pallas_call x1, Pallas kernels, local(): call(input_body, steps, [SMEM, eight, eight, small, whole_spec((512, 128)...  15.8 us
    all_to_all x1, blocking collectives, swapped_sum(): lax.all_to_all(spread, 'batch', 0, 0, axis_index_groups=groups, tiled=True)  14.2 us
    pallas_call x1, Pallas kernels, local(): call(second_body, steps, [SMEM, eight, eight, small, small, step_spec(til...  13 us
    pallas_call x1, Pallas kernels, local(): call(middle_body, steps + 1, [SMEM, eight, small, small, step_spec(tile(1...  12.6 us
    pallas_call x1, Pallas kernels, local(): call(first_body, steps, [SMEM, step_spec(tile(512)), whole_spec((512, 128...  11.7 us
  transfers between devices with their start and end apart: 11, of which 5 were waited for; matrix products, arithmetic and copies ran while one was open for 0% of the time, Pallas kernels for 12%

profile of v3, /device:TPU:0, one launch (start us, length us, event | category | flops | bytes accessed | tf_op | source)
XLA Modules:
  0.0 204.7 jit_solution(13026791626160266732)
XLA Ops:
  1.3 0.1 pad_add_fusion.info
  1.4 0.9 copy-done.1
  2.3 11.7 %first_norm_sums.1 = (f32[14,28,32,128]{3,2,1,0:T(8,128)}, f32[28,32,128]{2,1,0:T(8,128)S(1)}, f32[8,128]{1,0:T(8,128)S(1)}) custom-call(s32[2]{0:T(128)S(1)} %pad_add_fusion.info, bf16[14,28,32,512]{3,2,1,0:T(8,128)(2,1)} %bitcast.32, bf16[512,128]{1,0:T(8,128)(2,1)S(1)} %copy-done.1), custom_call_target="tpu_custom_call" | custom-call | flops 1644167168 | bytes 19267584 | tf_op jit(solution)/shard_map/first_norm_sums/pallas_call | solution.py:779
  14.0 0.4 collective-permute-start
  14.4 0.7 broadcast_in_dim.4
  15.1 7.0 %all-to-all-start = ((f32[32,8,128]{2,1,0:T(8,128)}), f32[32,8,128]{2,1,0:T(8,128)S(1)}, u32[]{:S(2)}, u32[]{:S(2)}) async-start(f32[32,8,128]{2,1,0:T(8,128)} %broadcast_in_dim.4), calls=%async_computation | async-start | bytes 262144 | tf_op jit(solution)/shard_map/all_to_all | solution.py:42
  22.1 0.2 copy.24
  22.3 0.0 copy-start.7
  22.4 0.0 copy-start.10
  22.4 9.3 %input_cross.1.xz_ref = f32[512,128]{1,0:T(8,128)S(1)} custom-call(bf16[14,28,32,512]{3,2,1,0:T(8,128)(2,1)} %bitcast.33, f32[14,28,32,128]{3,2,1,0:T(8,128)} %get-tuple-element.61.z_ref.z1_ref), custom_call_target="tpu_custom_call" | custom-call | flops 1644167168 | bytes 19267584 | tf_op jit(solution)/shard_map/input_cross/pallas_call | solution.py:795
  31.6 0.0 all-to-all-done
  31.7 0.0 collective-permute-done.edge_ref
  31.7 0.0 copy-start.3
  31.7 0.0 copy-start.8
  31.7 0.0 copy-start.9
  31.7 12.6 %middle_conv.1 = (f32[14,28,32,128]{3,2,1,0:T(8,128)}, bf16[14,28,32,128]{3,2,1,0:T(8,128)(2,1)}, f32[8,128]{1,0:T(8,128)S(1)}) custom-call(s32[2]{0:T(128)S(1)} %pad_add_fusion.info, f32[8,128]{1,0:T(8,128)S(1)} %reduce_sum.18.st1, f32[1,128]{1,0:T(1,128)S(1)} %bitcast.23, f32[1,128]{1,0:T(1,128)S(1)} %bitcast.30, ...), custom_call_target="tpu_custom_call" | custom-call | flops 4932501504 | bytes 16056320 | tf_op jit(solution)/shard_map/middle_conv/pallas_call | solution.py:811
  44.3 0.3 collective-permute-start.1
  44.6 0.9 collective-permute-done.1
  45.5 14.2 %all_to_all.30 = f32[16,8,128]{2,1,0:T(8,128)S(1)} all-to-all(f32[16,8,128]{2,1,0:T(8,128)S(1)} %broadcast_in_dim.5), channel_id=1, replica_groups={{0,2,4,6,8,10,12,14,16,18,20,22,24,26,28,30},{1,3,5,7,9,11,13,15,17,19,..., dimensions={0} | all-to-all | bytes 131072 | tf_op jit(solution)/shard_map/all_to_all | solution.py:31
  59.8 13.0 %second_norm.1 = (bf16[14,28,32,128]{3,2,1,0:T(8,128)(2,1)}, bf16[14,28,32,128]{3,2,1,0:T(8,128)(2,1)}, bf16[14,28,32,128]{3,2,1,0:T(8,128)(2,1)}, bf16[28,32,25...) custom-call(s32[2]{0:T(128)S(1)} %pad_add_fusion.info, ...), custom_call_target="tpu_custom_call" | custom-call | flops 1233125376 | bytes 16056320 | tf_op jit(solution)/shard_map/second_norm/pallas_call | solution.py:835
  72.8 0.0 collective-permute-start.2
  72.8 1.3 collective-permute-done.2.arrived_ref
  74.1 11.5 %all_to_all.31.in3 = f32[16,24,128]{2,1,0:T(8,128)S(1)} all-to-all(f32[16,24,128]{2,1,0:T(8,128)S(1)} %spread_third.1), channel_id=1, replica_groups=mesh['batch'=16,'rows'=2] {'batch'}, dimensions={0} | all-to-all | bytes 393216 | tf_op jit(solution)/shard_map/all_to_all | solution.py:36
  85.6 31.4 %last_norm.1 = (bf16[14,28,32,512]{3,2,1,0:T(8,128)(2,1)}, bf16[14,28,32,512]{3,2,1,0:T(8,128)(2,1)}, f32[14,28,32,128]{3,2,1,0:T(8,128)}, f32[28,32,128]{2,1,0:...) custom-call(s32[2]{0:T(128)S(1)} %pad_add_fusion.info, ...), custom_call_target="tpu_custom_call" | custom-call | flops 8220835840 | bytes 61014016 | tf_op jit(solution)/shard_map/last_norm/pallas_call | solution.py:867
  117.0 0.0 collective-permute-start.4
  117.0 0.5 collective-permute-start.5
  117.5 0.1 collective-permute-start.6
  117.6 0.4 collective-permute-start.3
  118.0 2.1 %collective-permute-done.3.arrived_ref = f32[24,128]{1,0:T(8,128)S(1)} collective-permute-done((f32[24,128]{1,0:T(8,128)S(1)}, f32[24,128]{1,0:T(8,128)S(1)}, u32[]{:S(2)}, u32[]{:S(2)}) %collective-permute-start.3) | collective-permute-done | bytes 12320 | tf_op jit(solution)/shard_map/ppermute | solution.py:25
  120.1 0.0 collective-permute-done.4.ye_ref
  120.1 0.0 collective-permute-done.5.ze_ref
  120.2 0.0 collective-permute-done.6.te_ref
  120.2 0.6 spread_fourth.1
  120.8 13.6 %all_to_all.32.in4 = f32[16,32,128]{2,1,0:T(8,128)S(1)} all-to-all(f32[16,32,128]{2,1,0:T(8,128)S(1)} %spread_fourth.1), channel_id=1, replica_groups=mesh['batch'=16,'rows'=2] {'batch'}, dimensions={0} | all-to-all | bytes 524288 | tf_op jit(solution)/shard_map/all_to_all | solution.py:36
  134.4 0.0 copy-start.2
  134.4 26.7 %middle_back.1 = (bf16[14,28,32,128]{3,2,1,0:T(8,128)(2,1)}, f32[1416,128]{1,0:T(8,128)}, f32[1416,128]{1,0:T(8,128)}, f32[16,128]{1,0:T(8,128)S(1)}) custom-call(s32[2]{0:T(128)S(1)} %pad_add_fusion.info, f32[8,128]{1,0:T(8,128)S(1)} %reduce_sum.18.st1, f32[8,128]{1,0:T(8,128)S(1)} %reduce_sum.19.st2, f32[16,128]{1,0:T(8,128)S(1)} %get-tuple-element.72.st3, ...), custom_call_target="tpu_custom_call" | custom-call | flops 13153337344 | bytes 50176000 | tf_op jit(solution)/shard_map/middle_back/pallas_call | solution.py:921
  161.0 0.1 collective-permute-start.7
  161.1 2.4 %collective-permute-done.7.arrived_ref = f32[1416,128]{1,0:T(8,128)S(1)} collective-permute-done((f32[1416,128]{1,0:T(8,128)}, f32[1416,128]{1,0:T(8,128)S(1)}, u32[]{:S(2)}, u32[]{:S(2)}) %collective-permute-start.7) | collective-permute-done | bytes 725024 | tf_op jit(solution)/shard_map/ppermute | solution.py:25
  163.5 1.1 copy-done
  164.6 0.1 pack_shares.1
  164.7 16.2 %all_to_all.33.in_ref = bf16[16,96,128]{2,1,0:T(8,128)(2,1)S(1)} all-to-all(bf16[16,96,128]{2,1,0:T(8,128)(2,1)S(1)} %pack_shares.1), channel_id=1, replica_groups=mesh['batch'=16,'rows'=2] {'batch'}, dimensions={0} | all-to-all | bytes 786432 | tf_op jit(solution)/shard_map/all_to_all | solution.py:36
  181.0 0.8 sum_shares.1
  181.8 3.6 %all-to-all-start.5 = ((bf16[16,96,128]{2,1,0:T(8,128)(2,1)}), bf16[16,96,128]{2,1,0:T(8,128)(2,1)S(1)}, u32[]{:S(2)}, u32[]{:S(2)}) async-start(bf16[16,96,128]{2,1,0:T(8,128)(2,1)} %get-tuple-element.93), calls=%async_computation.5 | async-start | bytes 786432 | tf_op jit(solution)/shard_map/all_to_all | solution.py:36
  185.4 15.8 %input_grad.1 = bf16[14,28,32,512]{3,2,1,0:T(8,128)(2,1)} custom-call(s32[2]{0:T(128)S(1)} %pad_add_fusion.info, f32[8,128]{1,0:T(8,128)S(1)} %reduce_sum.18.st1, f32[8,128]{1,0:T(8,128)S(1)} %get-tuple-element.94.st5, f32[1,128]{1,0:T(1,128)S(1)} %bitcast.25, bf16[512,128]{1,0:T(8,128)(2,1)S(1)} %copy-done.2, ...), custom_call_target="tpu_custom_call" | custom-call | flops 1644167168 | bytes 35323904 | tf_op jit(solution)/shard_map/input_grad/pallas_call | solution.py:986
  201.3 0.0 all-to-all-done.5.mine_ref
  201.3 0.0 collective-permute-start.8
  201.3 1.7 collective-permute-done.8.other_ref
  203.0 1.7 replicated_grads.1
  (26 shorter events, 0.1 us)
Async XLA Ops:
  1.4 0.9 copy-start.1
  2.3 19.8 %copy-start.4 = (bf16[3,3,128,128]{3,2,1,0:T(8,128)(2,1)S(1)}, bf16[3,3,128,128]{3,2,1,0:T(8,128)(2,1)}, u32[]{:S(2)}) copy-start(bf16[3,3,128,128]{3,2,1,0:T(8,128)(2,1)} %w_ref.3) | copy-start | bytes 884740
  14.0 17.7 %collective-permute-start = (f32[28,32,128]{2,1,0:T(8,128)S(1)}, f32[28,32,128]{2,1,0:T(8,128)S(1)}, u32[]{:S(2)}, u32[]{:S(2)}) collective-permute-start(f32[28,32,128]{2,1,0:T(8,128)S(1)} %get-tuple-element.62), channel_id=1, source_target_pairs={{0,1},{1,0},{2,3},{3,2},{4,5},{5,4},{6,7},{7,6},{8,9},{9,8},{10,11... | collective-permute-start | bytes 1376264 | tf_op jit(solution)/shard_map/ppermute | solution.py:25
  15.1 16.5 %all-to-all-start = ((f32[32,8,128]{2,1,0:T(8,128)}), f32[32,8,128]{2,1,0:T(8,128)S(1)}, u32[]{:S(2)}, u32[]{:S(2)}) async-start(f32[32,8,128]{2,1,0:T(8,128)} %broadcast_in_dim.4), calls=%async_computation | async-start | bytes 262144 | tf_op jit(solution)/shard_map/all_to_all | solution.py:42
  22.3 9.3 %copy-start.7 = (f32[128]{0:T(128)S(1)}, f32[128]{0:T(128)}, u32[]{:S(2)}) copy-start(f32[128]{0:T(128)} %param.15) | copy-start | bytes 1540
  22.4 9.3 %copy-start.10 = (f32[128]{0:T(128)S(1)}, f32[128]{0:T(128)}, u32[]{:S(2)}) copy-start(f32[128]{0:T(128)} %param.16) | copy-start | bytes 1540
  31.7 28.0 %copy-start.3 = (bf16[128,512]{1,0:T(8,128)(2,1)S(1)}, bf16[128,512]{1,0:T(8,128)(2,1)}, u32[]{:S(2)}) copy-start(bf16[128,512]{1,0:T(8,128)(2,1)} %wo_ref.5) | copy-start | bytes 393220
  31.7 28.0 %copy-start.8 = (f32[128]{0:T(128)S(1)}, f32[128]{0:T(128)}, u32[]{:S(2)}) copy-start(f32[128]{0:T(128)} %param.19) | copy-start | bytes 1540
  31.7 28.0 %copy-start.9 = (f32[128]{0:T(128)S(1)}, f32[128]{0:T(128)}, u32[]{:S(2)}) copy-start(f32[128]{0:T(128)} %param.18) | copy-start | bytes 1540
  44.3 41.3 %copy-start.5 = (f32[512]{0:T(512)S(1)}, f32[512]{0:T(512)}, u32[]{:S(2)}) copy-start(f32[512]{0:T(512)} %param.22) | copy-start | bytes 6148
  44.3 41.3 %copy-start.6 = (f32[512]{0:T(512)S(1)}, f32[512]{0:T(512)}, u32[]{:S(2)}) copy-start(f32[512]{0:T(512)} %param.21) | copy-start | bytes 6148
  44.3 1.2 collective-permute-start.1
  72.8 1.3 collective-permute-start.2
  117.0 3.1 %collective-permute-start.4 = (bf16[28,32,256]{2,1,0:T(8,128)(2,1)S(1)}, bf16[28,32,256]{2,1,0:T(8,128)(2,1)S(1)}, u32[]{:S(2)}, u32[]{:S(2)}) collective-permute-start(bf16[28,32,256]{2,1,0:T(8,128)(2,1)S(1)} %get-tuple-element.78), channel_id=1, source_target_pairs={{0,1},{1,0},{2,3},{3,2},{4,5},{5,4},{6,7},{7,6},{8,9},{9,8},{10,11... | collective-permute-start | bytes 1376264 | tf_op jit(solution)/shard_map/ppermute | solution.py:25
  117.0 3.1 %collective-permute-start.5 = (f32[28,32,128]{2,1,0:T(8,128)S(1)}, f32[28,32,128]{2,1,0:T(8,128)S(1)}, u32[]{:S(2)}, u32[]{:S(2)}) collective-permute-start(f32[28,32,128]{2,1,0:T(8,128)S(1)} %get-tuple-element.79), channel_id=1, source_target_pairs={{0,1},{1,0},{2,3},{3,2},{4,5},{5,4},{6,7},{7,6},{8,9},{9,8},{10,11... | collective-permute-start | bytes 1376264 | tf_op jit(solution)/shard_map/ppermute | solution.py:25
  117.5 2.7 %collective-permute-start.6 = (f32[28,32,128]{2,1,0:T(8,128)S(1)}, f32[28,32,128]{2,1,0:T(8,128)S(1)}, u32[]{:S(2)}, u32[]{:S(2)}) collective-permute-start(f32[28,32,128]{2,1,0:T(8,128)S(1)} %get-tuple-element.80), channel_id=1, source_target_pairs={{0,1},{1,0},{2,3},{3,2},{4,5},{5,4},{6,7},{7,6},{8,9},{9,8},{10,11... | collective-permute-start | bytes 1376264 | tf_op jit(solution)/shard_map/ppermute | solution.py:25
  117.6 2.6 %collective-permute-start.3 = (f32[24,128]{1,0:T(8,128)S(1)}, f32[24,128]{1,0:T(8,128)S(1)}, u32[]{:S(2)}, u32[]{:S(2)}) collective-permute-start(f32[24,128]{1,0:T(8,128)S(1)} %get-tuple-element.77.own_ref.own4), channel_id=1, source_target_pairs={{0,1},{1,0},{2,3},{3,2},{4,5},{5,4},{6,7},{7,6},{8,9},{9,8},{10,11... | collective-permute-start | bytes 36872 | tf_op jit(solution)/shard_map/ppermute | solution.py:25
  120.1 14.2 %copy-start.11 = (bf16[28,32,256]{2,1,0:T(8,128)(2,1)}, bf16[28,32,256]{2,1,0:T(8,128)(2,1)S(1)}, u32[]{:S(2)}) copy-start(bf16[28,32,256]{2,1,0:T(8,128)(2,1)S(1)} %collective-permute-done.4.ye_ref) | copy-start | bytes 1376260
  120.2 14.2 %copy-start.12 = (f32[28,32,128]{2,1,0:T(8,128)}, f32[28,32,128]{2,1,0:T(8,128)S(1)}, u32[]{:S(2)}) copy-start(f32[28,32,128]{2,1,0:T(8,128)S(1)} %collective-permute-done.5.ze_ref) | copy-start | bytes 1376260
  120.2 14.2 %copy-start.13 = (f32[28,32,128]{2,1,0:T(8,128)}, f32[28,32,128]{2,1,0:T(8,128)S(1)}, u32[]{:S(2)}) copy-start(f32[28,32,128]{2,1,0:T(8,128)S(1)} %collective-permute-done.6.te_ref) | copy-start | bytes 1376260
  134.4 51.1 %copy-start.2 = (bf16[512,128]{1,0:T(8,128)(2,1)S(1)}, bf16[512,128]{1,0:T(8,128)(2,1)}, u32[]{:S(2)}) copy-start(bf16[512,128]{1,0:T(8,128)(2,1)} %wi_ref.1) | copy-start | bytes 393220
  161.0 2.5 %collective-permute-start.7 = (f32[1416,128]{1,0:T(8,128)}, f32[1416,128]{1,0:T(8,128)S(1)}, u32[]{:S(2)}, u32[]{:S(2)}) collective-permute-start(f32[1416,128]{1,0:T(8,128)} %get-tuple-element.92), channel_id=1, source_target_pairs={{0,1},{1,0},{2,3},{3,2},{4,5},{5,4},{6,7},{7,6},{8,9},{9,8},{10,11... | collective-permute-start | bytes 2174984 | tf_op jit(solution)/shard_map/ppermute | solution.py:25
  163.5 1.1 copy-start
  181.8 19.5 %all-to-all-start.5 = ((bf16[16,96,128]{2,1,0:T(8,128)(2,1)}), bf16[16,96,128]{2,1,0:T(8,128)(2,1)S(1)}, u32[]{:S(2)}, u32[]{:S(2)}) async-start(bf16[16,96,128]{2,1,0:T(8,128)(2,1)} %get-tuple-element.93), calls=%async_computation.5 | async-start | bytes 786432 | tf_op jit(solution)/shard_map/all_to_all | solution.py:36
  201.3 1.7 collective-permute-start.8

commit v4 on v3

--- a/solution.py
+++ b/solution.py
@@ -120,7 +120,7 @@
     return (dot_nt(one, high) + dot_nt(one, low))[0:8, :]
 
 
-def call(body, grid, ins, outs, scratch, name, flops, bytes_moved):
+def call(body, grid, ins, outs, scratch, name, flops, bytes_moved, vmem=52):
     return pl.pallas_call(
         body,
         grid=(grid,),
@@ -130,7 +130,7 @@
         scratch_shapes=scratch,
         name=name,
         compiler_params=pltpu.CompilerParams(
-            dimension_semantics=("arbitrary",), vmem_limit_bytes=52 << 20
+            dimension_semantics=("arbitrary",), vmem_limit_bytes=vmem << 20
         ),
         cost_estimate=pl.CostEstimate(
             flops=int(flops), bytes_accessed=int(bytes_moved), transcendentals=0
@@ -468,7 +468,7 @@
     def through(r, c):
         y = dot(e_ref[r, c : c + piece].reshape(n, 512), w_turn[...])
         t = (y[:, 0:128] + y[:, 128:256]).reshape(piece, images, 128)
-        t_ref[r, c : c + piece] = t
+        t_ref[r, c : c + piece] = t.astype(bf16)
         sums_b[0] += fold8(t * g_ref[r, c : c + piece].astype(f32))
         sums_b[1] += fold8(t * gx_ref[r, c : c + piece].astype(f32))
 
@@ -521,7 +521,7 @@
 
     def second_back(t, product, slope, z):
         kappa, scale_b, beta, alpha = (coef[i : i + 1, :] for i in range(4))
-        through = t - kappa - product[..., 0:128] - product[..., 128:256]
+        through = t.astype(f32) - kappa - product[..., 0:128] - product[..., 128:256]
         grad = scale_b * (slope.astype(f32) * through) - (alpha + beta * z)
         return jnp.where(mask, grad, 0.0).astype(bf16)
 
@@ -850,6 +850,7 @@
         "second_norm",
         pixels * 384 * 128 * 2,
         pixels * 1280,
+        20,
     )(info, st1, st2, gb, sb, z2, w_out)
     arrived3 = swapped(
         call(
@@ -875,8 +876,8 @@
         [
             step_out(rows, tile(512), bf16),
             step_out(rows, tile(512), bf16),
-            step_out(rows, tile(128), f32),
-            whole_out(edge(128)),
+            step_out(rows, tile(128), bf16),
+            whole_out(edge(128), bf16),
             whole_out((16 + span, 128)),
             whole_out((16, 128)),
             whole_out((128, 512)),
@@ -894,6 +895,7 @@
         "last_norm",
         pixels * 512 * 128 * 10,
         pixels * 4864,
+        36,
     )(info, st1, arrived3, gc, sc, act_b, slope_b, dotted_b, images, cotangent, w_out)
 
     other4, y_edge, z2_edge, t_edge = lax.optimization_barrier(
@@ -954,6 +956,7 @@
         "middle_back",
         pixels * 32 * 128 * 128 * 2,
         pixels * 4000,
+        49,
     )(
         info, st1, st2, st3, arrived4, own4, xz, gram, u_local, ga, sa, gb, gc,
         w_out, w_scaled, w_back,

time: 206 us -> 202 us (0.981)
  Pallas kernels: 124 us -> 117 us
  local copies, waits for them, and re-layouts: 2.99 us -> 6.37 us
    unnamed x29, local copies, waits for them, and re-layouts: 2.29 us -> 5.67 us
    pallas_call x1, Pallas kernels: 13 us -> 10.1 us  [local(): call(second_body, steps, [SMEM, eight, eight, small, small, step_spec(til...]
    pallas_call x1, Pallas kernels: 31.4 us -> 29.1 us  [local(): call(last_body, steps, [SMEM, eight, whole_spec((shares, 16 + span, 128))...]
where the time goes in v4:
time: 202 us; the launch traced here: 201 us
  Pallas kernels  117 us (58%)
  blocking collectives  55.5 us (27%)
  starting transfers between devices  12.4 us (6%)
  waiting for transfers between devices  7.9 us (4%)
  local copies, waits for them, and re-layouts  6.37 us (3%)
    all_to_all x3, blocking collectives, swapped(): return lax.all_to_all(spread, 'batch', 0, 0, tiled=True)  41.3 us
    pallas_call x1, Pallas kernels, local(): call(last_body, steps, [SMEM, eight, whole_spec((shares, 16 + span, 128))...  29.1 us
    pallas_call x1, Pallas kernels, local(): call(back_body, steps + 1, [SMEM, eight, eight, whole_spec((16, 128)), wh...  25.3 us
    pallas_call x1, Pallas kernels, local(): call(input_body, steps, [SMEM, eight, eight, small, whole_spec((512, 128)...  15.8 us
    all_to_all x1, blocking collectives, swapped_sum(): lax.all_to_all(spread, 'batch', 0, 0, axis_index_groups=groups, tiled=True)  14.2 us
    pallas_call x1, Pallas kernels, local(): call(middle_body, steps + 1, [SMEM, eight, small, small, step_spec(tile(1...  12.6 us
    pallas_call x1, Pallas kernels, local(): call(first_body, steps, [SMEM, step_spec(tile(512)), whole_spec((512, 128...  11.7 us
    pallas_call x1, Pallas kernels, local(): call(second_body, steps, [SMEM, eight, eight, small, small, step_spec(til...  10.1 us
  transfers between devices with their start and end apart: 11, of which 5 were waited for; matrix products, arithmetic and copies ran while one was open for 0% of the time, Pallas kernels for 12%

profile of v4, /device:TPU:0, one launch (start us, length us, event | category | flops | bytes accessed | tf_op | source)
XLA Modules:
  0.0 201.0 jit_solution(1879653502194132424)
XLA Ops:
  1.3 0.1 pad_add_fusion.info
  1.4 0.9 copy-done.3
  2.3 11.7 %first_norm_sums.1 = (f32[14,28,32,128]{3,2,1,0:T(8,128)}, f32[28,32,128]{2,1,0:T(8,128)S(1)}, f32[8,128]{1,0:T(8,128)S(1)}) custom-call(s32[2]{0:T(128)S(1)} %pad_add_fusion.info, bf16[14,28,32,512]{3,2,1,0:T(8,128)(2,1)} %bitcast.32, bf16[512,128]{1,0:T(8,128)(2,1)S(1)} %copy-done.3), custom_call_target="tpu_custom_call" | custom-call | flops 1644167168 | bytes 19267584 | tf_op jit(solution)/shard_map/first_norm_sums/pallas_call | solution.py:779
  14.0 0.4 collective-permute-start
  14.4 0.7 broadcast_in_dim.4
  15.1 7.0 %all-to-all-start = ((f32[32,8,128]{2,1,0:T(8,128)}), f32[32,8,128]{2,1,0:T(8,128)S(1)}, u32[]{:S(2)}, u32[]{:S(2)}) async-start(f32[32,8,128]{2,1,0:T(8,128)} %broadcast_in_dim.4), calls=%async_computation | async-start | bytes 262144 | tf_op jit(solution)/shard_map/all_to_all | solution.py:42
  22.1 0.2 copy.24
  22.3 0.0 copy-start.9
  22.4 0.0 copy-start.13
  22.4 9.3 %input_cross.1.xz_ref = f32[512,128]{1,0:T(8,128)S(1)} custom-call(bf16[14,28,32,512]{3,2,1,0:T(8,128)(2,1)} %bitcast.33, f32[14,28,32,128]{3,2,1,0:T(8,128)} %get-tuple-element.61.z_ref.z1_ref), custom_call_target="tpu_custom_call" | custom-call | flops 1644167168 | bytes 19267584 | tf_op jit(solution)/shard_map/input_cross/pallas_call | solution.py:795
  31.6 0.0 all-to-all-done
  31.7 0.0 collective-permute-done.edge_ref
  31.7 0.0 copy-start.5
  31.7 0.0 copy-start.10
  31.7 0.0 copy-start.11
  31.7 12.6 %middle_conv.1 = (f32[14,28,32,128]{3,2,1,0:T(8,128)}, bf16[14,28,32,128]{3,2,1,0:T(8,128)(2,1)}, f32[8,128]{1,0:T(8,128)S(1)}) custom-call(s32[2]{0:T(128)S(1)} %pad_add_fusion.info, f32[8,128]{1,0:T(8,128)S(1)} %reduce_sum.18.st1, f32[1,128]{1,0:T(1,128)S(1)} %bitcast.23, f32[1,128]{1,0:T(1,128)S(1)} %bitcast.30, ...), custom_call_target="tpu_custom_call" | custom-call | flops 4932501504 | bytes 16056320 | tf_op jit(solution)/shard_map/middle_conv/pallas_call | solution.py:811
  44.4 0.2 collective-permute-start.1
  44.6 0.9 collective-permute-done.1
  45.6 14.2 %all_to_all.30 = f32[16,8,128]{2,1,0:T(8,128)S(1)} all-to-all(f32[16,8,128]{2,1,0:T(8,128)S(1)} %broadcast_in_dim.5), channel_id=1, replica_groups={{0,2,4,6,8,10,12,14,16,18,20,22,24,26,28,30},{1,3,5,7,9,11,13,15,17,19,..., dimensions={0} | all-to-all | bytes 131072 | tf_op jit(solution)/shard_map/all_to_all | solution.py:31
  59.8 0.0 copy-start
  59.8 2.8 %copy-done = f32[14,28,32,128]{3,2,1,0:T(8,128)S(1)} copy-done((f32[14,28,32,128]{3,2,1,0:T(8,128)S(1)}, f32[14,28,32,128]{3,2,1,0:T(8,128)}, u32[]{:S(2)}) %copy-start) | copy-done | bytes 6422552
  62.6 10.1 %second_norm.1 = (bf16[14,28,32,128]{3,2,1,0:T(8,128)(2,1)S(1)}, bf16[14,28,32,128]{3,2,1,0:T(8,128)(2,1)S(1)}, bf16[14,28,32,128]{3,2,1,0:T(8,128)(2,1)S(1)}, b...) custom-call(s32[2]{0:T(128)S(1)} %pad_add_fusion.info, ...), custom_call_target="tpu_custom_call" | custom-call | flops 1233125376 | bytes 16056320 | tf_op jit(solution)/shard_map/second_norm/pallas_call | solution.py:835
  72.8 0.1 collective-permute-start.2
  72.9 1.3 collective-permute-done.2.arrived_ref
  74.1 11.5 %all_to_all.31.in3 = f32[16,24,128]{2,1,0:T(8,128)S(1)} all-to-all(f32[16,24,128]{2,1,0:T(8,128)S(1)} %spread_third.1), channel_id=1, replica_groups=mesh['batch'=16,'rows'=2] {'batch'}, dimensions={0} | all-to-all | bytes 393216 | tf_op jit(solution)/shard_map/all_to_all | solution.py:36
  85.7 29.1 %last_norm.1 = (bf16[14,28,32,512]{3,2,1,0:T(8,128)(2,1)}, bf16[14,28,32,512]{3,2,1,0:T(8,128)(2,1)}, bf16[14,28,32,128]{3,2,1,0:T(8,128)(2,1)S(1)}, bf16[28,32,...) custom-call(s32[2]{0:T(128)S(1)} %pad_add_fusion.info, ...), custom_call_target="tpu_custom_call" | custom-call | flops 8220835840 | bytes 61014016 | tf_op jit(solution)/shard_map/last_norm/pallas_call | solution.py:868
  114.8 1.7 copy-done.12
  116.5 0.0 collective-permute-start.4
  116.5 0.5 collective-permute-start.5
  117.0 0.0 collective-permute-start.6
  117.0 0.5 collective-permute-start.3
  117.5 1.8 collective-permute-done.3.arrived_ref
  119.3 0.0 collective-permute-done.6.te_ref
  119.3 0.0 collective-permute-done.4.ye_ref
  119.3 0.0 collective-permute-done.5.ze_ref
  119.3 0.6 spread_fourth.1
  119.9 13.6 %all_to_all.32.in4 = f32[16,32,128]{2,1,0:T(8,128)S(1)} all-to-all(f32[16,32,128]{2,1,0:T(8,128)S(1)} %spread_fourth.1), channel_id=1, replica_groups=mesh['batch'=16,'rows'=2] {'batch'}, dimensions={0} | all-to-all | bytes 524288 | tf_op jit(solution)/shard_map/all_to_all | solution.py:36
  133.5 25.3 %middle_back.1 = (bf16[14,28,32,128]{3,2,1,0:T(8,128)(2,1)}, f32[1416,128]{1,0:T(8,128)S(1)}, f32[1416,128]{1,0:T(8,128)S(1)}, f32[16,128]{1,0:T(8,128)S(1)}) custom-call(s32[2]{0:T(128)S(1)} %pad_add_fusion.info, f32[8,128]{1,0:T(8,128)S(1)} %reduce_sum.18.st1, f32[8,128]{1,0:T(8,128)S(1)} %reduce_sum.19.st2, f32[16,128]{1,0:T(8,128)S(1)} %get-tuple-element.72.st3, ...), custom_call_target="tpu_custom_call" | custom-call | flops 13153337344 | bytes 50176000 | tf_op jit(solution)/shard_map/middle_back/pallas_call | solution.py:923
  158.8 2.2 %collective-permute-done.7.arrived_ref = f32[1416,128]{1,0:T(8,128)S(1)} collective-permute-done((f32[1416,128]{1,0:T(8,128)S(1)}, f32[1416,128]{1,0:T(8,128)S(1)}, u32[]{:S(2)}, u32[]{:S(2)}) %collective-permute-start.7) | collective-permute-done | bytes 725024 | tf_op jit(solution)/shard_map/ppermute | solution.py:25
  161.0 0.1 pack_shares.1
  161.1 16.2 %all_to_all.33.in_ref = bf16[16,96,128]{2,1,0:T(8,128)(2,1)S(1)} all-to-all(bf16[16,96,128]{2,1,0:T(8,128)(2,1)S(1)} %pack_shares.1), channel_id=1, replica_groups=mesh['batch'=16,'rows'=2] {'batch'}, dimensions={0} | all-to-all | bytes 786432 | tf_op jit(solution)/shard_map/all_to_all | solution.py:36
  177.3 0.8 sum_shares.1
  178.1 3.6 %all-to-all-start.5 = ((bf16[16,96,128]{2,1,0:T(8,128)(2,1)}), bf16[16,96,128]{2,1,0:T(8,128)(2,1)S(1)}, u32[]{:S(2)}, u32[]{:S(2)}) async-start(bf16[16,96,128]{2,1,0:T(8,128)(2,1)} %get-tuple-element.93), calls=%async_computation.5 | async-start | bytes 786432 | tf_op jit(solution)/shard_map/all_to_all | solution.py:36
  181.8 15.8 %input_grad.1 = bf16[14,28,32,512]{3,2,1,0:T(8,128)(2,1)} custom-call(s32[2]{0:T(128)S(1)} %pad_add_fusion.info, f32[8,128]{1,0:T(8,128)S(1)} %reduce_sum.18.st1, f32[8,128]{1,0:T(8,128)S(1)} %get-tuple-element.94.st5, f32[1,128]{1,0:T(1,128)S(1)} %bitcast.25, bf16[512,128]{1,0:T(8,128)(2,1)S(1)} %copy-done.4, ...), custom_call_target="tpu_custom_call" | custom-call | flops 1644167168 | bytes 35323904 | tf_op jit(solution)/shard_map/input_grad/pallas_call | solution.py:989
  197.6 0.0 all-to-all-done.5.mine_ref
  197.6 0.0 collective-permute-start.8
  197.6 1.7 collective-permute-done.8.other_ref
  199.3 1.7 replicated_grads.1
  (26 shorter events, 0.2 us)
Async XLA Ops:
  1.4 0.9 copy-start.3
  2.3 19.8 %copy-start.6 = (bf16[3,3,128,128]{3,2,1,0:T(8,128)(2,1)S(1)}, bf16[3,3,128,128]{3,2,1,0:T(8,128)(2,1)}, u32[]{:S(2)}) copy-start(bf16[3,3,128,128]{3,2,1,0:T(8,128)(2,1)} %w_ref.3) | copy-start | bytes 884740
  14.0 17.7 %collective-permute-start = (f32[28,32,128]{2,1,0:T(8,128)S(1)}, f32[28,32,128]{2,1,0:T(8,128)S(1)}, u32[]{:S(2)}, u32[]{:S(2)}) collective-permute-start(f32[28,32,128]{2,1,0:T(8,128)S(1)} %get-tuple-element.62), channel_id=1, source_target_pairs={{0,1},{1,0},{2,3},{3,2},{4,5},{5,4},{6,7},{7,6},{8,9},{9,8},{10,11... | collective-permute-start | bytes 1376264 | tf_op jit(solution)/shard_map/ppermute | solution.py:25
  15.1 16.5 %all-to-all-start = ((f32[32,8,128]{2,1,0:T(8,128)}), f32[32,8,128]{2,1,0:T(8,128)S(1)}, u32[]{:S(2)}, u32[]{:S(2)}) async-start(f32[32,8,128]{2,1,0:T(8,128)} %broadcast_in_dim.4), calls=%async_computation | async-start | bytes 262144 | tf_op jit(solution)/shard_map/all_to_all | solution.py:42
  22.3 9.3 %copy-start.9 = (f32[128]{0:T(128)S(1)}, f32[128]{0:T(128)}, u32[]{:S(2)}) copy-start(f32[128]{0:T(128)} %param.15) | copy-start | bytes 1540
  22.4 9.3 %copy-start.13 = (f32[128]{0:T(128)S(1)}, f32[128]{0:T(128)}, u32[]{:S(2)}) copy-start(f32[128]{0:T(128)} %param.16) | copy-start | bytes 1540
  31.7 28.1 %copy-start.5 = (bf16[128,512]{1,0:T(8,128)(2,1)S(1)}, bf16[128,512]{1,0:T(8,128)(2,1)}, u32[]{:S(2)}) copy-start(bf16[128,512]{1,0:T(8,128)(2,1)} %wo_ref.5) | copy-start | bytes 393220
  31.7 28.1 %copy-start.10 = (f32[128]{0:T(128)S(1)}, f32[128]{0:T(128)}, u32[]{:S(2)}) copy-start(f32[128]{0:T(128)} %param.19) | copy-start | bytes 1540
  31.7 28.1 %copy-start.11 = (f32[128]{0:T(128)S(1)}, f32[128]{0:T(128)}, u32[]{:S(2)}) copy-start(f32[128]{0:T(128)} %param.18) | copy-start | bytes 1540
  44.4 41.3 %copy-start.7 = (f32[512]{0:T(512)S(1)}, f32[512]{0:T(512)}, u32[]{:S(2)}) copy-start(f32[512]{0:T(512)} %param.22) | copy-start | bytes 6148
  44.4 41.3 %copy-start.8 = (f32[512]{0:T(512)S(1)}, f32[512]{0:T(512)}, u32[]{:S(2)}) copy-start(f32[512]{0:T(512)} %param.21) | copy-start | bytes 6148
  44.4 1.2 collective-permute-start.1
  59.8 2.8 %copy-start = (f32[14,28,32,128]{3,2,1,0:T(8,128)S(1)}, f32[14,28,32,128]{3,2,1,0:T(8,128)}, u32[]{:S(2)}) copy-start(f32[14,28,32,128]{3,2,1,0:T(8,128)} %get-tuple-element.65.z_ref.z2_ref) | copy-start | bytes 19267588
  72.8 42.0 %copy-start.1 = (bf16[14,28,32,128]{3,2,1,0:T(8,128)(2,1)}, bf16[14,28,32,128]{3,2,1,0:T(8,128)(2,1)S(1)}, u32[]{:S(2)}) copy-start(bf16[14,28,32,128]{3,2,1,0:T(8,128)(2,1)S(1)} %get-tuple-element.68.y_ref) | copy-start | bytes 9633796
  72.8 42.0 %copy-start.2 = (bf16[14,28,32,128]{3,2,1,0:T(8,128)(2,1)}, bf16[14,28,32,128]{3,2,1,0:T(8,128)(2,1)S(1)}, u32[]{:S(2)}) copy-start(bf16[14,28,32,128]{3,2,1,0:T(8,128)(2,1)S(1)} %get-tuple-element.69.g_ref.s_ref) | copy-start | bytes 9633796
  72.8 1.3 collective-permute-start.2
  114.8 1.7 copy-start.12
  116.5 2.8 %collective-permute-start.4 = (bf16[28,32,256]{2,1,0:T(8,128)(2,1)S(1)}, bf16[28,32,256]{2,1,0:T(8,128)(2,1)S(1)}, u32[]{:S(2)}, u32[]{:S(2)}) collective-permute-start(bf16[28,32,256]{2,1,0:T(8,128)(2,1)S(1)} %get-tuple-element.78), channel_id=1, source_target_pairs={{0,1},{1,0},{2,3},{3,2},{4,5},{5,4},{6,7},{7,6},{8,9},{9,8},{10,11... | collective-permute-start | bytes 1376264 | tf_op jit(solution)/shard_map/ppermute | solution.py:25
  116.5 2.8 %collective-permute-start.5 = (f32[28,32,128]{2,1,0:T(8,128)S(1)}, f32[28,32,128]{2,1,0:T(8,128)S(1)}, u32[]{:S(2)}, u32[]{:S(2)}) collective-permute-start(f32[28,32,128]{2,1,0:T(8,128)S(1)} %get-tuple-element.79), channel_id=1, source_target_pairs={{0,1},{1,0},{2,3},{3,2},{4,5},{5,4},{6,7},{7,6},{8,9},{9,8},{10,11... | collective-permute-start | bytes 1376264 | tf_op jit(solution)/shard_map/ppermute | solution.py:25
  117.0 2.3 %collective-permute-start.6 = (bf16[28,32,128]{2,1,0:T(8,128)(2,1)S(1)}, bf16[28,32,128]{2,1,0:T(8,128)(2,1)S(1)}, u32[]{:S(2)}, u32[]{:S(2)}) collective-permute-start(bf16[28,32,128]{2,1,0:T(8,128)(2,1)S(1)} %get-tuple-element.80), channel_id=1, source_target_pairs={{0,1},{1,0},{2,3},{3,2},{4,5},{5,4},{6,7},{7,6},{8,9},{9,8},{10,11... | collective-permute-start | bytes 688136 | tf_op jit(solution)/shard_map/ppermute | solution.py:25
  117.0 2.3 %collective-permute-start.3 = (f32[24,128]{1,0:T(8,128)S(1)}, f32[24,128]{1,0:T(8,128)S(1)}, u32[]{:S(2)}, u32[]{:S(2)}) collective-permute-start(f32[24,128]{1,0:T(8,128)S(1)} %get-tuple-element.77.own_ref.own4), channel_id=1, source_target_pairs={{0,1},{1,0},{2,3},{3,2},{4,5},{5,4},{6,7},{7,6},{8,9},{9,8},{10,11... | collective-permute-start | bytes 36872 | tf_op jit(solution)/shard_map/ppermute | solution.py:25
  133.5 48.3 %copy-start.4 = (bf16[512,128]{1,0:T(8,128)(2,1)S(1)}, bf16[512,128]{1,0:T(8,128)(2,1)}, u32[]{:S(2)}) copy-start(bf16[512,128]{1,0:T(8,128)(2,1)} %wi_ref.1) | copy-start | bytes 393220
  158.8 2.2 %collective-permute-start.7 = (f32[1416,128]{1,0:T(8,128)S(1)}, f32[1416,128]{1,0:T(8,128)S(1)}, u32[]{:S(2)}, u32[]{:S(2)}) collective-permute-start(f32[1416,128]{1,0:T(8,128)S(1)} %get-tuple-element.92), channel_id=1, source_target_pairs={{0,1},{1,0},{2,3},{3,2},{4,5},{5,4},{6,7},{7,6},{8,9},{9,8},{10,11... | collective-permute-start | bytes 2174984 | tf_op jit(solution)/shard_map/ppermute | solution.py:25
  178.1 19.5 %all-to-all-start.5 = ((bf16[16,96,128]{2,1,0:T(8,128)(2,1)}), bf16[16,96,128]{2,1,0:T(8,128)(2,1)S(1)}, u32[]{:S(2)}, u32[]{:S(2)}) async-start(bf16[16,96,128]{2,1,0:T(8,128)(2,1)} %get-tuple-element.93), calls=%async_computation.5 | async-start | bytes 786432 | tf_op jit(solution)/shard_map/all_to_all | solution.py:36
  197.6 1.7 collective-permute-start.8

commit v5 on v4

--- a/solution.py
+++ b/solution.py
@@ -850,7 +850,7 @@
         "second_norm",
         pixels * 384 * 128 * 2,
         pixels * 1280,
-        20,
+        42,
     )(info, st1, st2, gb, sb, z2, w_out)
     arrived3 = swapped(
         call(
@@ -876,7 +876,7 @@
         [
             step_out(rows, tile(512), bf16),
             step_out(rows, tile(512), bf16),
-            step_out(rows, tile(128), bf16),
+            (step_spec(tile(128)), pltpu.HBM((rows, columns, count, 128), bf16)),
             whole_out(edge(128), bf16),
             whole_out((16 + span, 128)),
             whole_out((16, 128)),

time: 202 us -> 198 us (0.980)
  local copies, waits for them, and re-layouts: 6.37 us -> 1.87 us
    unnamed x29 -> x25, local copies, waits for them, and re-layouts: 5.67 us -> 1.18 us
  transfers between devices with their start and end apart: 11 -> 11, of which waited for: 5 -> 5; matrix products, arithmetic and copies ran while one was open for 0% -> 0% of each run, Pallas kernels for 12% -> 13%
where the time goes in v5:
time: 198 us; the launch traced here: 197 us
  Pallas kernels  118 us (60%)
  blocking collectives  55.5 us (28%)
  starting transfers between devices  12.5 us (6%)
  waiting for transfers between devices  7.88 us (4%)
    all_to_all x3, blocking collectives, swapped(): return lax.all_to_all(spread, 'batch', 0, 0, tiled=True)  41.3 us
    pallas_call x1, Pallas kernels, local(): call(last_body, steps, [SMEM, eight, whole_spec((shares, 16 + span, 128))...  29.3 us
    pallas_call x1, Pallas kernels, local(): call(back_body, steps + 1, [SMEM, eight, eight, whole_spec((16, 128)), wh...  25.3 us
    pallas_call x1, Pallas kernels, local(): call(input_body, steps, [SMEM, eight, eight, small, whole_spec((512, 128)...  15.8 us
    all_to_all x1, blocking collectives, swapped_sum(): lax.all_to_all(spread, 'batch', 0, 0, axis_index_groups=groups, tiled=True)  14.2 us
    pallas_call x1, Pallas kernels, local(): call(middle_body, steps + 1, [SMEM, eight, small, small, step_spec(tile(1...  12.6 us
    pallas_call x1, Pallas kernels, local(): call(first_body, steps, [SMEM, step_spec(tile(512)), whole_spec((512, 128...  11.7 us
    pallas_call x1, Pallas kernels, local(): call(second_body, steps, [SMEM, eight, eight, small, small, step_spec(til...  10.8 us
  transfers between devices with their start and end apart: 11, of which 5 were waited for; matrix products, arithmetic and copies ran while one was open for 0% of the time, Pallas kernels for 13%

profile of v5, /device:TPU:0, one launch (start us, length us, event | category | flops | bytes accessed | tf_op | source)
XLA Modules:
  0.0 197.4 jit_solution(7131811771393402151)
XLA Ops:
  1.3 0.1 pad_add_fusion.info
  1.4 0.9 copy-done.2
  2.3 11.7 %first_norm_sums.1 = (f32[14,28,32,128]{3,2,1,0:T(8,128)}, f32[28,32,128]{2,1,0:T(8,128)S(1)}, f32[8,128]{1,0:T(8,128)S(1)}) custom-call(s32[2]{0:T(128)S(1)} %pad_add_fusion.info, bf16[14,28,32,512]{3,2,1,0:T(8,128)(2,1)} %bitcast.32, bf16[512,128]{1,0:T(8,128)(2,1)S(1)} %copy-done.2), custom_call_target="tpu_custom_call" | custom-call | flops 1644167168 | bytes 19267584 | tf_op jit(solution)/shard_map/first_norm_sums/pallas_call | solution.py:779
  14.0 0.4 collective-permute-start
  14.4 0.7 broadcast_in_dim.4
  15.1 7.0 %all-to-all-start = ((f32[32,8,128]{2,1,0:T(8,128)}), f32[32,8,128]{2,1,0:T(8,128)S(1)}, u32[]{:S(2)}, u32[]{:S(2)}) async-start(f32[32,8,128]{2,1,0:T(8,128)} %broadcast_in_dim.4), calls=%async_computation | async-start | bytes 262144 | tf_op jit(solution)/shard_map/all_to_all | solution.py:42
  22.1 0.0 copy-done.5
  22.1 0.2 copy.24
  22.4 0.0 copy-start.8
  22.4 0.0 copy-start.11
  22.4 9.2 %input_cross.1.xz_ref = f32[512,128]{1,0:T(8,128)S(1)} custom-call(bf16[14,28,32,512]{3,2,1,0:T(8,128)(2,1)} %bitcast.33, f32[14,28,32,128]{3,2,1,0:T(8,128)} %get-tuple-element.61.z_ref.z1_ref), custom_call_target="tpu_custom_call" | custom-call | flops 1644167168 | bytes 19267584 | tf_op jit(solution)/shard_map/input_cross/pallas_call | solution.py:795
  31.6 0.0 all-to-all-done
  31.7 0.0 collective-permute-done.edge_ref
  31.7 0.0 copy-start.4
  31.7 0.0 copy-start.9
  31.7 0.0 copy-start.10
  31.7 12.6 %middle_conv.1 = (f32[14,28,32,128]{3,2,1,0:T(8,128)}, bf16[14,28,32,128]{3,2,1,0:T(8,128)(2,1)}, f32[8,128]{1,0:T(8,128)S(1)}) custom-call(s32[2]{0:T(128)S(1)} %pad_add_fusion.info, f32[8,128]{1,0:T(8,128)S(1)} %reduce_sum.18.st1, f32[1,128]{1,0:T(1,128)S(1)} %bitcast.23, f32[1,128]{1,0:T(1,128)S(1)} %bitcast.30, ...), custom_call_target="tpu_custom_call" | custom-call | flops 4932501504 | bytes 16056320 | tf_op jit(solution)/shard_map/middle_conv/pallas_call | solution.py:811
  44.4 0.3 collective-permute-start.1
  44.6 0.9 collective-permute-done.1
  45.6 14.2 %all_to_all.30 = f32[16,8,128]{2,1,0:T(8,128)S(1)} all-to-all(f32[16,8,128]{2,1,0:T(8,128)S(1)} %broadcast_in_dim.5), channel_id=1, replica_groups={{0,2,4,6,8,10,12,14,16,18,20,22,24,26,28,30},{1,3,5,7,9,11,13,15,17,19,..., dimensions={0} | all-to-all | bytes 131072 | tf_op jit(solution)/shard_map/all_to_all | solution.py:31
  59.8 10.8 %second_norm.1 = (bf16[14,28,32,128]{3,2,1,0:T(8,128)(2,1)S(1)}, bf16[14,28,32,128]{3,2,1,0:T(8,128)(2,1)S(1)}, bf16[14,28,32,128]{3,2,1,0:T(8,128)(2,1)S(1)}, b...) custom-call(s32[2]{0:T(128)S(1)} %pad_add_fusion.info, ...), custom_call_target="tpu_custom_call" | custom-call | flops 1233125376 | bytes 16056320 | tf_op jit(solution)/shard_map/second_norm/pallas_call | solution.py:835
  70.7 0.1 collective-permute-start.2
  70.7 1.3 collective-permute-done.2.arrived_ref
  72.0 11.5 %all_to_all.31.in3 = f32[16,24,128]{2,1,0:T(8,128)S(1)} all-to-all(f32[16,24,128]{2,1,0:T(8,128)S(1)} %spread_third.1), channel_id=1, replica_groups=mesh['batch'=16,'rows'=2] {'batch'}, dimensions={0} | all-to-all | bytes 393216 | tf_op jit(solution)/shard_map/all_to_all | solution.py:36
  83.5 29.3 %last_norm.1 = (bf16[14,28,32,512]{3,2,1,0:T(8,128)(2,1)}, bf16[14,28,32,512]{3,2,1,0:T(8,128)(2,1)}, bf16[14,28,32,128]{3,2,1,0:T(8,128)(2,1)}, bf16[28,32,128]...) custom-call(s32[2]{0:T(128)S(1)} %pad_add_fusion.info, ...), custom_call_target="tpu_custom_call" | custom-call | flops 8220835840 | bytes 61014016 | tf_op jit(solution)/shard_map/last_norm/pallas_call | solution.py:868
  112.8 0.0 copy-done.1
  112.8 0.1 collective-permute-start.4
  112.9 0.5 collective-permute-start.5
  113.4 0.1 collective-permute-start.6
  113.5 0.4 collective-permute-start.3
  113.9 1.8 collective-permute-done.3.arrived_ref
  115.7 0.0 collective-permute-done.6.te_ref
  115.7 0.0 collective-permute-done.4.ye_ref
  115.7 0.0 collective-permute-done.5.ze_ref
  115.7 0.6 spread_fourth.1
  116.3 13.6 %all_to_all.32.in4 = f32[16,32,128]{2,1,0:T(8,128)S(1)} all-to-all(f32[16,32,128]{2,1,0:T(8,128)S(1)} %spread_fourth.1), channel_id=1, replica_groups=mesh['batch'=16,'rows'=2] {'batch'}, dimensions={0} | all-to-all | bytes 524288 | tf_op jit(solution)/shard_map/all_to_all | solution.py:36
  129.9 25.3 %middle_back.1 = (bf16[14,28,32,128]{3,2,1,0:T(8,128)(2,1)}, f32[1416,128]{1,0:T(8,128)S(1)}, f32[1416,128]{1,0:T(8,128)S(1)}, f32[16,128]{1,0:T(8,128)S(1)}) custom-call(s32[2]{0:T(128)S(1)} %pad_add_fusion.info, f32[8,128]{1,0:T(8,128)S(1)} %reduce_sum.18.st1, f32[8,128]{1,0:T(8,128)S(1)} %reduce_sum.19.st2, f32[16,128]{1,0:T(8,128)S(1)} %get-tuple-element.72.st3, ...), custom_call_target="tpu_custom_call" | custom-call | flops 13153337344 | bytes 50176000 | tf_op jit(solution)/shard_map/middle_back/pallas_call | solution.py:923
  155.2 0.0 collective-permute-start.7
  155.2 2.2 %collective-permute-done.7.arrived_ref = f32[1416,128]{1,0:T(8,128)S(1)} collective-permute-done((f32[1416,128]{1,0:T(8,128)S(1)}, f32[1416,128]{1,0:T(8,128)S(1)}, u32[]{:S(2)}, u32[]{:S(2)}) %collective-permute-start.7) | collective-permute-done | bytes 725024 | tf_op jit(solution)/shard_map/ppermute | solution.py:25
  157.4 0.1 pack_shares.1
  157.5 16.2 %all_to_all.33.in_ref = bf16[16,96,128]{2,1,0:T(8,128)(2,1)S(1)} all-to-all(bf16[16,96,128]{2,1,0:T(8,128)(2,1)S(1)} %pack_shares.1), channel_id=1, replica_groups=mesh['batch'=16,'rows'=2] {'batch'}, dimensions={0} | all-to-all | bytes 786432 | tf_op jit(solution)/shard_map/all_to_all | solution.py:36
  173.7 0.8 sum_shares.1
  174.5 3.6 %all-to-all-start.5 = ((bf16[16,96,128]{2,1,0:T(8,128)(2,1)}), bf16[16,96,128]{2,1,0:T(8,128)(2,1)S(1)}, u32[]{:S(2)}, u32[]{:S(2)}) async-start(bf16[16,96,128]{2,1,0:T(8,128)(2,1)} %get-tuple-element.93), calls=%async_computation.5 | async-start | bytes 786432 | tf_op jit(solution)/shard_map/all_to_all | solution.py:36
  178.2 15.8 %input_grad.1 = bf16[14,28,32,512]{3,2,1,0:T(8,128)(2,1)} custom-call(s32[2]{0:T(128)S(1)} %pad_add_fusion.info, f32[8,128]{1,0:T(8,128)S(1)} %reduce_sum.18.st1, f32[8,128]{1,0:T(8,128)S(1)} %get-tuple-element.94.st5, f32[1,128]{1,0:T(1,128)S(1)} %bitcast.25, bf16[512,128]{1,0:T(8,128)(2,1)S(1)} %copy-done.3, ...), custom_call_target="tpu_custom_call" | custom-call | flops 1644167168 | bytes 35323904 | tf_op jit(solution)/shard_map/input_grad/pallas_call | solution.py:989
  194.0 0.0 all-to-all-done.5.mine_ref
  194.0 0.0 collective-permute-start.8
  194.0 1.7 collective-permute-done.8.other_ref
  195.7 1.7 replicated_grads.1
  (22 shorter events, 0.1 us)
Async XLA Ops:
  1.4 0.9 copy-start.2
  2.3 19.8 %copy-start.5 = (bf16[3,3,128,128]{3,2,1,0:T(8,128)(2,1)S(1)}, bf16[3,3,128,128]{3,2,1,0:T(8,128)(2,1)}, u32[]{:S(2)}) copy-start(bf16[3,3,128,128]{3,2,1,0:T(8,128)(2,1)} %w_ref.3) | copy-start | bytes 884740
  14.0 17.7 %collective-permute-start = (f32[28,32,128]{2,1,0:T(8,128)S(1)}, f32[28,32,128]{2,1,0:T(8,128)S(1)}, u32[]{:S(2)}, u32[]{:S(2)}) collective-permute-start(f32[28,32,128]{2,1,0:T(8,128)S(1)} %get-tuple-element.62), channel_id=1, source_target_pairs={{0,1},{1,0},{2,3},{3,2},{4,5},{5,4},{6,7},{7,6},{8,9},{9,8},{10,11... | collective-permute-start | bytes 1376264 | tf_op jit(solution)/shard_map/ppermute | solution.py:25
  15.1 16.5 %all-to-all-start = ((f32[32,8,128]{2,1,0:T(8,128)}), f32[32,8,128]{2,1,0:T(8,128)S(1)}, u32[]{:S(2)}, u32[]{:S(2)}) async-start(f32[32,8,128]{2,1,0:T(8,128)} %broadcast_in_dim.4), calls=%async_computation | async-start | bytes 262144 | tf_op jit(solution)/shard_map/all_to_all | solution.py:42
  22.4 9.3 %copy-start.8 = (f32[128]{0:T(128)S(1)}, f32[128]{0:T(128)}, u32[]{:S(2)}) copy-start(f32[128]{0:T(128)} %param.15) | copy-start | bytes 1540
  22.4 9.3 %copy-start.11 = (f32[128]{0:T(128)S(1)}, f32[128]{0:T(128)}, u32[]{:S(2)}) copy-start(f32[128]{0:T(128)} %param.16) | copy-start | bytes 1540
  31.7 28.1 %copy-start.4 = (bf16[128,512]{1,0:T(8,128)(2,1)S(1)}, bf16[128,512]{1,0:T(8,128)(2,1)}, u32[]{:S(2)}) copy-start(bf16[128,512]{1,0:T(8,128)(2,1)} %wo_ref.5) | copy-start | bytes 393220
  31.7 28.1 %copy-start.9 = (f32[128]{0:T(128)S(1)}, f32[128]{0:T(128)}, u32[]{:S(2)}) copy-start(f32[128]{0:T(128)} %param.19) | copy-start | bytes 1540
  31.7 28.1 %copy-start.10 = (f32[128]{0:T(128)S(1)}, f32[128]{0:T(128)}, u32[]{:S(2)}) copy-start(f32[128]{0:T(128)} %param.18) | copy-start | bytes 1540
  44.4 39.2 %copy-start.6 = (f32[512]{0:T(512)S(1)}, f32[512]{0:T(512)}, u32[]{:S(2)}) copy-start(f32[512]{0:T(512)} %param.22) | copy-start | bytes 6148
  44.4 39.2 %copy-start.7 = (f32[512]{0:T(512)S(1)}, f32[512]{0:T(512)}, u32[]{:S(2)}) copy-start(f32[512]{0:T(512)} %param.21) | copy-start | bytes 6148
  44.4 1.2 collective-permute-start.1
  70.6 42.2 %copy-start = (bf16[14,28,32,128]{3,2,1,0:T(8,128)(2,1)}, bf16[14,28,32,128]{3,2,1,0:T(8,128)(2,1)S(1)}, u32[]{:S(2)}) copy-start(bf16[14,28,32,128]{3,2,1,0:T(8,128)(2,1)S(1)} %get-tuple-element.68.y_ref) | copy-start | bytes 9633796
  70.7 42.2 %copy-start.1 = (bf16[14,28,32,128]{3,2,1,0:T(8,128)(2,1)}, bf16[14,28,32,128]{3,2,1,0:T(8,128)(2,1)S(1)}, u32[]{:S(2)}) copy-start(bf16[14,28,32,128]{3,2,1,0:T(8,128)(2,1)S(1)} %get-tuple-element.69.g_ref.s_ref) | copy-start | bytes 9633796
  70.7 1.3 collective-permute-start.2
  112.8 2.9 %collective-permute-start.4 = (bf16[28,32,256]{2,1,0:T(8,128)(2,1)S(1)}, bf16[28,32,256]{2,1,0:T(8,128)(2,1)S(1)}, u32[]{:S(2)}, u32[]{:S(2)}) collective-permute-start(bf16[28,32,256]{2,1,0:T(8,128)(2,1)S(1)} %get-tuple-element.78), channel_id=1, source_target_pairs={{0,1},{1,0},{2,3},{3,2},{4,5},{5,4},{6,7},{7,6},{8,9},{9,8},{10,11... | collective-permute-start | bytes 1376264 | tf_op jit(solution)/shard_map/ppermute | solution.py:25
  112.9 2.8 %collective-permute-start.5 = (f32[28,32,128]{2,1,0:T(8,128)S(1)}, f32[28,32,128]{2,1,0:T(8,128)S(1)}, u32[]{:S(2)}, u32[]{:S(2)}) collective-permute-start(f32[28,32,128]{2,1,0:T(8,128)S(1)} %get-tuple-element.79), channel_id=1, source_target_pairs={{0,1},{1,0},{2,3},{3,2},{4,5},{5,4},{6,7},{7,6},{8,9},{9,8},{10,11... | collective-permute-start | bytes 1376264 | tf_op jit(solution)/shard_map/ppermute | solution.py:25
  113.4 2.3 %collective-permute-start.6 = (bf16[28,32,128]{2,1,0:T(8,128)(2,1)S(1)}, bf16[28,32,128]{2,1,0:T(8,128)(2,1)S(1)}, u32[]{:S(2)}, u32[]{:S(2)}) collective-permute-start(bf16[28,32,128]{2,1,0:T(8,128)(2,1)S(1)} %get-tuple-element.80), channel_id=1, source_target_pairs={{0,1},{1,0},{2,3},{3,2},{4,5},{5,4},{6,7},{7,6},{8,9},{9,8},{10,11... | collective-permute-start | bytes 688136 | tf_op jit(solution)/shard_map/ppermute | solution.py:25
  113.5 2.2 %collective-permute-start.3 = (f32[24,128]{1,0:T(8,128)S(1)}, f32[24,128]{1,0:T(8,128)S(1)}, u32[]{:S(2)}, u32[]{:S(2)}) collective-permute-start(f32[24,128]{1,0:T(8,128)S(1)} %get-tuple-element.77.own_ref.own4), channel_id=1, source_target_pairs={{0,1},{1,0},{2,3},{3,2},{4,5},{5,4},{6,7},{7,6},{8,9},{9,8},{10,11... | collective-permute-start | bytes 36872 | tf_op jit(solution)/shard_map/ppermute | solution.py:25
  129.9 48.3 %copy-start.3 = (bf16[512,128]{1,0:T(8,128)(2,1)S(1)}, bf16[512,128]{1,0:T(8,128)(2,1)}, u32[]{:S(2)}) copy-start(bf16[512,128]{1,0:T(8,128)(2,1)} %wi_ref.1) | copy-start | bytes 393220
  155.2 2.2 %collective-permute-start.7 = (f32[1416,128]{1,0:T(8,128)S(1)}, f32[1416,128]{1,0:T(8,128)S(1)}, u32[]{:S(2)}, u32[]{:S(2)}) collective-permute-start(f32[1416,128]{1,0:T(8,128)S(1)} %get-tuple-element.92), channel_id=1, source_target_pairs={{0,1},{1,0},{2,3},{3,2},{4,5},{5,4},{6,7},{7,6},{8,9},{9,8},{10,11... | collective-permute-start | bytes 2174984 | tf_op jit(solution)/shard_map/ppermute | solution.py:25
  174.5 19.5 %all-to-all-start.5 = ((bf16[16,96,128]{2,1,0:T(8,128)(2,1)}), bf16[16,96,128]{2,1,0:T(8,128)(2,1)S(1)}, u32[]{:S(2)}, u32[]{:S(2)}) async-start(bf16[16,96,128]{2,1,0:T(8,128)(2,1)} %get-tuple-element.93), calls=%async_computation.5 | async-start | bytes 786432 | tf_op jit(solution)/shard_map/all_to_all | solution.py:36
  194.0 1.7 collective-permute-start.8

commit v6 on v5

--- a/solution.py
+++ b/solution.py
@@ -36,9 +36,7 @@
     return lax.all_to_all(spread, "batch", 0, 0, tiled=True)
 
 
-def summed_at_once(block):
-    total = lax.axis_size("batch") * lax.axis_size("rows")
-    spread = jnp.broadcast_to(block[None], (total,) + block.shape)
+def summed_at_once(spread):
     return jnp.sum(lax.all_to_all(spread, axes, 0, 0, tiled=True), axis=0)
 
 
@@ -203,10 +201,17 @@
     @pl.when(step == pl.num_programs(0) - 1)
     def _():
         pixels = (info[0] * (pl.num_programs(0) * tall * columns)).astype(f32)
-        stat_ref[...] = jnp.zeros_like(stat_ref)
-        stat_ref[0:1, :] = total_row(zacc[0])
-        stat_ref[1:2, :] = total_row(zacc[1])
-        stat_ref[2:3, :] = jnp.full((1, 128), pixels, f32)
+        block = jnp.concatenate(
+            [
+                total_row(zacc[0]),
+                total_row(zacc[1]),
+                jnp.full((1, 128), pixels, f32),
+                jnp.zeros((5, 128), f32),
+            ],
+            axis=0,
+        )
+        for k in range(stat_ref.shape[0]):
+            stat_ref[k] = block
 
 
 def cross_body(x_ref, z_ref, xz_ref, acc):
@@ -775,6 +780,7 @@
         return pltpu.VMEM((rows + 2, columns + 2, count, 128), bf16)
 
     pixels = count * rows * columns
+    shares = lax.axis_size("batch")
 
     z1, z1_edge, st1 = call(
         first_body,
@@ -783,12 +789,13 @@
         [
             step_out(rows, tile(128), f32),
             whole_out(edge(128)),
-            whole_out((8, 128)),
+            whole_out((shares * lax.axis_size("rows"), 8, 128)),
         ],
         [pltpu.VMEM((2, 8, 128), f32)],
         "first_norm_sums",
         pixels * 512 * 128 * 2,
         pixels * 1536,
+        58,
     )(info, images, w_in)
     z1_edge = partner(z1_edge, 1)
     st1 = summed_at_once(st1)
@@ -805,7 +812,6 @@
     w_back = jnp.swapaxes(w_mid[::-1, ::-1], 2, 3)
     xz, w_back = lax.optimization_barrier((xz, w_back))
 
-    shares = lax.axis_size("batch")
     span = max(8, 128 // shares)
     everyone = [list(range(lax.axis_size("batch")))]
     z2, act_a, st2 = call(

time: 198 us -> 197 us (level)
  no operation moved by 1% of the time
where the time goes in v6:
time: 197 us
  Pallas kernels  118 us (60%)
  blocking collectives  55.5 us (28%)
  starting transfers between devices  12.5 us (6%)
  waiting for transfers between devices  7.88 us (4%)
    all_to_all x3, blocking collectives, swapped(): return lax.all_to_all(spread, 'batch', 0, 0, tiled=True)  41.3 us
    pallas_call x1, Pallas kernels, local(): call(last_body, steps, [SMEM, eight, whole_spec((shares, 16 + span, 128))...  29.3 us
    pallas_call x1, Pallas kernels, local(): call(back_body, steps + 1, [SMEM, eight, eight, whole_spec((16, 128)), wh...  25.3 us
    pallas_call x1, Pallas kernels, local(): call(input_body, steps, [SMEM, eight, eight, small, whole_spec((512, 128)...  15.8 us
    all_to_all x1, blocking collectives, swapped_sum(): lax.all_to_all(spread, 'batch', 0, 0, axis_index_groups=groups, tiled=True)  14.2 us
    pallas_call x1, Pallas kernels, local(): call(middle_body, steps + 1, [SMEM, eight, small, small, step_spec(tile(1...  12.6 us
    pallas_call x1, Pallas kernels, local(): call(first_body, steps, [SMEM, step_spec(tile(512)), whole_spec((512, 128...  11.9 us
    pallas_call x1, Pallas kernels, local(): call(second_body, steps, [SMEM, eight, eight, small, small, step_spec(til...  10.8 us
  transfers between devices with their start and end apart: 11, of which 5 were waited for; matrix products, arithmetic and copies ran while one was open for 0% of the time, Pallas kernels for 13%

profile of v6, /device:TPU:0, one launch (start us, length us, event | category | flops | bytes accessed | tf_op | source)
XLA Modules:
  0.0 196.5 jit_solution(9254725427531316963)
XLA Ops:
  1.3 0.6 pad_add_fusion.info
  1.9 11.9 %first_norm_sums.1 = (f32[14,28,32,128]{3,2,1,0:T(8,128)}, f32[28,32,128]{2,1,0:T(8,128)}, f32[32,8,128]{2,1,0:T(8,128)}) custom-call(s32[2]{0:T(128)} %pad_add_fusion.info, bf16[14,28,32,512]{3,2,1,0:T(8,128)(2,1)} %bitcast.32, bf16[512,128]{1,0:T(8,128)(2,1)} %wi_ref.1), custom_call_target="tpu_custom_call" | custom-call | flops 1644167168 | bytes 19267584 | tf_op jit(solution)/shard_map/first_norm_sums/pallas_call | solution.py:785
  13.8 0.5 collective-permute-start
  14.2 7.0 %all-to-all-start = ((f32[32,8,128]{2,1,0:T(8,128)}), f32[32,8,128]{2,1,0:T(8,128)S(1)}, u32[]{:S(2)}, u32[]{:S(2)}) async-start(f32[32,8,128]{2,1,0:T(8,128)} %get-tuple-element.60), calls=%async_computation | async-start | bytes 262144 | tf_op jit(solution)/shard_map/all_to_all | solution.py:40
  21.2 0.2 copy.24
  21.4 0.0 copy-start.5
  21.5 0.0 copy-start.8
  21.5 0.0 copy-start.11
  21.5 9.2 %input_cross.1.xz_ref = f32[512,128]{1,0:T(8,128)S(1)} custom-call(bf16[14,28,32,512]{3,2,1,0:T(8,128)(2,1)} %bitcast.33, f32[14,28,32,128]{3,2,1,0:T(8,128)} %get-tuple-element.61.z_ref.z1_ref), custom_call_target="tpu_custom_call" | custom-call | flops 1644167168 | bytes 19267584 | tf_op jit(solution)/shard_map/input_cross/pallas_call | solution.py:802
  30.7 0.0 all-to-all-done
  30.8 0.0 collective-permute-done.edge_ref
  30.8 0.0 copy-start.3
  30.8 0.0 copy-start.9
  30.8 0.0 copy-start.10
  30.9 12.6 %middle_conv.1 = (f32[14,28,32,128]{3,2,1,0:T(8,128)}, bf16[14,28,32,128]{3,2,1,0:T(8,128)(2,1)}, f32[8,128]{1,0:T(8,128)S(1)}) custom-call(s32[2]{0:T(128)S(1)} %copy-done.5, f32[8,128]{1,0:T(8,128)S(1)} %reduce_sum.18.st1, f32[1,128]{1,0:T(1,128)S(1)} %bitcast.23, f32[1,128]{1,0:T(1,128)S(1)} %bitcast.30, ...), custom_call_target="tpu_custom_call" | custom-call | flops 4932501504 | bytes 16056320 | tf_op jit(solution)/shard_map/middle_conv/pallas_call | solution.py:817
  43.5 0.3 collective-permute-start.1
  43.8 0.9 collective-permute-done.1
  44.7 14.2 %all_to_all.30 = f32[16,8,128]{2,1,0:T(8,128)S(1)} all-to-all(f32[16,8,128]{2,1,0:T(8,128)S(1)} %broadcast_in_dim.2), channel_id=1, replica_groups={{0,2,4,6,8,10,12,14,16,18,20,22,24,26,28,30},{1,3,5,7,9,11,13,15,17,19,..., dimensions={0} | all-to-all | bytes 131072 | tf_op jit(solution)/shard_map/all_to_all | solution.py:31
  58.9 0.0 copy-done.3
  58.9 10.8 %second_norm.1 = (bf16[14,28,32,128]{3,2,1,0:T(8,128)(2,1)S(1)}, bf16[14,28,32,128]{3,2,1,0:T(8,128)(2,1)S(1)}, bf16[14,28,32,128]{3,2,1,0:T(8,128)(2,1)S(1)}, b...) custom-call(s32[2]{0:T(128)S(1)} %copy-done.5, ...), custom_call_target="tpu_custom_call" | custom-call | flops 1233125376 | bytes 16056320 | tf_op jit(solution)/shard_map/second_norm/pallas_call | solution.py:841
  69.8 0.1 collective-permute-start.2
  69.9 1.3 collective-permute-done.2.arrived_ref
  71.1 11.5 %all_to_all.31.in3 = f32[16,24,128]{2,1,0:T(8,128)S(1)} all-to-all(f32[16,24,128]{2,1,0:T(8,128)S(1)} %spread_third.1), channel_id=1, replica_groups=mesh['batch'=16,'rows'=2] {'batch'}, dimensions={0} | all-to-all | bytes 393216 | tf_op jit(solution)/shard_map/all_to_all | solution.py:36
  82.6 0.0 copy-done.6
  82.7 29.3 %last_norm.1 = (bf16[14,28,32,512]{3,2,1,0:T(8,128)(2,1)}, bf16[14,28,32,512]{3,2,1,0:T(8,128)(2,1)}, bf16[14,28,32,128]{3,2,1,0:T(8,128)(2,1)}, bf16[28,32,128]...) custom-call(s32[2]{0:T(128)S(1)} %copy-done.5, ...), custom_call_target="tpu_custom_call" | custom-call | flops 8220835840 | bytes 61014016 | tf_op jit(solution)/shard_map/last_norm/pallas_call | solution.py:874
  111.9 0.0 copy-done
  111.9 0.1 collective-permute-start.4
  112.0 0.5 collective-permute-start.5
  112.5 0.1 collective-permute-start.6
  112.6 0.4 collective-permute-start.3
  113.0 1.8 collective-permute-done.3.arrived_ref
  114.8 0.0 collective-permute-done.6.te_ref
  114.8 0.0 collective-permute-done.4.ye_ref
  114.8 0.0 collective-permute-done.5.ze_ref
  114.8 0.6 spread_fourth.1
  115.4 13.6 %all_to_all.32.in4 = f32[16,32,128]{2,1,0:T(8,128)S(1)} all-to-all(f32[16,32,128]{2,1,0:T(8,128)S(1)} %spread_fourth.1), channel_id=1, replica_groups=mesh['batch'=16,'rows'=2] {'batch'}, dimensions={0} | all-to-all | bytes 524288 | tf_op jit(solution)/shard_map/all_to_all | solution.py:36
  129.0 25.3 %middle_back.1 = (bf16[14,28,32,128]{3,2,1,0:T(8,128)(2,1)}, f32[1416,128]{1,0:T(8,128)S(1)}, f32[1416,128]{1,0:T(8,128)S(1)}, f32[16,128]{1,0:T(8,128)S(1)}) custom-call(s32[2]{0:T(128)S(1)} %copy-done.5, f32[8,128]{1,0:T(8,128)S(1)} %reduce_sum.18.st1, f32[8,128]{1,0:T(8,128)S(1)} %reduce_sum.19.st2, f32[16,128]{1,0:T(8,128)S(1)} %get-tuple-element.72.st3, ...), custom_call_target="tpu_custom_call" | custom-call | flops 13153337344 | bytes 50176000 | tf_op jit(solution)/shard_map/middle_back/pallas_call | solution.py:929
  154.3 0.0 collective-permute-start.7
  154.3 2.2 %collective-permute-done.7.arrived_ref = f32[1416,128]{1,0:T(8,128)S(1)} collective-permute-done((f32[1416,128]{1,0:T(8,128)S(1)}, f32[1416,128]{1,0:T(8,128)S(1)}, u32[]{:S(2)}, u32[]{:S(2)}) %collective-permute-start.7) | collective-permute-done | bytes 725024 | tf_op jit(solution)/shard_map/ppermute | solution.py:25
  156.5 0.1 pack_shares.1
  156.6 16.2 %all_to_all.33.in_ref = bf16[16,96,128]{2,1,0:T(8,128)(2,1)S(1)} all-to-all(bf16[16,96,128]{2,1,0:T(8,128)(2,1)S(1)} %pack_shares.1), channel_id=1, replica_groups=mesh['batch'=16,'rows'=2] {'batch'}, dimensions={0} | all-to-all | bytes 786432 | tf_op jit(solution)/shard_map/all_to_all | solution.py:36
  172.8 0.8 sum_shares.1
  173.6 3.6 %all-to-all-start.5 = ((bf16[16,96,128]{2,1,0:T(8,128)(2,1)}), bf16[16,96,128]{2,1,0:T(8,128)(2,1)S(1)}, u32[]{:S(2)}, u32[]{:S(2)}) async-start(bf16[16,96,128]{2,1,0:T(8,128)(2,1)} %get-tuple-element.93), calls=%async_computation.5 | async-start | bytes 786432 | tf_op jit(solution)/shard_map/all_to_all | solution.py:36
  177.3 15.8 %input_grad.1 = bf16[14,28,32,512]{3,2,1,0:T(8,128)(2,1)} custom-call(s32[2]{0:T(128)S(1)} %copy-done.5, f32[8,128]{1,0:T(8,128)S(1)} %reduce_sum.18.st1, f32[8,128]{1,0:T(8,128)S(1)} %get-tuple-element.94.st5, f32[1,128]{1,0:T(1,128)S(1)} %bitcast.25, bf16[512,128]{1,0:T(8,128)(2,1)S(1)} %copy-done.2, bf16[14,28,32,128]{3,2,1,0:T(8,128)(2,1)} %get-tuple-element.95.h_ref, ...), custom_call_target="tpu_custom_call" | custom-call | flops 1644167168 | bytes 35323904 | tf_op jit(solution)/shard_map/input_grad/pallas_call | solution.py:995
  193.1 0.0 all-to-all-done.5.mine_ref
  193.1 0.0 collective-permute-start.8
  193.1 1.7 collective-permute-done.8.other_ref
  194.8 1.7 replicated_grads.1
  (21 shorter events, 0.1 us)
Async XLA Ops:
  1.9 19.3 %copy-start.4 = (bf16[3,3,128,128]{3,2,1,0:T(8,128)(2,1)S(1)}, bf16[3,3,128,128]{3,2,1,0:T(8,128)(2,1)}, u32[]{:S(2)}) copy-start(bf16[3,3,128,128]{3,2,1,0:T(8,128)(2,1)} %w_ref.3) | copy-start | bytes 884740
  13.8 17.0 %collective-permute-start = (f32[28,32,128]{2,1,0:T(8,128)}, f32[28,32,128]{2,1,0:T(8,128)S(1)}, u32[]{:S(2)}, u32[]{:S(2)}) collective-permute-start(f32[28,32,128]{2,1,0:T(8,128)} %get-tuple-element.62), channel_id=1, source_target_pairs={{0,1},{1,0},{2,3},{3,2},{4,5},{5,4},{6,7},{7,6},{8,9},{9,8},{10,11... | collective-permute-start | bytes 1376264 | tf_op jit(solution)/shard_map/ppermute | solution.py:25
  14.2 16.5 %all-to-all-start = ((f32[32,8,128]{2,1,0:T(8,128)}), f32[32,8,128]{2,1,0:T(8,128)S(1)}, u32[]{:S(2)}, u32[]{:S(2)}) async-start(f32[32,8,128]{2,1,0:T(8,128)} %get-tuple-element.60), calls=%async_computation | async-start | bytes 262144 | tf_op jit(solution)/shard_map/all_to_all | solution.py:40
  21.4 9.3 %copy-start.5 = (s32[2]{0:T(128)S(1)}, s32[2]{0:T(128)}, u32[]{:S(2)}) copy-start(s32[2]{0:T(128)} %pad_add_fusion.info) | copy-start | bytes 28
  21.5 9.3 %copy-start.8 = (f32[128]{0:T(128)S(1)}, f32[128]{0:T(128)}, u32[]{:S(2)}) copy-start(f32[128]{0:T(128)} %param.15) | copy-start | bytes 1540
  21.5 9.3 %copy-start.11 = (f32[128]{0:T(128)S(1)}, f32[128]{0:T(128)}, u32[]{:S(2)}) copy-start(f32[128]{0:T(128)} %param.16) | copy-start | bytes 1540
  30.8 28.1 %copy-start.3 = (bf16[128,512]{1,0:T(8,128)(2,1)S(1)}, bf16[128,512]{1,0:T(8,128)(2,1)}, u32[]{:S(2)}) copy-start(bf16[128,512]{1,0:T(8,128)(2,1)} %wo_ref.5) | copy-start | bytes 393220
  30.8 28.1 %copy-start.9 = (f32[128]{0:T(128)S(1)}, f32[128]{0:T(128)}, u32[]{:S(2)}) copy-start(f32[128]{0:T(128)} %param.19) | copy-start | bytes 1540
  30.8 28.1 %copy-start.10 = (f32[128]{0:T(128)S(1)}, f32[128]{0:T(128)}, u32[]{:S(2)}) copy-start(f32[128]{0:T(128)} %param.18) | copy-start | bytes 1540
  43.5 39.2 %copy-start.6 = (f32[512]{0:T(512)S(1)}, f32[512]{0:T(512)}, u32[]{:S(2)}) copy-start(f32[512]{0:T(512)} %param.22) | copy-start | bytes 6148
  43.5 39.2 %copy-start.7 = (f32[512]{0:T(512)S(1)}, f32[512]{0:T(512)}, u32[]{:S(2)}) copy-start(f32[512]{0:T(512)} %param.21) | copy-start | bytes 6148
  43.5 1.2 collective-permute-start.1
  69.8 42.2 %copy-start = (bf16[14,28,32,128]{3,2,1,0:T(8,128)(2,1)}, bf16[14,28,32,128]{3,2,1,0:T(8,128)(2,1)S(1)}, u32[]{:S(2)}) copy-start(bf16[14,28,32,128]{3,2,1,0:T(8,128)(2,1)S(1)} %get-tuple-element.68.y_ref) | copy-start | bytes 9633796
  69.8 42.2 %copy-start.1 = (bf16[14,28,32,128]{3,2,1,0:T(8,128)(2,1)}, bf16[14,28,32,128]{3,2,1,0:T(8,128)(2,1)S(1)}, u32[]{:S(2)}) copy-start(bf16[14,28,32,128]{3,2,1,0:T(8,128)(2,1)S(1)} %get-tuple-element.69.g_ref.s_ref) | copy-start | bytes 9633796
  69.8 1.3 collective-permute-start.2
  111.9 2.9 %collective-permute-start.4 = (bf16[28,32,256]{2,1,0:T(8,128)(2,1)S(1)}, bf16[28,32,256]{2,1,0:T(8,128)(2,1)S(1)}, u32[]{:S(2)}, u32[]{:S(2)}) collective-permute-start(bf16[28,32,256]{2,1,0:T(8,128)(2,1)S(1)} %get-tuple-element.78), channel_id=1, source_target_pairs={{0,1},{1,0},{2,3},{3,2},{4,5},{5,4},{6,7},{7,6},{8,9},{9,8},{10,11... | collective-permute-start | bytes 1376264 | tf_op jit(solution)/shard_map/ppermute | solution.py:25
  112.0 2.8 %collective-permute-start.5 = (f32[28,32,128]{2,1,0:T(8,128)S(1)}, f32[28,32,128]{2,1,0:T(8,128)S(1)}, u32[]{:S(2)}, u32[]{:S(2)}) collective-permute-start(f32[28,32,128]{2,1,0:T(8,128)S(1)} %get-tuple-element.79), channel_id=1, source_target_pairs={{0,1},{1,0},{2,3},{3,2},{4,5},{5,4},{6,7},{7,6},{8,9},{9,8},{10,11... | collective-permute-start | bytes 1376264 | tf_op jit(solution)/shard_map/ppermute | solution.py:25
  112.5 2.3 %collective-permute-start.6 = (bf16[28,32,128]{2,1,0:T(8,128)(2,1)S(1)}, bf16[28,32,128]{2,1,0:T(8,128)(2,1)S(1)}, u32[]{:S(2)}, u32[]{:S(2)}) collective-permute-start(bf16[28,32,128]{2,1,0:T(8,128)(2,1)S(1)} %get-tuple-element.80), channel_id=1, source_target_pairs={{0,1},{1,0},{2,3},{3,2},{4,5},{5,4},{6,7},{7,6},{8,9},{9,8},{10,11... | collective-permute-start | bytes 688136 | tf_op jit(solution)/shard_map/ppermute | solution.py:25
  112.6 2.2 %collective-permute-start.3 = (f32[24,128]{1,0:T(8,128)S(1)}, f32[24,128]{1,0:T(8,128)S(1)}, u32[]{:S(2)}, u32[]{:S(2)}) collective-permute-start(f32[24,128]{1,0:T(8,128)S(1)} %get-tuple-element.77.own_ref.own4), channel_id=1, source_target_pairs={{0,1},{1,0},{2,3},{3,2},{4,5},{5,4},{6,7},{7,6},{8,9},{9,8},{10,11... | collective-permute-start | bytes 36872 | tf_op jit(solution)/shard_map/ppermute | solution.py:25
  129.0 48.3 %copy-start.2 = (bf16[512,128]{1,0:T(8,128)(2,1)S(1)}, bf16[512,128]{1,0:T(8,128)(2,1)}, u32[]{:S(2)}) copy-start(bf16[512,128]{1,0:T(8,128)(2,1)} %wi_ref.1) | copy-start | bytes 393220
  154.3 2.2 %collective-permute-start.7 = (f32[1416,128]{1,0:T(8,128)S(1)}, f32[1416,128]{1,0:T(8,128)S(1)}, u32[]{:S(2)}, u32[]{:S(2)}) collective-permute-start(f32[1416,128]{1,0:T(8,128)S(1)} %get-tuple-element.92), channel_id=1, source_target_pairs={{0,1},{1,0},{2,3},{3,2},{4,5},{5,4},{6,7},{7,6},{8,9},{9,8},{10,11... | collective-permute-start | bytes 2174984 | tf_op jit(solution)/shard_map/ppermute | solution.py:25
  173.6 19.5 %all-to-all-start.5 = ((bf16[16,96,128]{2,1,0:T(8,128)(2,1)}), bf16[16,96,128]{2,1,0:T(8,128)(2,1)S(1)}, u32[]{:S(2)}, u32[]{:S(2)}) async-start(bf16[16,96,128]{2,1,0:T(8,128)(2,1)} %get-tuple-element.93), calls=%async_computation.5 | async-start | bytes 786432 | tf_op jit(solution)/shard_map/all_to_all | solution.py:36
  193.1 1.7 collective-permute-start.8

commit v7 on v6

--- a/solution.py
+++ b/solution.py
@@ -448,7 +448,7 @@
     mask = live(info, images, 512)
     bias = coef[0:1, :]
     zero = jnp.zeros((), bf16)
-    piece = columns // 4
+    piece = columns
     parts = [(r, c) for r in range(tall) for c in range(0, columns, piece)]
     n = piece * images
 

time: 197 us -> 199 us (1.010)
  no operation moved by 1% of the time
where the time goes in v7:
time: 199 us; the launch traced here: 198 us
  Pallas kernels  119 us (60%)
  blocking collectives  55.5 us (28%)
  starting transfers between devices  12.5 us (6%)
  waiting for transfers between devices  7.88 us (4%)
    all_to_all x3, blocking collectives, swapped(): return lax.all_to_all(spread, 'batch', 0, 0, tiled=True)  41.3 us
    pallas_call x1, Pallas kernels, local(): call(last_body, steps, [SMEM, eight, whole_spec((shares, 16 + span, 128))...  30.5 us
    pallas_call x1, Pallas kernels, local(): call(back_body, steps + 1, [SMEM, eight, eight, whole_spec((16, 128)), wh...  25.3 us
    pallas_call x1, Pallas kernels, local(): call(input_body, steps, [SMEM, eight, eight, small, whole_spec((512, 128)...  15.8 us
    all_to_all x1, blocking collectives, swapped_sum(): lax.all_to_all(spread, 'batch', 0, 0, axis_index_groups=groups, tiled=True)  14.2 us
    pallas_call x1, Pallas kernels, local(): call(middle_body, steps + 1, [SMEM, eight, small, small, step_spec(tile(1...  12.6 us
    pallas_call x1, Pallas kernels, local(): call(first_body, steps, [SMEM, step_spec(tile(512)), whole_spec((512, 128...  11.9 us
    pallas_call x1, Pallas kernels, local(): call(second_body, steps, [SMEM, eight, eight, small, small, step_spec(til...  10.8 us
  transfers between devices with their start and end apart: 11, of which 5 were waited for; matrix products, arithmetic and copies ran while one was open for 0% of the time, Pallas kernels for 13%

profile of v7, /device:TPU:0, one launch (start us, length us, event | category | flops | bytes accessed | tf_op | source)
XLA Modules:
  0.0 197.8 jit_solution(12698618576694334384)
XLA Ops:
  1.3 0.6 pad_add_fusion.info
  1.9 11.9 %first_norm_sums.1 = (f32[14,28,32,128]{3,2,1,0:T(8,128)}, f32[28,32,128]{2,1,0:T(8,128)}, f32[32,8,128]{2,1,0:T(8,128)}) custom-call(s32[2]{0:T(128)} %pad_add_fusion.info, bf16[14,28,32,512]{3,2,1,0:T(8,128)(2,1)} %bitcast.32, bf16[512,128]{1,0:T(8,128)(2,1)} %wi_ref.1), custom_call_target="tpu_custom_call" | custom-call | flops 1644167168 | bytes 19267584 | tf_op jit(solution)/shard_map/first_norm_sums/pallas_call | solution.py:785
  13.8 0.5 collective-permute-start
  14.2 7.0 %all-to-all-start = ((f32[32,8,128]{2,1,0:T(8,128)}), f32[32,8,128]{2,1,0:T(8,128)S(1)}, u32[]{:S(2)}, u32[]{:S(2)}) async-start(f32[32,8,128]{2,1,0:T(8,128)} %get-tuple-element.60), calls=%async_computation | async-start | bytes 262144 | tf_op jit(solution)/shard_map/all_to_all | solution.py:40
  21.2 0.0 copy-done.4
  21.2 0.2 copy.24
  21.4 0.0 copy-start.5
  21.5 0.0 copy-start.8
  21.5 0.0 copy-start.11
  21.5 9.2 %input_cross.1.xz_ref = f32[512,128]{1,0:T(8,128)S(1)} custom-call(bf16[14,28,32,512]{3,2,1,0:T(8,128)(2,1)} %bitcast.33, f32[14,28,32,128]{3,2,1,0:T(8,128)} %get-tuple-element.61.z_ref.z1_ref), custom_call_target="tpu_custom_call" | custom-call | flops 1644167168 | bytes 19267584 | tf_op jit(solution)/shard_map/input_cross/pallas_call | solution.py:802
  30.7 0.0 all-to-all-done
  30.8 0.0 collective-permute-done.edge_ref
  30.8 0.0 copy-start.3
  30.8 0.0 copy-start.9
  30.8 0.0 copy-start.10
  30.9 12.6 %middle_conv.1 = (f32[14,28,32,128]{3,2,1,0:T(8,128)}, bf16[14,28,32,128]{3,2,1,0:T(8,128)(2,1)}, f32[8,128]{1,0:T(8,128)S(1)}) custom-call(s32[2]{0:T(128)S(1)} %copy-done.5, f32[8,128]{1,0:T(8,128)S(1)} %reduce_sum.18.st1, f32[1,128]{1,0:T(1,128)S(1)} %bitcast.23, f32[1,128]{1,0:T(1,128)S(1)} %bitcast.30, ...), custom_call_target="tpu_custom_call" | custom-call | flops 4932501504 | bytes 16056320 | tf_op jit(solution)/shard_map/middle_conv/pallas_call | solution.py:817
  43.5 0.3 collective-permute-start.1
  43.8 0.9 collective-permute-done.1
  44.7 14.2 %all_to_all.30 = f32[16,8,128]{2,1,0:T(8,128)S(1)} all-to-all(f32[16,8,128]{2,1,0:T(8,128)S(1)} %broadcast_in_dim.2), channel_id=1, replica_groups={{0,2,4,6,8,10,12,14,16,18,20,22,24,26,28,30},{1,3,5,7,9,11,13,15,17,19,..., dimensions={0} | all-to-all | bytes 131072 | tf_op jit(solution)/shard_map/all_to_all | solution.py:31
  58.9 0.0 copy-done.3
  58.9 10.8 %second_norm.1 = (bf16[14,28,32,128]{3,2,1,0:T(8,128)(2,1)S(1)}, bf16[14,28,32,128]{3,2,1,0:T(8,128)(2,1)S(1)}, bf16[14,28,32,128]{3,2,1,0:T(8,128)(2,1)S(1)}, b...) custom-call(s32[2]{0:T(128)S(1)} %copy-done.5, ...), custom_call_target="tpu_custom_call" | custom-call | flops 1233125376 | bytes 16056320 | tf_op jit(solution)/shard_map/second_norm/pallas_call | solution.py:841
  69.8 0.1 collective-permute-start.2
  69.9 1.3 collective-permute-done.2.arrived_ref
  71.1 11.5 %all_to_all.31.in3 = f32[16,24,128]{2,1,0:T(8,128)S(1)} all-to-all(f32[16,24,128]{2,1,0:T(8,128)S(1)} %spread_third.1), channel_id=1, replica_groups=mesh['batch'=16,'rows'=2] {'batch'}, dimensions={0} | all-to-all | bytes 393216 | tf_op jit(solution)/shard_map/all_to_all | solution.py:36
  82.6 0.0 copy-done.6
  82.7 30.5 %last_norm.1 = (bf16[14,28,32,512]{3,2,1,0:T(8,128)(2,1)}, bf16[14,28,32,512]{3,2,1,0:T(8,128)(2,1)}, bf16[14,28,32,128]{3,2,1,0:T(8,128)(2,1)}, bf16[28,32,128]...) custom-call(s32[2]{0:T(128)S(1)} %copy-done.5, ...), custom_call_target="tpu_custom_call" | custom-call | flops 8220835840 | bytes 61014016 | tf_op jit(solution)/shard_map/last_norm/pallas_call | solution.py:874
  113.2 0.1 collective-permute-start.4
  113.3 0.5 collective-permute-start.5
  113.8 0.1 collective-permute-start.6
  113.8 0.4 collective-permute-start.3
  114.3 1.8 collective-permute-done.3.arrived_ref
  116.1 0.0 collective-permute-done.6.te_ref
  116.1 0.0 collective-permute-done.4.ye_ref
  116.1 0.0 collective-permute-done.5.ze_ref
  116.1 0.6 spread_fourth.1
  116.6 13.6 %all_to_all.32.in4 = f32[16,32,128]{2,1,0:T(8,128)S(1)} all-to-all(f32[16,32,128]{2,1,0:T(8,128)S(1)} %spread_fourth.1), channel_id=1, replica_groups=mesh['batch'=16,'rows'=2] {'batch'}, dimensions={0} | all-to-all | bytes 524288 | tf_op jit(solution)/shard_map/all_to_all | solution.py:36
  130.2 25.3 %middle_back.1 = (bf16[14,28,32,128]{3,2,1,0:T(8,128)(2,1)}, f32[1416,128]{1,0:T(8,128)S(1)}, f32[1416,128]{1,0:T(8,128)S(1)}, f32[16,128]{1,0:T(8,128)S(1)}) custom-call(s32[2]{0:T(128)S(1)} %copy-done.5, f32[8,128]{1,0:T(8,128)S(1)} %reduce_sum.18.st1, f32[8,128]{1,0:T(8,128)S(1)} %reduce_sum.19.st2, f32[16,128]{1,0:T(8,128)S(1)} %get-tuple-element.72.st3, ...), custom_call_target="tpu_custom_call" | custom-call | flops 13153337344 | bytes 50176000 | tf_op jit(solution)/shard_map/middle_back/pallas_call | solution.py:929
  155.6 0.0 collective-permute-start.7
  155.6 2.2 %collective-permute-done.7.arrived_ref = f32[1416,128]{1,0:T(8,128)S(1)} collective-permute-done((f32[1416,128]{1,0:T(8,128)S(1)}, f32[1416,128]{1,0:T(8,128)S(1)}, u32[]{:S(2)}, u32[]{:S(2)}) %collective-permute-start.7) | collective-permute-done | bytes 725024 | tf_op jit(solution)/shard_map/ppermute | solution.py:25
  157.8 0.1 pack_shares.1
  157.9 16.2 %all_to_all.33.in_ref = bf16[16,96,128]{2,1,0:T(8,128)(2,1)S(1)} all-to-all(bf16[16,96,128]{2,1,0:T(8,128)(2,1)S(1)} %pack_shares.1), channel_id=1, replica_groups=mesh['batch'=16,'rows'=2] {'batch'}, dimensions={0} | all-to-all | bytes 786432 | tf_op jit(solution)/shard_map/all_to_all | solution.py:36
  174.1 0.8 sum_shares.1
  174.9 3.6 %all-to-all-start.5 = ((bf16[16,96,128]{2,1,0:T(8,128)(2,1)}), bf16[16,96,128]{2,1,0:T(8,128)(2,1)S(1)}, u32[]{:S(2)}, u32[]{:S(2)}) async-start(bf16[16,96,128]{2,1,0:T(8,128)(2,1)} %get-tuple-element.93), calls=%async_computation.5 | async-start | bytes 786432 | tf_op jit(solution)/shard_map/all_to_all | solution.py:36
  178.5 15.8 %input_grad.1 = bf16[14,28,32,512]{3,2,1,0:T(8,128)(2,1)} custom-call(s32[2]{0:T(128)S(1)} %copy-done.5, f32[8,128]{1,0:T(8,128)S(1)} %reduce_sum.18.st1, f32[8,128]{1,0:T(8,128)S(1)} %get-tuple-element.94.st5, f32[1,128]{1,0:T(1,128)S(1)} %bitcast.25, bf16[512,128]{1,0:T(8,128)(2,1)S(1)} %copy-done.2, bf16[14,28,32,128]{3,2,1,0:T(8,128)(2,1)} %get-tuple-element.95.h_ref, ...), custom_call_target="tpu_custom_call" | custom-call | flops 1644167168 | bytes 35323904 | tf_op jit(solution)/shard_map/input_grad/pallas_call | solution.py:995
  194.3 0.0 all-to-all-done.5.mine_ref
  194.3 0.0 collective-permute-start.8
  194.4 1.7 collective-permute-done.8.other_ref
  196.1 1.7 replicated_grads.1
  (21 shorter events, 0.1 us)
Async XLA Ops:
  1.9 19.3 %copy-start.4 = (bf16[3,3,128,128]{3,2,1,0:T(8,128)(2,1)S(1)}, bf16[3,3,128,128]{3,2,1,0:T(8,128)(2,1)}, u32[]{:S(2)}) copy-start(bf16[3,3,128,128]{3,2,1,0:T(8,128)(2,1)} %w_ref.3) | copy-start | bytes 884740
  13.8 17.0 %collective-permute-start = (f32[28,32,128]{2,1,0:T(8,128)}, f32[28,32,128]{2,1,0:T(8,128)S(1)}, u32[]{:S(2)}, u32[]{:S(2)}) collective-permute-start(f32[28,32,128]{2,1,0:T(8,128)} %get-tuple-element.62), channel_id=1, source_target_pairs={{0,1},{1,0},{2,3},{3,2},{4,5},{5,4},{6,7},{7,6},{8,9},{9,8},{10,11... | collective-permute-start | bytes 1376264 | tf_op jit(solution)/shard_map/ppermute | solution.py:25
  14.2 16.5 %all-to-all-start = ((f32[32,8,128]{2,1,0:T(8,128)}), f32[32,8,128]{2,1,0:T(8,128)S(1)}, u32[]{:S(2)}, u32[]{:S(2)}) async-start(f32[32,8,128]{2,1,0:T(8,128)} %get-tuple-element.60), calls=%async_computation | async-start | bytes 262144 | tf_op jit(solution)/shard_map/all_to_all | solution.py:40
  21.4 9.3 %copy-start.5 = (s32[2]{0:T(128)S(1)}, s32[2]{0:T(128)}, u32[]{:S(2)}) copy-start(s32[2]{0:T(128)} %pad_add_fusion.info) | copy-start | bytes 28
  21.5 9.3 %copy-start.8 = (f32[128]{0:T(128)S(1)}, f32[128]{0:T(128)}, u32[]{:S(2)}) copy-start(f32[128]{0:T(128)} %param.15) | copy-start | bytes 1540
  21.5 9.3 %copy-start.11 = (f32[128]{0:T(128)S(1)}, f32[128]{0:T(128)}, u32[]{:S(2)}) copy-start(f32[128]{0:T(128)} %param.16) | copy-start | bytes 1540
  30.8 28.1 %copy-start.3 = (bf16[128,512]{1,0:T(8,128)(2,1)S(1)}, bf16[128,512]{1,0:T(8,128)(2,1)}, u32[]{:S(2)}) copy-start(bf16[128,512]{1,0:T(8,128)(2,1)} %wo_ref.5) | copy-start | bytes 393220
  30.8 28.1 %copy-start.9 = (f32[128]{0:T(128)S(1)}, f32[128]{0:T(128)}, u32[]{:S(2)}) copy-start(f32[128]{0:T(128)} %param.19) | copy-start | bytes 1540
  30.8 28.1 %copy-start.10 = (f32[128]{0:T(128)S(1)}, f32[128]{0:T(128)}, u32[]{:S(2)}) copy-start(f32[128]{0:T(128)} %param.18) | copy-start | bytes 1540
  43.5 39.2 %copy-start.6 = (f32[512]{0:T(512)S(1)}, f32[512]{0:T(512)}, u32[]{:S(2)}) copy-start(f32[512]{0:T(512)} %param.22) | copy-start | bytes 6148
  43.5 39.2 %copy-start.7 = (f32[512]{0:T(512)S(1)}, f32[512]{0:T(512)}, u32[]{:S(2)}) copy-start(f32[512]{0:T(512)} %param.21) | copy-start | bytes 6148
  43.5 1.2 collective-permute-start.1
  69.8 43.4 %copy-start = (bf16[14,28,32,128]{3,2,1,0:T(8,128)(2,1)}, bf16[14,28,32,128]{3,2,1,0:T(8,128)(2,1)S(1)}, u32[]{:S(2)}) copy-start(bf16[14,28,32,128]{3,2,1,0:T(8,128)(2,1)S(1)} %get-tuple-element.68.y_ref) | copy-start | bytes 9633796
  69.8 43.4 %copy-start.1 = (bf16[14,28,32,128]{3,2,1,0:T(8,128)(2,1)}, bf16[14,28,32,128]{3,2,1,0:T(8,128)(2,1)S(1)}, u32[]{:S(2)}) copy-start(bf16[14,28,32,128]{3,2,1,0:T(8,128)(2,1)S(1)} %get-tuple-element.69.g_ref.s_ref) | copy-start | bytes 9633796
  69.8 1.3 collective-permute-start.2
  113.2 2.9 %collective-permute-start.4 = (bf16[28,32,256]{2,1,0:T(8,128)(2,1)S(1)}, bf16[28,32,256]{2,1,0:T(8,128)(2,1)S(1)}, u32[]{:S(2)}, u32[]{:S(2)}) collective-permute-start(bf16[28,32,256]{2,1,0:T(8,128)(2,1)S(1)} %get-tuple-element.78), channel_id=1, source_target_pairs={{0,1},{1,0},{2,3},{3,2},{4,5},{5,4},{6,7},{7,6},{8,9},{9,8},{10,11... | collective-permute-start | bytes 1376264 | tf_op jit(solution)/shard_map/ppermute | solution.py:25
  113.3 2.8 %collective-permute-start.5 = (f32[28,32,128]{2,1,0:T(8,128)S(1)}, f32[28,32,128]{2,1,0:T(8,128)S(1)}, u32[]{:S(2)}, u32[]{:S(2)}) collective-permute-start(f32[28,32,128]{2,1,0:T(8,128)S(1)} %get-tuple-element.79), channel_id=1, source_target_pairs={{0,1},{1,0},{2,3},{3,2},{4,5},{5,4},{6,7},{7,6},{8,9},{9,8},{10,11... | collective-permute-start | bytes 1376264 | tf_op jit(solution)/shard_map/ppermute | solution.py:25
  113.8 2.3 %collective-permute-start.6 = (bf16[28,32,128]{2,1,0:T(8,128)(2,1)S(1)}, bf16[28,32,128]{2,1,0:T(8,128)(2,1)S(1)}, u32[]{:S(2)}, u32[]{:S(2)}) collective-permute-start(bf16[28,32,128]{2,1,0:T(8,128)(2,1)S(1)} %get-tuple-element.80), channel_id=1, source_target_pairs={{0,1},{1,0},{2,3},{3,2},{4,5},{5,4},{6,7},{7,6},{8,9},{9,8},{10,11... | collective-permute-start | bytes 688136 | tf_op jit(solution)/shard_map/ppermute | solution.py:25
  113.8 2.2 %collective-permute-start.3 = (f32[24,128]{1,0:T(8,128)S(1)}, f32[24,128]{1,0:T(8,128)S(1)}, u32[]{:S(2)}, u32[]{:S(2)}) collective-permute-start(f32[24,128]{1,0:T(8,128)S(1)} %get-tuple-element.77.own_ref.own4), channel_id=1, source_target_pairs={{0,1},{1,0},{2,3},{3,2},{4,5},{5,4},{6,7},{7,6},{8,9},{9,8},{10,11... | collective-permute-start | bytes 36872 | tf_op jit(solution)/shard_map/ppermute | solution.py:25
  130.2 48.3 %copy-start.2 = (bf16[512,128]{1,0:T(8,128)(2,1)S(1)}, bf16[512,128]{1,0:T(8,128)(2,1)}, u32[]{:S(2)}) copy-start(bf16[512,128]{1,0:T(8,128)(2,1)} %wi_ref.1) | copy-start | bytes 393220
  155.6 2.2 %collective-permute-start.7 = (f32[1416,128]{1,0:T(8,128)S(1)}, f32[1416,128]{1,0:T(8,128)S(1)}, u32[]{:S(2)}, u32[]{:S(2)}) collective-permute-start(f32[1416,128]{1,0:T(8,128)S(1)} %get-tuple-element.92), channel_id=1, source_target_pairs={{0,1},{1,0},{2,3},{3,2},{4,5},{5,4},{6,7},{7,6},{8,9},{9,8},{10,11... | collective-permute-start | bytes 2174984 | tf_op jit(solution)/shard_map/ppermute | solution.py:25
  174.9 19.5 %all-to-all-start.5 = ((bf16[16,96,128]{2,1,0:T(8,128)(2,1)}), bf16[16,96,128]{2,1,0:T(8,128)(2,1)S(1)}, u32[]{:S(2)}, u32[]{:S(2)}) async-start(bf16[16,96,128]{2,1,0:T(8,128)(2,1)} %get-tuple-element.93), calls=%async_computation.5 | async-start | bytes 786432 | tf_op jit(solution)/shard_map/all_to_all | solution.py:36
  194.3 1.7 collective-permute-start.8
